TPU v7x, 512 devices: a whole 4x4x16 slice. The times are simulated.
512 devices in a mesh: ctx: 64 (over y_hi, z, core), exp: 8 (over x, y_lo).
Axes of the slice: x: 4, y: 4 (y_hi: 2, y_lo: 2; y = y_hi * 2 + y_lo), z: 16, core: 2. Of those that a mesh axis runs over, the one named last changes fastest.
Arguments:
- normed: bfloat16 [8192, 8192], P('ctx', 'exp'), may hold values from -6 to 6
- frozen_query: bfloat16 [8192, 4096], P('ctx', 'exp'), may hold values from -5 to 5
- input_keys: bfloat16 [8192, 1024], P('ctx', 'exp'), may hold values from -5 to 5
- input_values: bfloat16 [8192, 1024], P('ctx', 'exp'), may hold values from -6 to 6
- document_index: int32 [8192], P('ctx'), may hold values from 0 to 31, never falling along the last dimension, each value on 1 to 5120 neighbouring positions
- routes: int32 [64, 2], P('ctx'), may hold values from 0 to 15, all different within a row
- adapter_down_weight: bfloat16 [16, 8192, 64], P(None, 'exp'), may hold values from -0.0625 to 0.0625
- adapter_up_weight: bfloat16 [1024, 4096], P('ctx', 'exp'), may hold values from -0.75 to 0.75
- output_gradient: bfloat16 [8192, 4096], P('ctx', 'exp'), may hold values from -6 to 6
Outputs:
- attended: float32 [8192, 4096], P('ctx', 'exp')
- query_gradient: float32 [8192, 4096], P('ctx', 'exp')
- key_gradient: float32 [8192, 1024], P('ctx', 'exp')
- value_gradient: float32 [8192, 1024], P('ctx', 'exp')
- up_gradient: float32 [1024, 4096], P('ctx', 'exp')
Inputs may be any that keep to these rules, and one draw needn't show every extreme that they name: `document_index`: document ids never fall along the sequence; each document holds 1 to 5120 tokens, and one holds exactly 5120. `routes`: each row names 2 different experts; every expert is named by some row.
All inputs are finite; a program needn't handle non-finite values.
Results may differ from a plain program's by a relative error of at most 0.04.
Values may be sent and summed in bfloat16 or wider, within the bound.
No kernel may reach another device: no remote copies, remote signals or barrier semaphores. Data moves between devices by JAX's collectives and lax.ppermute only.
A program may use at most 64 MiB of HBM per device.

v0:
```python
import math

import jax
import jax.numpy as jnp
from jax import lax
from jax.sharding import PartitionSpec as P

HEAD_SIZE = 128
EXPERT_RANK = 64
EXPERT_COUNT = 16
TOP = 2
BLOCK = 128


adapter_scale = 0.5
far_below = -1e30


def passed_along(block, axis, distance):
    devices = range(lax.axis_size(axis))
    route = [((i - distance) % len(devices), i) for i in devices]
    return lax.ppermute(block, axis, route)


def head_scores(query_heads, key_rows, inverse):
    kv_heads = query_heads.shape[1]
    key_head_rows = key_rows.reshape(key_rows.shape[0], kv_heads, -1)
    return (
        jnp.einsum("tkgd,skd->kgts", query_heads, key_head_rows, preferred_element_type=jnp.float32)
        * inverse
    )


def visible(query_pos, query_docs, key_pos, key_docs):
    same_doc = query_docs[:, None] == key_docs[None, :]
    return same_doc & (key_pos[None, :] <= query_pos[:, None])


def shards(
    normed,
    frozen_query,
    input_keys,
    input_values,
    document_index,
    routes,
    adapter_down_weight,
    adapter_up_weight,
    output_gradient,
):
    ctx_count = lax.axis_size("ctx")
    ctx_place = lax.axis_index("ctx")
    local_rows = normed.shape[0]
    total_rows = local_rows * ctx_count
    kv_local = input_keys.shape[1] // HEAD_SIZE
    heads_local = frozen_query.shape[1] // HEAD_SIZE
    heads_per_group = heads_local // kv_local
    inverse = 1.0 / math.sqrt(HEAD_SIZE)
    first_row = ctx_place * local_rows
    last_row = first_row + local_rows - 1
    query_pos = first_row + jnp.arange(local_rows, dtype=jnp.int32)

    def is_live(key_first):
        causal = key_first <= last_row
        return causal

    block_count = routes.shape[0]
    row_blocks = normed.reshape(block_count, BLOCK, normed.shape[1])
    chosen_experts = adapter_down_weight[routes]
    partial_low = jnp.einsum(
        "bnd,bjdr->bnjr", row_blocks, chosen_experts, preferred_element_type=jnp.float32
    )
    partial_low = partial_low.reshape(block_count, BLOCK, TOP * EXPERT_RANK)
    low_rank = lax.psum(partial_low, "exp").astype(jnp.bfloat16)
    low_rank = low_rank.reshape(block_count, BLOCK, TOP, EXPERT_RANK)
    selector = (
        routes[:, :, None] == jnp.arange(EXPERT_COUNT, dtype=jnp.int32)[None, None, :]
    ).astype(jnp.bfloat16)
    reduced_full = jnp.einsum(
        "bnjr,bje->bner", low_rank, selector, preferred_element_type=jnp.float32
    )
    reduced_full = reduced_full.reshape(local_rows, EXPERT_COUNT * EXPERT_RANK).astype(jnp.bfloat16)
    columns = reduced_full
    adapter_delta = jnp.dot(
        columns,
        lax.all_gather(adapter_up_weight, "ctx", axis=0, tiled=True),
        preferred_element_type=jnp.float32,
    )
    query_rows = (frozen_query.astype(jnp.float32) + adapter_scale * adapter_delta).astype(
        jnp.bfloat16
    )
    query_heads = query_rows.reshape(local_rows, kv_local, heads_per_group, HEAD_SIZE)
    fold_row_top = jnp.full((kv_local, heads_per_group, local_rows), far_below, jnp.float32)
    fold_row_total = jnp.zeros((kv_local, heads_per_group, local_rows), jnp.float32)
    doc_buf = jnp.zeros((total_rows,), jnp.int32)
    key_piece = lax.all_gather(input_keys, "ctx", axis=0, tiled=True)
    value_piece = lax.all_gather(input_values, "ctx", axis=0, tiled=True)
    doc_piece = lax.all_gather(document_index, "ctx", axis=0, tiled=True)
    piece_rows = key_piece.shape[0]
    doc_buf = lax.dynamic_update_slice_in_dim(doc_buf, doc_piece, jnp.int32(0), 0)
    width = math.gcd(piece_rows, 8 * local_rows)

    def one_part(part_index, stats):
        key_first = part_index * width
        part_keys = lax.dynamic_slice_in_dim(key_piece, part_index * width, width, 0)
        part_docs = lax.dynamic_slice_in_dim(doc_piece, part_index * width, width, 0)

        def update(current):
            old_top, old_total = current
            scores = head_scores(query_heads, part_keys, inverse)
            allowed = visible(
                query_pos, document_index, key_first + jnp.arange(width, dtype=jnp.int32), part_docs
            )
            new_top = jnp.maximum(old_top, jnp.max(jnp.where(allowed, scores, far_below), axis=3))
            added = jnp.sum(jnp.where(allowed, jnp.exp(scores - new_top[..., None]), 0.0), axis=3)
            return (new_top, old_total * jnp.exp(old_top - new_top) + added)

        return lax.cond(is_live(key_first), update, lambda current: current, stats)

    fold_row_top, fold_row_total = lax.fori_loop(
        0, piece_rows // width, one_part, (fold_row_top, fold_row_total)
    )
    row_top = fold_row_top
    row_total = fold_row_total
    doc_all = doc_buf
    span = local_rows * math.gcd(8, ctx_count)

    def attend_block(block_index, accum):
        key_first = block_index * span
        block_keys = lax.dynamic_slice_in_dim(key_piece, key_first, span, 0)
        block_values = lax.dynamic_slice_in_dim(value_piece, key_first, span, 0)
        block_docs = lax.dynamic_slice_in_dim(doc_all, key_first, span, 0)

        def accumulate(current):
            scores = head_scores(query_heads, block_keys, inverse)
            allowed = visible(
                query_pos, document_index, key_first + jnp.arange(span, dtype=jnp.int32), block_docs
            )
            prob_low = (
                jnp.where(allowed, jnp.exp(scores - row_top[..., None]), 0.0) / row_total[..., None]
            ).astype(jnp.bfloat16)
            value_head_rows = block_values.reshape(span, kv_local, HEAD_SIZE)
            return current + jnp.einsum(
                "kgts,skd->kgtd", prob_low, value_head_rows, preferred_element_type=jnp.float32
            )

        return lax.cond(is_live(key_first), accumulate, lambda current: current, accum)

    attended_sum = lax.fori_loop(
        0,
        total_rows // span,
        attend_block,
        jnp.zeros((kv_local, heads_per_group, local_rows, HEAD_SIZE), jnp.float32),
    )
    attended_heads = attended_sum.astype(jnp.bfloat16)
    attended = attended_sum.transpose(2, 0, 1, 3).reshape(local_rows, heads_local * HEAD_SIZE)
    out_heads = output_gradient.reshape(local_rows, kv_local, heads_per_group, HEAD_SIZE)
    row_delta = jnp.sum(
        out_heads.transpose(1, 2, 0, 3).astype(jnp.float32) * attended_heads.astype(jnp.float32),
        axis=3,
    )
    key_zero = jnp.zeros((local_rows, kv_local, HEAD_SIZE), jnp.float32)

    def hop_terms(target, valid, low_head, high_head):
        key_first = target * local_rows
        block_keys = lax.dynamic_slice_in_dim(key_piece, key_first, local_rows, 0)
        block_values = lax.dynamic_slice_in_dim(value_piece, key_first, local_rows, 0)
        block_docs = lax.dynamic_slice_in_dim(doc_all, key_first, local_rows, 0)
        query_zero = jnp.zeros((kv_local, high_head - low_head, local_rows, HEAD_SIZE), jnp.float32)

        def work(unused):
            scores = head_scores(query_heads, block_keys, inverse)
            allowed = visible(
                query_pos,
                document_index,
                key_first + jnp.arange(local_rows, dtype=jnp.int32),
                block_docs,
            )
            prob = (
                jnp.where(allowed, jnp.exp(scores - row_top[..., None]), 0.0) / row_total[..., None]
            )
            value_head_rows = block_values.reshape(local_rows, kv_local, HEAD_SIZE)
            key_head_rows = block_keys.reshape(local_rows, kv_local, HEAD_SIZE)
            dprob = jnp.einsum(
                "tkgd,skd->kgts", out_heads, value_head_rows, preferred_element_type=jnp.float32
            )
            dscore = (prob * (dprob - row_delta[..., None])).astype(jnp.bfloat16)
            dquery = (
                jnp.einsum(
                    "kgts,skd->kgtd", dscore, key_head_rows, preferred_element_type=jnp.float32
                )
                * inverse
            )
            dkey = (
                jnp.einsum(
                    "kgts,tkgd->skd", dscore, query_heads, preferred_element_type=jnp.float32
                )
                * inverse
            )
            dvalue = jnp.einsum(
                "kgts,tkgd->skd",
                prob.astype(jnp.bfloat16),
                out_heads,
                preferred_element_type=jnp.float32,
            )
            return (dquery, dkey, dvalue)

        live_here = valid & is_live(key_first)
        return lax.cond(live_here, work, lambda unused: (query_zero, key_zero, key_zero), 0)

    always_valid = jnp.asarray(True)
    first_terms = hop_terms(jnp.mod(ctx_place - 1, ctx_count), always_valid, 0, heads_per_group)

    def cycle_hop(hop_index, state):
        dquery_sum, key_acc, value_acc = state
        key_acc, value_acc = passed_along((key_acc, value_acc), "ctx", 1)
        dquery, dkey, dvalue = hop_terms(
            jnp.mod(ctx_place - 1 - hop_index, ctx_count), always_valid, 0, heads_per_group
        )
        return (dquery_sum + dquery, key_acc + dkey, value_acc + dvalue)

    dquery_sum, key_grad, value_grad = lax.fori_loop(1, ctx_count, cycle_hop, first_terms)
    query_gradient = dquery_sum.transpose(2, 0, 1, 3).reshape(local_rows, heads_local * HEAD_SIZE)
    query_low = query_gradient.astype(jnp.bfloat16)
    key_gradient = key_grad.reshape(local_rows, kv_local * HEAD_SIZE)
    value_gradient = value_grad.reshape(local_rows, kv_local * HEAD_SIZE)
    columns = reduced_full
    up_gradient = lax.psum_scatter(
        adapter_scale
        * lax.dot_general(
            columns, query_low, (((0,), (0,)), ((), ())), preferred_element_type=jnp.float32
        ),
        "ctx",
        scatter_dimension=0,
        tiled=True,
    )
    return (attended, query_gradient, key_gradient, value_gradient, up_gradient)


def solution(mesh):
    return jax.shard_map(
        shards,
        mesh=mesh,
        in_specs=(
            P("ctx", "exp"),
            P("ctx", "exp"),
            P("ctx", "exp"),
            P("ctx", "exp"),
            P("ctx"),
            P("ctx", None),
            P(None, "exp", None),
            P("ctx", "exp"),
            P("ctx", "exp"),
        ),
        out_specs=(
            P("ctx", "exp"),
            P("ctx", "exp"),
            P("ctx", "exp"),
            P("ctx", "exp"),
            P("ctx", "exp"),
        ),
        check_vma=False,
    )
```

profile of v0, /device:TPU:6, one launch (start us, length us, event | category | flops | bytes accessed | tf_op | source)
XLA Modules:
  0.0 1502.4 jit_solution(7567299854928345670)
XLA Ops:
  11.9 34.2 %psum.7 = bf16[1,128,128]{1,2,0:T(8,128)(2,1)S(1)} all-reduce(f32[1,128,128]{1,2,0:T(8,128)S(1)} %convolution_bitcast_fusion.6), channel_id=1, replica_groups=mesh['ctx'=64,'exp'=8] {'exp'}, use_global_device_ids=true, to_apply=%region_0.0 | all-reduce | flops 16384 | bytes 98304 | tf_op jit(solution)/shard_map/psum | solution.py:73
  47.5 81.0 %all-gather = s32[64,1,128]{2,1,0:T(1,128)S(1)} all-gather(s32[1,1,128]{2,1,0:T(1,128)S(1)} %bitcast.288), channel_id=1, replica_groups=mesh['ctx'=64,'exp'=8] {'ctx'}, dimensions={0}, use_global_device_ids=true | all-gather | bytes 33280 | tf_op jit(solution)/shard_map/all_gather | solution.py:97
  129.1 26.4 %all-gather.7.cloned.1.call-done = bf16[1024,512]{1,0:T(8,128)(2,1)} async-done(((bf16[16,512]{1,0:T(8,128)(2,1)}), bf16[1024,512]{1,0:T(8,128)(2,1)}) %all-gather.7.cloned.1.call-update) | async-done | bytes 1048592 | tf_op jit(solution)/shard_map/all_gather | solution.py:85
  157.2 141.1 %all-gather.5.cloned.1.call-done = bf16[8192,128]{1,0:T(8,128)(2,1)} async-done(((bf16[128,128]{1,0:T(8,128)(2,1)}), bf16[8192,128]{1,0:T(8,128)(2,1)}) %all-gather.5.cloned.1.call-update) | async-done | bytes 2097168 | tf_op jit(solution)/shard_map/all_gather | solution.py:95
  300.9 138.8 %all-gather.9.cloned.1.call-done = bf16[8192,128]{1,0:T(8,128)(2,1)} async-done(((bf16[128,128]{1,0:T(8,128)(2,1)}), bf16[8192,128]{1,0:T(8,128)(2,1)}) %all-gather.9.cloned.1.call-update) | async-done | bytes 2097168 | tf_op jit(solution)/shard_map/all_gather | solution.py:96
  444.5 830.6 %while.55 = (s32[]{:T(128)}, f32[1,4,128,128]{3,2,1,0:T(8,128)S(1)}, f32[128,1,128]{2,0,1:T(8,128)}, f32[128,1,128]{2,0,1:T(8,128)}, s32[]{:T(128)}, /*index=5*/...) while((s32[]{:T(128)}, ...), condition=%wide.region_17.18_spmd.clone, body=%wide.region_14.17_spmd.clone.sunk | while | flops 84640016 | bytes 3944018 | solution.py:221
  444.5 6.2 collective-permute-start
  454.6 16.6 %collective-permute-done = f32[128,1,128]{2,0,1:T(8,128)} collective-permute-done((f32[128,1,128]{2,0,1:T(8,128)}, f32[128,1,128]{2,0,1:T(8,128)}, u32[]{:S(2)}, u32[]{:S(2)}) %collective-permute-start) | collective-permute-done | bytes 65568 | tf_op jit(solution)/shard_map/while/body/eval_jaxpr/ppermute | solution.py:22
  492.1 5.0 collective-permute-done
  505.0 5.0 collective-permute-done
  530.8 5.0 collective-permute-done
  556.6 5.0 collective-permute-done
  569.6 5.0 collective-permute-done
  595.4 5.0 collective-permute-done
  608.3 5.0 collective-permute-done
  634.1 5.0 collective-permute-done
  672.8 5.0 collective-permute-done
  698.7 5.0 collective-permute-done
  711.6 5.0 collective-permute-done
  737.4 5.0 collective-permute-done
  750.3 5.0 collective-permute-done
  776.1 5.0 collective-permute-done
  802.0 5.0 collective-permute-done
  1278.8 217.0 %reduce-scatter.2.cloned.1.call-done = f32[16,512]{1,0:T(8,128)} async-done(((f32[1024,512]{1,0:T(8,128)}), f32[16,512]{1,0:T(8,128)}) %reduce-scatter.2.cloned.1.call-update) | async-done | bytes 32784 | tf_op jit(solution)/shard_map/reduce_scatter | solution.py:227
  (837 shorter events, 766.1 us)
Async XLA Ops:
  7.2 148.3 %all-gather.7.cloned.1.call-start = ((), (), s32[]{:S(2)}) async-start(), calls=%async_computation.2 | async-start | bytes 1064960 | tf_op jit(solution)/shard_map/all_gather | solution.py:85
  7.9 290.3 %all-gather.5.cloned.1.call-start = ((), (), s32[]{:S(2)}) async-start(), calls=%async_computation.1 | async-start | bytes 2129920 | tf_op jit(solution)/shard_map/all_gather | solution.py:95
  8.7 431.1 %all-gather.9.cloned.1.call-start = ((), (), s32[]{:S(2)}) async-start(), calls=%async_computation.3 | async-start | bytes 2129920 | tf_op jit(solution)/shard_map/all_gather | solution.py:96
  9.4 1486.4 %reduce-scatter.2.cloned.1.call-start = ((), (), s32[]{:S(2)}) async-start(), calls=%async_computation.4 | async-start | bytes 2129920 | tf_op jit(solution)/shard_map/reduce_scatter | solution.py:227
  444.5 26.7 %collective-permute-start = (f32[128,1,128]{2,0,1:T(8,128)}, f32[128,1,128]{2,0,1:T(8,128)}, u32[]{:S(2)}, u32[]{:S(2)}) collective-permute-start(f32[128,1,128]{2,0,1:T(8,128)} %get-tuple-element.1894), channel_id=1, source_target_pairs={{504,0},{0,8},{8,16},{16,24},{24,32},{32,40},{40,48},{48,56},{56,6... | collective-permute-start | bytes 196616 | tf_op jit(solution)/shard_map/while/body/eval_jaxpr/ppermute | solution.py:22
  450.8 22.4 %collective-permute-start.1 = (f32[128,1,128]{2,0,1:T(8,128)}, f32[128,1,128]{2,0,1:T(8,128)}, u32[]{:S(2)}, u32[]{:S(2)}) collective-permute-start(f32[128,1,128]{2,0,1:T(8,128)} %get-tuple-element.1895), channel_id=1, source_target_pairs={{504,0},{0,8},{8,16},{16,24},{24,32},{32,40},{40,48},{48,56},{56,6... | collective-permute-start | bytes 196616 | tf_op jit(solution)/shard_map/while/body/eval_jaxpr/ppermute | solution.py:22
  489.5 9.5 collective-permute-start.1
  502.4 9.5 collective-permute-start.1
  528.2 9.5 collective-permute-start.1
  566.9 9.5 collective-permute-start.1
  592.8 9.5 collective-permute-start.1
  605.7 9.5 collective-permute-start.1
  631.5 9.5 collective-permute-start.1
  670.2 9.5 collective-permute-start.1
  709.0 9.5 collective-permute-start.1
  734.8 9.5 collective-permute-start.1
  747.7 9.5 collective-permute-start.1
  773.5 9.5 collective-permute-start.1
  812.3 9.5 collective-permute-start.1
  838.1 9.5 collective-permute-start.1
  851.0 9.5 collective-permute-start.1
  876.8 9.5 collective-permute-start.1
  915.5 9.5 collective-permute-start.1
  954.3 9.5 collective-permute-start.1
  (111 other events, 1240.2 us)
Sparse Core Ops, SparseCore 0:
  11.3 144.1 all-gather.6
  158.8 139.3 all-gather.4
  301.5 138.1 all-gather.8
  1277.2 218.5 reduce-scatter.1
where the time goes:
time: 1530 us; the launch traced here: 1500 us
  waiting for transfers between devices  874 us (57%)
  starting transfers between devices  247 us (16%)
  other arithmetic  193 us (13%)
  blocking collectives  115 us (8%)
  local copies, waits for them, and re-layouts  40.9 us (3%)
    ppermute x126, waiting for transfers between devices, passed_along(): return lax.ppermute(block, axis, route)  349 us
    ppermute x126, starting transfers between devices, passed_along(): return lax.ppermute(block, axis, route)  247 us
    reduce_scatter x1, waiting for transfers between devices, shards(): lax.psum_scatter(adapter_scale * lax.dot_general(columns, query_low, (((0...  217 us
    add x189, other arithmetic, cycle_hop(): return (dquery_sum + dquery, key_acc + dkey, value_acc + dvalue)  190 us
    all_gather x1, waiting for transfers between devices, shards(): key_piece = lax.all_gather(input_keys, 'ctx', axis=0, tiled=True)  141 us
    all_gather x1, waiting for transfers between devices, shards(): value_piece = lax.all_gather(input_values, 'ctx', axis=0, tiled=True)  139 us
    all_gather x1, blocking collectives, shards(): doc_piece = lax.all_gather(document_index, 'ctx', axis=0, tiled=True)  81 us
    psum x1, blocking collectives, shards(): low_rank = lax.psum(partial_low, 'exp').astype(jnp.bfloat16)  34.2 us
  transfers between devices with their start and end apart: 130, of which 130 were waited for; matrix products, arithmetic and copies ran while one was open for 10% of the time, Pallas kernels for 0%

commit v1 on v0

v1 whole, which is shorter than its diff:
```python
import functools
import math

import jax
import jax.numpy as jnp
from jax import lax
from jax.experimental import pallas as pl
from jax.experimental.pallas import tpu as pltpu
from jax.sharding import PartitionSpec as P

HEAD = 128
RANK = 64
BLOCK = 128
QUAD = 4 * BLOCK

adapter_scale = 0.5
far_below = -1e30
to_two = math.log2(math.e) / math.sqrt(HEAD)
inverse = 1.0 / math.sqrt(HEAD)
f32 = jnp.float32
bf16 = jnp.bfloat16

KV = 2 * BLOCK
UPS = 64
GRAD = KV + 2 * UPS
PACK = GRAD + 16
KEYS, VALUES = slice(0, BLOCK), slice(BLOCK, KV)


def last_last(a, b):
    return lax.dot_general(a, b, (((1,), (1,)), ((), ())), preferred_element_type=f32)


def first_first(a, b):
    return lax.dot_general(a, b, (((0,), (0,)), ((), ())), preferred_element_type=f32)


def plain(a, b):
    return lax.dot_general(a, b, (((1,), (0,)), ((), ())), preferred_element_type=f32)


def sum_low(lows, low_out):
    low = lows[0]
    for i in range(1, lows.shape[0]):
        low = low + lows[i]
    low_out[...] = low.astype(bf16)


def prepare(heads, pair, docs, frozen_out, gout_t, pick):
    lane = lax.broadcasted_iota(jnp.int32, (128, BLOCK), 0)
    for w in range(2):
        for h in range(heads):
            columns = slice(h * HEAD, (h + 1) * HEAD)
            frozen_out[w, h * BLOCK : (h + 1) * BLOCK, :] = pair[w, 0:BLOCK, columns]
            gout_t[w, :, columns] = pair[w, BLOCK : 2 * BLOCK, columns].astype(f32).T
        pick[w] = jnp.where(lane == docs[w, 0:1, :], 1.0, 0.0).astype(bf16)


def expert_at(meta, z_count, w, j):
    first = meta[3 + 2 * w + j] * 4
    return lax.rem(first, 2 * z_count) // 2, lax.div(first, 2 * z_count) ^ meta[0]


def query_base(meta, z_count, w):
    yh, z, core = meta[0], meta[1], meta[2]
    across = (1 - 2 * yh) * 2 * z_count * BLOCK
    return (2 * z + core) * BLOCK + w * across


def quad_range(meta, z_count, w, start):
    base = query_base(meta, z_count, w)
    first_key = jnp.min(start.astype(f32)).astype(jnp.int32)
    first = jnp.clip(first_key, 0, z_count * KV) // QUAD
    last = jnp.clip(base, -QUAD, z_count * KV - 1) // QUAD
    last = jnp.where(base < 0, -1, last)
    return first, last


def chip_pieces(core, own, other, quad):
    z_at = quad * 2
    return [
        (own, z_at, core),
        (other, z_at, 1 - core),
        (own, z_at + 1, 2 + core),
        (other, z_at + 1, 3 - core),
    ]


def rows_of(n):
    return slice(n * BLOCK, (n + 1) * BLOCK)


def forward(
    heads,
    z_count,
    meta,
    own,
    other,
    low_ref,
    frozen,
    pick_ref,
    query,
    start_out,
    prob,
    out_ref,
    stats,
    payload,
    score,
):
    wide = heads * BLOCK
    yh, core = meta[0], meta[2]

    for w in range(2):
        low = low_ref[w]
        for h in range(heads):
            rows = []
            for j in range(2):
                z_at, slot = expert_at(meta, z_count, w, j)
                at = pl.ds(pl.multiple_of(KV + slot * UPS + 16 * h, 16), 16)
                for step in range(2):
                    mine, theirs = own[z_at + step, at, :], other[z_at + step, at, :]
                    rows.append(jnp.where(core == 0, mine, theirs))
                    rows.append(jnp.where(core == 0, theirs, mine))
            delta = plain(low, jnp.concatenate(rows, axis=0))
            block = slice(h * BLOCK, (h + 1) * BLOCK)
            query[w, block, :] = (
                frozen[w, block, :].astype(f32) + adapter_scale * delta
            ).astype(bf16)

    counts = jnp.zeros((16, 128), f32)
    for i in range(z_count):
        counts += own[i, GRAD:PACK, :].astype(f32) + other[i, GRAD:PACK, :].astype(f32)
    high = jnp.floor(counts * (1.0 / 128.0))
    rest = counts - 128.0 * high
    high, rest = high.astype(bf16), rest.astype(bf16)
    ramp = lax.broadcasted_iota(jnp.int32, (BLOCK, wide), 0)

    for w in range(2):
        pick = pick_ref[w]
        start = jnp.sum(128.0 * plain(high, pick) + plain(rest, pick), axis=0, keepdims=True)
        start = start.astype(jnp.int32) - yh * (z_count * KV)
        whole_key = jnp.max(start.astype(f32)).astype(jnp.int32)
        first_quad, last_quad = quad_range(meta, z_count, w, start)
        start = jnp.concatenate([start] * heads, axis=1)
        start_out[w] = jnp.broadcast_to(start, (8, wide))
        place = query_base(meta, z_count, w) + lax.broadcasted_iota(jnp.int32, (1, BLOCK), 1)
        place = jnp.concatenate([place] * heads, axis=1)
        whole_key = jnp.clip(whole_key, 0, z_count * KV)
        whole_quad = jnp.minimum(
            jnp.maximum((whole_key + QUAD - 1) // QUAD, first_quad), last_quad
        )
        queries = query[w]

        def scores(masked, quad, top):
            for n, (src, z_at, at) in enumerate(chip_pieces(core, own, other, quad)):
                s = last_last(src[z_at, KEYS, :], queries)
                if masked:
                    base = quad * QUAD + at * BLOCK
                    s = jnp.where((ramp >= start - base) & (ramp <= place - base), s, far_below)
                score[quad, rows_of(n), :] = s
                top = jnp.maximum(top, jnp.max(s.reshape(BLOCK // 8, 8, wide), axis=0))
            return top

        top = jnp.full((8, wide), far_below, f32)
        top = lax.fori_loop(
            first_quad,
            jnp.where(last_quad >= first_quad, whole_quad + 1, first_quad),
            lambda i, t: scores(True, jnp.where(i == whole_quad, last_quad, i), t),
            top,
        )
        top = lax.fori_loop(
            jnp.maximum(whole_quad, first_quad),
            last_quad,
            functools.partial(scores, False),
            top,
        )
        top = jnp.max(top, axis=0, keepdims=True)
        top = jnp.where(top < 0.5 * far_below, 0.0, top)

        def attend(quad, carry):
            total, out = carry
            values = []
            for n, (src, z_at, _) in enumerate(chip_pieces(core, own, other, quad)):
                p = jnp.exp2((score[quad, rows_of(n), :] - top) * to_two)
                total = total + jnp.sum(p.reshape(BLOCK // 8, 8, wide), axis=0)
                prob[w, quad, rows_of(n), :] = p.astype(bf16)
                values.append(src[z_at, VALUES, :])
            out = out + first_first(jnp.concatenate(values, axis=0), prob[w, quad])
            return total, out

        total, out = lax.fori_loop(
            first_quad,
            last_quad + 1,
            attend,
            (jnp.zeros((8, wide), f32), jnp.zeros((HEAD, wide), f32)),
        )
        total = jnp.sum(total, axis=0, keepdims=True)
        some = total > 0.0
        safe = jnp.where(some, total, 1.0)
        out_ref[w] = out * (1.0 / safe)
        log_top = top * to_two
        log_sum = jnp.where(some, log_top + jnp.log2(safe), far_below)
        filled = jnp.where(some, 1.0, 0.0)
        stats[w] = jnp.concatenate(
            [log_top, log_sum, filled, jnp.zeros((5, wide), f32)], axis=0
        )

    cross = 1 - yh
    payload[0:HEAD, :] = out_ref[cross].astype(bf16)
    log_sum = stats[cross, 1:2, :]
    high = log_sum.astype(bf16)
    rest = log_sum - high.astype(f32)
    mid = rest.astype(bf16)
    low = (rest - mid.astype(f32)).astype(bf16)
    payload[HEAD : HEAD + 16, :] = jnp.concatenate(
        [high, mid, low, jnp.zeros((13, wide), bf16)], axis=0
    )


def backward(
    heads,
    z_count,
    meta,
    own,
    other,
    query,
    start_ref,
    prob,
    out_ref,
    stats,
    come,
    gout_t,
    low_ref,
    attended,
    dquery,
    dquery_across,
    send_own,
    send_other,
    sum_own,
    sum_other,
    gscaled,
):
    wide = heads * BLOCK
    yh, core = meta[0], meta[2]
    sum_own[...] = jnp.zeros(sum_own.shape, f32)
    sum_other[...] = jnp.zeros(sum_other.shape, f32)
    send_own[:, KV:GRAD, :] = jnp.zeros((z_count, 2 * UPS, HEAD), bf16)
    send_other[:, KV:GRAD, :] = jnp.zeros((z_count, 2 * UPS, HEAD), bf16)
    pieces = come[HEAD : HEAD + 16, :].astype(f32)
    come_log = pieces[0:1] + pieces[1:2] + pieces[2:3]

    for w in range(2):
        crossed = (1 - yh) == w
        log_top, log_sum, filled = (stats[w, i : i + 1, :] for i in range(3))
        far_log = jnp.where(crossed, come_log, far_below)
        most = jnp.maximum(log_sum, far_log)
        log_all = most + jnp.log2(jnp.exp2(log_sum - most) + jnp.exp2(far_log - most))
        far_share = jnp.where(crossed, jnp.exp2(far_log - log_all), 0.0)
        out = (
            out_ref[w] * jnp.exp2(log_sum - log_all)
            + come[0:HEAD, :].astype(f32) * far_share
        )
        scale = jnp.where(filled > 0.0, jnp.exp2(log_top - log_all), 0.0)
        gout = gout_t[w]
        delta = jnp.sum(gout * out.astype(bf16).astype(f32), axis=0, keepdims=True) * scale
        gout = gout * scale
        for h in range(heads):
            columns = slice(h * HEAD, (h + 1) * HEAD)
            if w == 0:
                attended[:, columns] = out[:, columns].T
            gscaled[h * BLOCK : (h + 1) * BLOCK, :] = gout[:, columns].T.astype(bf16)
        grads = gscaled[...]
        queries = query[w]
        first_quad, last_quad = quad_range(meta, z_count, w, start_ref[w])

        def step(quad, dq):
            keys, dscores = [], []
            places = chip_pieces(core, (own, sum_own), (other, sum_other), quad)
            for n, ((src, dst), z_at, _) in enumerate(places):
                p = prob[w, quad, rows_of(n), :]
                dp = last_last(src[z_at, VALUES, :], grads)
                ds = (p.astype(f32) * (dp - delta)).astype(bf16)
                dst[z_at, KEYS, :] += plain(ds, queries)
                dst[z_at, VALUES, :] += plain(p, grads)
                keys.append(src[z_at, KEYS, :])
                dscores.append(ds)
            return dq + first_first(
                jnp.concatenate(keys, axis=0), jnp.concatenate(dscores, axis=0)
            )

        dq = lax.fori_loop(first_quad, last_quad + 1, step, jnp.zeros((HEAD, wide), f32))
        dq = dq * inverse
        low = low_ref[w]
        for h in range(heads):
            columns = slice(h * HEAD, (h + 1) * HEAD)
            dq_h = dq[:, columns].T
            dq_low = dq_h.astype(bf16)
            if w == 0:
                dquery[:, columns] = dq_h
            else:
                dquery_across[:, columns] = dq_low
            up = adapter_scale * first_first(low, dq_low)
            for j in range(2):
                z_at, slot = expert_at(meta, z_count, w, j)
                at = pl.ds(pl.multiple_of(KV + slot * UPS + 16 * h, 16), 16)
                for i in range(2):
                    row = j * RANK + 32 * i
                    even, odd = up[row : row + 16, :], up[row + 16 : row + 32, :]
                    for ref, part in (
                        (send_own, jnp.where(core == 0, even, odd)),
                        (send_other, jnp.where(core == 0, odd, even)),
                    ):
                        ref[z_at + i, at, :] = (
                            ref[z_at + i, at, :].astype(f32) + part
                        ).astype(bf16)

    for src, dst in ((sum_own, send_own), (sum_other, send_other)):
        dst[:, KEYS, :] = (src[:, KEYS, :] * inverse).astype(bf16)
        dst[:, VALUES, :] = src[:, VALUES, :].astype(bf16)


def swap(array, distance):
    count = lax.axis_size("ctx")
    return lax.ppermute(array, "ctx", [(i, i ^ distance) for i in range(count)])


def shards(
    normed,
    frozen_query,
    input_keys,
    input_values,
    document_index,
    routes,
    adapter_down_weight,
    adapter_up_weight,
    output_gradient,
):
    z_count = lax.axis_size("ctx") // 4
    across = 2 * z_count
    exp_count = lax.axis_size("exp")
    place = lax.axis_index("ctx")
    runs = [
        [(yh * z_count + z) * 2 + core for z in range(z_count)]
        for yh in range(2)
        for core in range(2)
    ]
    rows = normed.shape[0]
    wide = frozen_query.shape[1]
    heads = wide // HEAD
    stack = heads * rows
    up_rows = adapter_up_weight.shape[0]
    vmem = pl.BlockSpec(memory_space=pltpu.VMEM)
    smem = pl.BlockSpec(memory_space=pltpu.SMEM)

    ups = adapter_up_weight.reshape(up_rows, heads, HEAD).transpose(1, 0, 2)
    ups = ups.reshape(up_rows * heads, HEAD)
    lower = document_index[:, None] < jnp.arange(128, dtype=jnp.int32)[None, :]
    counts = jnp.sum(lower.astype(f32), axis=0, keepdims=True).astype(bf16)
    small = jnp.concatenate([ups, jnp.pad(counts, ((0, 15), (0, 0)))], axis=0)
    small_across = swap(small, across)
    pack = jnp.concatenate(
        [
            input_keys,
            input_values,
            ups,
            small_across[:UPS],
            small[UPS:] + small_across[UPS:],
        ],
        axis=0,
    )
    own = lax.all_gather(pack, "ctx", axis=0, tiled=False, axis_index_groups=runs)

    chosen = [
        lax.dynamic_index_in_dim(adapter_down_weight, routes[0, j], 0, keepdims=False)
        for j in range(2)
    ]
    partial = jnp.dot(normed, jnp.concatenate(chosen, axis=1), preferred_element_type=f32)
    lows = lax.all_to_all(
        jnp.broadcast_to(partial[None], (exp_count,) + partial.shape), "exp", 0, 0
    )
    low = pl.pallas_call(
        sum_low,
        out_shape=jax.ShapeDtypeStruct(partial.shape, bf16),
        in_specs=[vmem],
        out_specs=vmem,
    )(lows)
    low = jnp.stack([low, swap(low, across)])
    local = jnp.concatenate([frozen_query, output_gradient], axis=0)
    local, _ = lax.optimization_barrier((local, pack))
    pair = jnp.stack([local, swap(local, across)])
    ints = jnp.concatenate(
        [document_index.reshape(1, rows), jnp.pad(routes, ((0, 7 - 1), (0, rows - 2)))], axis=0
    )
    ints, _ = lax.optimization_barrier((ints, pack))
    ints = jnp.stack([ints, swap(ints, across)])
    frozen, gout_t, pick = pl.pallas_call(
        functools.partial(prepare, heads),
        out_shape=(
            jax.ShapeDtypeStruct((2, stack, HEAD), bf16),
            jax.ShapeDtypeStruct((2, HEAD, stack), f32),
            jax.ShapeDtypeStruct((2, 128, rows), bf16),
        ),
        in_specs=[vmem] * 2,
        out_specs=(vmem,) * 3,
    )(pair, ints)
    meta = jnp.stack(
        [
            place // across,
            place // 2 % z_count,
            place % 2,
            ints[0, 1, 0],
            ints[0, 1, 1],
            ints[1, 1, 0],
            ints[1, 1, 1],
        ]
    ).astype(jnp.int32)
    own, low, frozen, gout_t, pick, meta = lax.optimization_barrier(
        (own, low, frozen, gout_t, pick, meta)
    )
    other = swap(own, 1)

    quads = z_count // 2
    query, start, prob, out, stats, payload = pl.pallas_call(
        functools.partial(forward, heads, z_count),
        out_shape=(
            jax.ShapeDtypeStruct((2, stack, HEAD), bf16),
            jax.ShapeDtypeStruct((2, 8, stack), jnp.int32),
            jax.ShapeDtypeStruct((2, quads, QUAD, stack), bf16),
            jax.ShapeDtypeStruct((2, HEAD, stack), f32),
            jax.ShapeDtypeStruct((2, 8, stack), f32),
            jax.ShapeDtypeStruct((HEAD + 16, stack), bf16),
        ),
        in_specs=[smem] + [vmem] * 5,
        out_specs=(vmem,) * 6,
        scratch_shapes=[pltpu.VMEM((quads, QUAD, stack), f32)],
        compiler_params=pltpu.CompilerParams(vmem_limit_bytes=30 * 1024 * 1024),
    )(meta, own, other, low, frozen, pick)
    come = swap(payload, across)

    send = jax.ShapeDtypeStruct((z_count, GRAD, HEAD), bf16)
    attended, dquery, dquery_across, send_own, send_other = pl.pallas_call(
        functools.partial(backward, heads, z_count),
        out_shape=(
            jax.ShapeDtypeStruct((rows, wide), f32),
            jax.ShapeDtypeStruct((rows, wide), f32),
            jax.ShapeDtypeStruct((rows, wide), bf16),
            send,
            send,
        ),
        in_specs=[smem] + [vmem] * 10,
        out_specs=(vmem,) * 5,
        scratch_shapes=[
            pltpu.VMEM((z_count, KV, HEAD), f32),
            pltpu.VMEM((z_count, KV, HEAD), f32),
            pltpu.VMEM((stack, HEAD), bf16),
        ],
        compiler_params=pltpu.CompilerParams(vmem_limit_bytes=30 * 1024 * 1024),
    )(meta, own, other, query, start, prob, out, stats, come, gout_t, low)

    chip = send_own + swap(send_other, 1)
    grads = lax.psum_scatter(
        chip, "ctx", scatter_dimension=0, tiled=False, axis_index_groups=runs
    )
    dquery_across, _ = lax.optimization_barrier((dquery_across, chip))
    dquery = dquery + swap(dquery_across, across).astype(f32)
    up_grad = grads[KV : KV + UPS].astype(f32) + swap(grads[KV + UPS :], across).astype(f32)
    up_grad = up_grad.reshape(heads, up_rows, HEAD).transpose(1, 0, 2)
    return (
        attended,
        dquery,
        grads[KEYS].astype(f32),
        grads[VALUES].astype(f32),
        up_grad.reshape(up_rows, wide),
    )


def solution(mesh):
    both = P("ctx", "exp")
    return jax.shard_map(
        shards,
        mesh=mesh,
        in_specs=(
            both,
            both,
            both,
            both,
            P("ctx"),
            P("ctx", None),
            P(None, "exp", None),
            both,
            both,
        ),
        out_specs=(both,) * 5,
        check_vma=False,
    )
```

time: 1530 us -> 224 us (0.15); the launches traced: 1500 us -> 222 us
  waiting for transfers between devices: 874 us -> 123 us
  starting transfers between devices: 247 us -> 36.2 us
  other arithmetic: 193 us -> 7.56 us
  blocking collectives: 115 us -> 0 us
  local copies, waits for them, and re-layouts: 40.9 us -> 15.6 us
  Pallas kernels: 0 us -> 21.7 us
    ppermute x126 -> x9, waiting for transfers between devices: 349 us -> 25.4 us  [swap(): return lax.ppermute(array, 'ctx', [(i, i ^ distance) for i in range(count)])]
    all_gather x3 -> x1, waiting for transfers between devices: 306 us -> 37.7 us  [shards(): lax.all_gather(pack, 'ctx', axis=0, tiled=False, axis_index_groups=runs)]
    ppermute x126 -> x9, starting transfers between devices: 247 us -> 26.9 us  [swap(): return lax.ppermute(array, 'ctx', [(i, i ^ distance) for i in range(count)])]
    add x196 -> x3, other arithmetic: 191 us -> 3.06 us  [the longest x1 1.61 us: shards(): chip = send_own + swap(send_other, 1)]
    reduce_scatter x1, waiting for transfers between devices: 217 us -> 59.8 us  [shards(): lax.psum_scatter(chip, 'ctx', scatter_dimension=0, tiled=False, axis_inde...]
    all_gather x1 -> x0, blocking collectives: 81 us -> none  [shards(): doc_piece = lax.all_gather(document_index, 'ctx', axis=0, tiled=True)]
    psum x1 -> x0, blocking collectives: 34.2 us -> none  [shards(): low_rank = lax.psum(partial_low, 'exp').astype(jnp.bfloat16)]
    iota x79 -> x0, local copies, waits for them, and re-layouts: 33.6 us -> none  [shards(): query_pos = first_row + jnp.arange(local_rows, dtype=jnp.int32)]
  transfers between devices with their start and end apart: 130 -> 12, of which waited for: 130 -> 9; matrix products, arithmetic and copies ran while one was open for 10% -> 6% of each run, Pallas kernels for 0% -> 2%
where the time goes in v1:
time: 224 us; the launch traced here: 222 us
  waiting for transfers between devices  123 us (55%)
  starting transfers between devices  36.2 us (16%)
  Pallas kernels  21.7 us (10%)
  between operations  18.1 us (8%)
  local copies, waits for them, and re-layouts  15.6 us (7%)
  other arithmetic  7.56 us (3%)
    reduce_scatter x1, waiting for transfers between devices, shards(): lax.psum_scatter(chip, 'ctx', scatter_dimension=0, tiled=False, axis_inde...  59.8 us
    all_gather x1, waiting for transfers between devices, shards(): lax.all_gather(pack, 'ctx', axis=0, tiled=False, axis_index_groups=runs)  37.7 us
    ppermute x9, starting transfers between devices, swap(): return lax.ppermute(array, 'ctx', [(i, i ^ distance) for i in range(count)])  26.9 us
    ppermute x9, waiting for transfers between devices, swap(): return lax.ppermute(array, 'ctx', [(i, i ^ distance) for i in range(count)])  25.4 us
    pallas_call x1, Pallas kernels, shards(): pl.pallas_call(functools.partial(backward, heads, z_count), out_shape=(ja...  11.2 us
    all_to_all x1, starting transfers between devices, shards(): lax.all_to_all(jnp.broadcast_to(partial[None], (exp_count,) + partial.sha...  9.28 us
    pallas_call x1, Pallas kernels, shards(): pl.pallas_call(functools.partial(forward, heads, z_count), out_shape=(jax...  6.74 us
    unnamed x28, local copies, waits for them, and re-layouts  6.26 us
  transfers between devices with their start and end apart: 12, of which 9 were waited for; matrix products, arithmetic and copies ran while one was open for 6% of the time, Pallas kernels for 2%

profile of v1, /device:TPU:6, one launch (start us, length us, event | category | flops | bytes accessed | tf_op | source)
XLA Modules:
  0.0 222.3 jit_solution(9571443066413974367)
XLA Ops:
  8.7 5.1 %collective-permute-start = (bf16[80,128]{1,0:T(8,128)(2,1)S(1)}, bf16[80,128]{1,0:T(8,128)(2,1)S(1)}, u32[]{:S(2)}, u32[]{:S(2)}) collective-permute-start(bf16[80,128]{1,0:T(8,128)(2,1)S(1)} %pad_maximum_fusion.3), channel_id=1, source_target_pairs={{0,256},{8,264},{16,272},{24,280},{32,288},{40,296},{48,304},{56,3... | collective-permute-start | bytes 61448 | tf_op jit(solution)/shard_map/ppermute | solution.py:324
  24.0 9.3 %all-to-all-start = ((f32[8,128,128]{2,1,0:T(8,128)}), f32[8,128,128]{2,1,0:T(8,128)S(1)}, u32[]{:S(2)}, u32[]{:S(2)}) async-start(f32[8,128,128]{2,1,0:T(8,128)} %broadcast_in_dim.2), calls=%async_computation | async-start | bytes 1048576 | tf_op jit(solution)/shard_map/all_to_all | solution.py:378
  33.4 1.9 collective-permute-start.3
  35.3 5.4 %collective-permute-start.2 = (bf16[256,512]{1,0:T(8,128)(2,1)S(1)}, bf16[256,512]{1,0:T(8,128)(2,1)S(1)}, u32[]{:S(2)}, u32[]{:S(2)}) collective-permute-start(bf16[256,512]{1,0:T(8,128)(2,1)S(1)} %pad_maximum_fusion.1), channel_id=1, source_target_pairs={{0,256},{8,264},{16,272},{24,280},{32,288},{40,296},{48,304},{56,3... | collective-permute-start | bytes 786440 | tf_op jit(solution)/shard_map/ppermute | solution.py:324
  42.0 2.7 %stack.51.meta = s32[7]{0:T(128)S(1)} concatenate(s32[1]{0:T(128)} %bitcast.17, s32[1]{0:T(128)} %bitcast.18, s32[1]{0:T(128)} %bitcast.19, s32[1]{0:T(128)} %bitcast.20, s32[1]{0:T(128)} %bitcast.21, s32[1]{0:T(128)} %bitcast.22, s32[1]{0:T(128)} %bitcast.23), dimensions={0} | concatenate | bytes 56 | tf_op jit(solution)/shard_map/stack | solution.py:406
  46.2 1.7 shard_map.128
  47.9 1.9 collective-permute-start.1
  50.6 2.0 shard_map.129
  52.7 2.7 %collective-permute-done.1 = bf16[128,128]{1,0:T(8,128)(2,1)S(1)} collective-permute-done((bf16[128,128]{1,0:T(8,128)(2,1)}, bf16[128,128]{1,0:T(8,128)(2,1)S(1)}, u32[]{:S(2)}, u32[]{:S(2)}) %collective-permute-start.1) | collective-permute-done | bytes 32800 | tf_op jit(solution)/shard_map/ppermute | solution.py:324
  56.1 37.7 %all-gather.3.cloned.1.call-done = bf16[6400,128]{1,0:T(8,128)(2,1)} async-done(((bf16[400,128]{1,0:T(8,128)(2,1)}), bf16[6400,128]{1,0:T(8,128)(2,1)}) %all-gather.3.cloned.1.call-update) | async-done | bytes 1638416 | tf_op jit(solution)/shard_map/all_gather | solution.py:371
  93.8 1.9 collective-permute-start.4
  95.7 3.7 %collective-permute-done.4.other = bf16[16,400,128]{2,1,0:T(8,128)(2,1)S(1)} collective-permute-done((bf16[16,400,128]{2,1,0:T(8,128)(2,1)}, bf16[16,400,128]{2,1,0:T(8,128)(2,1)S(1)}, u32[]{:S(2)}, u32[]{:S(2)}) %collective-permute-start.4) | collective-permute-done | bytes 1638432 | tf_op jit(solution)/shard_map/ppermute | solution.py:324
  102.6 6.7 %shard_map.130 = (bf16[2,512,128]{2,1,0:T(8,128)(2,1)S(1)}, s32[2,8,512]{2,1,0:T(8,128)S(1)}, bf16[2,8,512,512]{3,2,1,0:T(8,128)(2,1)S(1)}, f32[2,128,512]{2,1,0...) custom-call(s32[7]{0:T(128)S(1)} %stack.51.meta, bf16[16,400,128]{2,1,0:T(8,128)(2,1)S(1)} %bitcast.60, ...), custom_call_target="tpu_custom_call" | custom-call | tf_op jit(solution)/shard_map/pallas_call | solution.py:423
  109.4 1.9 collective-permute-start.5
  111.3 7.4 %collective-permute-done.5.come = bf16[144,512]{1,0:T(8,128)(2,1)S(1)} collective-permute-done((bf16[144,512]{1,0:T(8,128)(2,1)S(1)}, bf16[144,512]{1,0:T(8,128)(2,1)S(1)}, u32[]{:S(2)}, u32[]{:S(2)}) %collective-permute-start.5) | collective-permute-done | bytes 147488 | tf_op jit(solution)/shard_map/ppermute | solution.py:324
  118.7 11.2 %shard_map.131 = (f32[128,512]{1,0:T(8,128)}, f32[128,512]{1,0:T(8,128)S(1)}, bf16[128,512]{1,0:T(8,128)(2,1)S(1)}, bf16[16,384,128]{2,1,0:T(8,128)(2,1)S(1)}, bf16[16,384,128]{2,1,0:T(8,128)(2,1)S(1)}) custom-call(s32[7]{0:T(128)S(1)} %stack.51.meta, bf16[16,400,128]{2,1,0:T(8,128)(2,1)S(1)} %bitcast.61, ...), custom_call_target="tpu_custom_call" | custom-call | tf_op jit(solution)/shard_map/pallas_call | solution.py:441
  129.9 1.9 collective-permute-start.6
  131.8 3.4 %collective-permute-done.6 = bf16[16,384,128]{2,1,0:T(8,128)(2,1)S(1)} collective-permute-done((bf16[16,384,128]{2,1,0:T(8,128)(2,1)S(1)}, bf16[16,384,128]{2,1,0:T(8,128)(2,1)S(1)}, u32[]{:S(2)}, u32[]{:S(2)}) %collective-permute-start.6) | collective-permute-done | bytes 1572896 | tf_op jit(solution)/shard_map/ppermute | solution.py:324
  135.2 1.6 add.39
  136.8 1.9 collective-permute-start.7
  138.8 7.0 %collective-permute-done.7 = bf16[128,512]{1,0:T(8,128)(2,1)S(1)} collective-permute-done((bf16[128,512]{1,0:T(8,128)(2,1)S(1)}, bf16[128,512]{1,0:T(8,128)(2,1)S(1)}, u32[]{:S(2)}, u32[]{:S(2)}) %collective-permute-start.7) | collective-permute-done | bytes 131104 | tf_op jit(solution)/shard_map/ppermute | solution.py:324
  146.5 59.8 %reduce-scatter.2.cloned.1.call-done = bf16[1,384,128]{2,1,0:T(8,128)(2,1)} async-done(((bf16[16,384,128]{2,1,0:T(8,128)(2,1)}), bf16[1,384,128]{2,1,0:T(8,128)(2,1)}) %reduce-scatter.2.cloned.1.call-update) | async-done | bytes 98320 | tf_op jit(solution)/shard_map/reduce_scatter | solution.py:461
  207.0 4.9 %collective-permute-start.8 = (bf16[64,128]{1,0:T(8,128)(2,1)S(1)}, bf16[64,128]{1,0:T(8,128)(2,1)S(1)}, u32[]{:S(2)}, u32[]{:S(2)}) collective-permute-start(bf16[64,128]{1,0:T(8,128)(2,1)S(1)} %slice_bitcast_fusion.2), channel_id=1, source_target_pairs={{0,256},{8,264},{16,272},{24,280},{32,288},{40,296},{48,304},{56,3... | collective-permute-start | bytes 49160 | tf_op jit(solution)/shard_map/ppermute | solution.py:324
  211.9 1.4 fusion.3
  (58 shorter events, 18.9 us)
Async XLA Ops:
  7.2 15.6 %copy-start = (bf16[128,1024]{1,0:T(8,128)(2,1)S(1)}, bf16[128,1024]{1,0:T(8,128)(2,1)}, u32[]{:S(2)}) copy-start(bf16[128,1024]{1,0:T(8,128)(2,1)} %param.9) | copy-start | bytes 786436
  7.2 86.6 %all-gather.3.cloned.1.call-start = ((), (), s32[]{:S(2)}) async-start(), calls=%async_computation.3 | async-start | bytes 1740800 | tf_op jit(solution)/shard_map/all_gather | solution.py:371
  8.7 7.2 %collective-permute-start = (bf16[80,128]{1,0:T(8,128)(2,1)S(1)}, bf16[80,128]{1,0:T(8,128)(2,1)S(1)}, u32[]{:S(2)}, u32[]{:S(2)}) collective-permute-start(bf16[80,128]{1,0:T(8,128)(2,1)S(1)} %pad_maximum_fusion.3), channel_id=1, source_target_pairs={{0,256},{8,264},{16,272},{24,280},{32,288},{40,296},{48,304},{56,3... | collective-permute-start | bytes 61448 | tf_op jit(solution)/shard_map/ppermute | solution.py:324
  14.6 18.7 %copy-start.10 = (s32[1,2]{1,0:T(1,128)S(1)}, s32[1,2]{1,0:T(1,128)}, u32[]{:S(2)}) copy-start(s32[1,2]{1,0:T(1,128)} %param.14) | copy-start | bytes 28
  14.6 18.7 %copy-start.11 = (s32[128]{0:T(128)S(1)}, s32[128]{0:T(128)}, u32[]{:S(2)}) copy-start(s32[128]{0:T(128)} %param.13) | copy-start | bytes 1540
  15.4 17.9 %copy-start.8 = (bf16[128,512]{1,0:T(8,128)(2,1)S(1)}, bf16[128,512]{1,0:T(8,128)(2,1)}, u32[]{:S(2)}) copy-start(bf16[128,512]{1,0:T(8,128)(2,1)} %param.17) | copy-start | bytes 393220
  15.4 17.9 %copy-start.9 = (bf16[128,512]{1,0:T(8,128)(2,1)S(1)}, bf16[128,512]{1,0:T(8,128)(2,1)}, u32[]{:S(2)}) copy-start(bf16[128,512]{1,0:T(8,128)(2,1)} %param.10) | copy-start | bytes 393220
  15.9 0.6 copy-start.7
  24.0 21.4 %all-to-all-start = ((f32[8,128,128]{2,1,0:T(8,128)}), f32[8,128,128]{2,1,0:T(8,128)S(1)}, u32[]{:S(2)}, u32[]{:S(2)}) async-start(f32[8,128,128]{2,1,0:T(8,128)} %broadcast_in_dim.2), calls=%async_computation | async-start | bytes 1048576 | tf_op jit(solution)/shard_map/all_to_all | solution.py:378
  33.3 173.0 %reduce-scatter.2.cloned.1.call-start = ((), (), s32[]{:S(2)}) async-start(), calls=%async_computation.2 | async-start | bytes 1671168 | tf_op jit(solution)/shard_map/reduce_scatter | solution.py:461
  33.4 8.0 %collective-permute-start.3 = (s32[8,128]{1,0:T(8,128)S(1)}, s32[8,128]{1,0:T(8,128)S(1)}, u32[]{:S(2)}, u32[]{:S(2)}) collective-permute-start(s32[8,128]{1,0:T(8,128)S(1)} %pad_add_fusion.1), channel_id=1, source_target_pairs={{0,256},{8,264},{16,272},{24,280},{32,288},{40,296},{48,304},{56,3... | collective-permute-start | bytes 12296 | tf_op jit(solution)/shard_map/ppermute | solution.py:324
  35.3 14.4 %collective-permute-start.2 = (bf16[256,512]{1,0:T(8,128)(2,1)S(1)}, bf16[256,512]{1,0:T(8,128)(2,1)S(1)}, u32[]{:S(2)}, u32[]{:S(2)}) collective-permute-start(bf16[256,512]{1,0:T(8,128)(2,1)S(1)} %pad_maximum_fusion.1), channel_id=1, source_target_pairs={{0,256},{8,264},{16,272},{24,280},{32,288},{40,296},{48,304},{56,3... | collective-permute-start | bytes 786440 | tf_op jit(solution)/shard_map/ppermute | solution.py:324
  45.4 0.8 copy-start.6
  47.9 7.5 %collective-permute-start.1 = (bf16[128,128]{1,0:T(8,128)(2,1)}, bf16[128,128]{1,0:T(8,128)(2,1)S(1)}, u32[]{:S(2)}, u32[]{:S(2)}) collective-permute-start(bf16[128,128]{1,0:T(8,128)(2,1)} %shard_map.128), channel_id=1, source_target_pairs={{0,256},{8,264},{16,272},{24,280},{32,288},{40,296},{48,304},{56,3... | collective-permute-start | bytes 98312 | tf_op jit(solution)/shard_map/ppermute | solution.py:324
  93.8 5.6 %collective-permute-start.4 = (bf16[16,400,128]{2,1,0:T(8,128)(2,1)}, bf16[16,400,128]{2,1,0:T(8,128)(2,1)S(1)}, u32[]{:S(2)}, u32[]{:S(2)}) collective-permute-start(bf16[16,400,128]{2,1,0:T(8,128)(2,1)} %bitcast.59), channel_id=1, source_target_pairs={{0,8},{8,0},{16,24},{24,16},{32,40},{40,32},{48,56},{56,48},{64,72... | collective-permute-start | bytes 4915208 | tf_op jit(solution)/shard_map/ppermute | solution.py:324
  99.4 1.4 copy-start.1
  100.8 0.9 copy-start.4
  101.8 0.8 copy-start.5
  102.6 16.0 %copy-start.2 = (bf16[6400,128]{1,0:T(8,128)(2,1)S(1)}, bf16[6400,128]{1,0:T(8,128)(2,1)}, u32[]{:S(2)}) copy-start(bf16[6400,128]{1,0:T(8,128)(2,1)} %all-gather.3.cloned.1.call-done) | copy-start | bytes 4915204
  102.6 16.0 %copy-start.3 = (f32[2,128,512]{2,1,0:T(8,128)S(1)}, f32[2,128,512]{2,1,0:T(8,128)}, u32[]{:S(2)}) copy-start(f32[2,128,512]{2,1,0:T(8,128)} %get-tuple-element.44.gout_t) | copy-start | bytes 1572868
  109.4 9.3 %collective-permute-start.5 = (bf16[144,512]{1,0:T(8,128)(2,1)S(1)}, bf16[144,512]{1,0:T(8,128)(2,1)S(1)}, u32[]{:S(2)}, u32[]{:S(2)}) collective-permute-start(bf16[144,512]{1,0:T(8,128)(2,1)S(1)} %get-tuple-element.43), channel_id=1, source_target_pairs={{0,256},{8,264},{16,272},{24,280},{32,288},{40,296},{48,304},{56,3... | collective-permute-start | bytes 442376 | tf_op jit(solution)/shard_map/ppermute | solution.py:324
  129.9 5.3 %collective-permute-start.6 = (bf16[16,384,128]{2,1,0:T(8,128)(2,1)S(1)}, bf16[16,384,128]{2,1,0:T(8,128)(2,1)S(1)}, u32[]{:S(2)}, u32[]{:S(2)}) collective-permute-start(bf16[16,384,128]{2,1,0:T(8,128)(2,1)S(1)} %get-tuple-element.49), channel_id=1, source_target_pairs={{0,8},{8,0},{16,24},{24,16},{32,40},{40,32},{48,56},{56,48},{64,72... | collective-permute-start | bytes 4718600 | tf_op jit(solution)/shard_map/ppermute | solution.py:324
  136.8 8.9 %collective-permute-start.7 = (bf16[128,512]{1,0:T(8,128)(2,1)S(1)}, bf16[128,512]{1,0:T(8,128)(2,1)S(1)}, u32[]{:S(2)}, u32[]{:S(2)}) collective-permute-start(bf16[128,512]{1,0:T(8,128)(2,1)S(1)} %get-tuple-element.50), channel_id=1, source_target_pairs={{0,256},{8,264},{16,272},{24,280},{32,288},{40,296},{48,304},{56,3... | collective-permute-start | bytes 393224 | tf_op jit(solution)/shard_map/ppermute | solution.py:324
  207.0 7.1 %collective-permute-start.8 = (bf16[64,128]{1,0:T(8,128)(2,1)S(1)}, bf16[64,128]{1,0:T(8,128)(2,1)S(1)}, u32[]{:S(2)}, u32[]{:S(2)}) collective-permute-start(bf16[64,128]{1,0:T(8,128)(2,1)S(1)} %slice_bitcast_fusion.2), channel_id=1, source_target_pairs={{0,256},{8,264},{16,272},{24,280},{32,288},{40,296},{48,304},{56,3... | collective-permute-start | bytes 49160 | tf_op jit(solution)/shard_map/ppermute | solution.py:324
Sparse Core Ops, SparseCore 0:
  16.7 77.0 all-gather.2
  136.9 69.3 reduce-scatter.1

commit v2 on v1

--- a/solution.py
+++ b/solution.py
@@ -23,6 +23,7 @@
 KV = 2 * BLOCK
 UPS = 64
 GRAD = KV + 2 * UPS
+HALF = GRAD // 2
 PACK = GRAD + 16
 KEYS, VALUES = slice(0, BLOCK), slice(BLOCK, KV)
 
@@ -99,12 +100,12 @@
     low_ref,
     frozen,
     pick_ref,
+    gout_t,
     query,
     start_out,
     prob,
     out_ref,
     stats,
-    payload,
     score,
 ):
     wide = heads * BLOCK
@@ -197,24 +198,23 @@
         total = jnp.sum(total, axis=0, keepdims=True)
         some = total > 0.0
         safe = jnp.where(some, total, 1.0)
-        out_ref[w] = out * (1.0 / safe)
+        out = out * (1.0 / safe)
+        out_ref[w] = out
+        row_delta = jnp.sum(gout_t[w] * out, axis=0, keepdims=True)
         log_top = top * to_two
         log_sum = jnp.where(some, log_top + jnp.log2(safe), far_below)
         filled = jnp.where(some, 1.0, 0.0)
         stats[w] = jnp.concatenate(
-            [log_top, log_sum, filled, jnp.zeros((5, wide), f32)], axis=0
+            [log_sum, row_delta, log_top, filled, jnp.zeros((4, wide), f32)], axis=0
         )
 
-    cross = 1 - yh
-    payload[0:HEAD, :] = out_ref[cross].astype(bf16)
-    log_sum = stats[cross, 1:2, :]
-    high = log_sum.astype(bf16)
-    rest = log_sum - high.astype(f32)
-    mid = rest.astype(bf16)
-    low = (rest - mid.astype(f32)).astype(bf16)
-    payload[HEAD : HEAD + 16, :] = jnp.concatenate(
-        [high, mid, low, jnp.zeros((13, wide), bf16)], axis=0
-    )
+
+def shares(log_sum, far_log, crossed):
+    far_log = jnp.where(crossed, far_log, far_below)
+    most = jnp.maximum(log_sum, far_log)
+    log_all = most + jnp.log2(jnp.exp2(log_sum - most) + jnp.exp2(far_log - most))
+    far = jnp.where(crossed, jnp.exp2(far_log - log_all), 0.0)
+    return log_all, jnp.exp2(log_sum - log_all), far
 
 
 def backward(
@@ -226,48 +226,35 @@
     query,
     start_ref,
     prob,
-    out_ref,
     stats,
     come,
     gout_t,
     low_ref,
-    attended,
     dquery,
     dquery_across,
-    send_own,
-    send_other,
+    to_own_a,
+    to_own_b,
+    to_mine_a,
+    to_mine_b,
+    to_theirs_a,
+    to_theirs_b,
     sum_own,
     sum_other,
     gscaled,
 ):
     wide = heads * BLOCK
-    yh, core = meta[0], meta[2]
+    yh, z, core = meta[0], meta[1], meta[2]
     sum_own[...] = jnp.zeros(sum_own.shape, f32)
     sum_other[...] = jnp.zeros(sum_other.shape, f32)
-    send_own[:, KV:GRAD, :] = jnp.zeros((z_count, 2 * UPS, HEAD), bf16)
-    send_other[:, KV:GRAD, :] = jnp.zeros((z_count, 2 * UPS, HEAD), bf16)
-    pieces = come[HEAD : HEAD + 16, :].astype(f32)
-    come_log = pieces[0:1] + pieces[1:2] + pieces[2:3]
 
     for w in range(2):
-        crossed = (1 - yh) == w
-        log_top, log_sum, filled = (stats[w, i : i + 1, :] for i in range(3))
-        far_log = jnp.where(crossed, come_log, far_below)
-        most = jnp.maximum(log_sum, far_log)
-        log_all = most + jnp.log2(jnp.exp2(log_sum - most) + jnp.exp2(far_log - most))
-        far_share = jnp.where(crossed, jnp.exp2(far_log - log_all), 0.0)
-        out = (
-            out_ref[w] * jnp.exp2(log_sum - log_all)
-            + come[0:HEAD, :].astype(f32) * far_share
-        )
+        log_sum, row_delta, log_top, filled = (stats[w, i : i + 1, :] for i in range(4))
+        log_all, near, far = shares(log_sum, come[0:1, :], (1 - yh) == w)
         scale = jnp.where(filled > 0.0, jnp.exp2(log_top - log_all), 0.0)
-        gout = gout_t[w]
-        delta = jnp.sum(gout * out.astype(bf16).astype(f32), axis=0, keepdims=True) * scale
-        gout = gout * scale
+        delta = (row_delta * near + come[1:2, :] * far) * scale
+        gout = gout_t[w] * scale
         for h in range(heads):
             columns = slice(h * HEAD, (h + 1) * HEAD)
-            if w == 0:
-                attended[:, columns] = out[:, columns].T
             gscaled[h * BLOCK : (h + 1) * BLOCK, :] = gout[:, columns].T.astype(bf16)
         grads = gscaled[...]
         queries = query[w]
@@ -306,22 +293,56 @@
                 for i in range(2):
                     row = j * RANK + 32 * i
                     even, odd = up[row : row + 16, :], up[row + 16 : row + 32, :]
-                    for ref, part in (
-                        (send_own, jnp.where(core == 0, even, odd)),
-                        (send_other, jnp.where(core == 0, odd, even)),
-                    ):
-                        ref[z_at + i, at, :] = (
-                            ref[z_at + i, at, :].astype(f32) + part
-                        ).astype(bf16)
-
-    for src, dst in ((sum_own, send_own), (sum_other, send_other)):
-        dst[:, KEYS, :] = (src[:, KEYS, :] * inverse).astype(bf16)
-        dst[:, VALUES, :] = src[:, VALUES, :].astype(bf16)
+                    sum_own[z_at + i, at, :] += jnp.where(core == 0, even, odd)
+                    sum_other[z_at + i, at, :] += jnp.where(core == 0, odd, even)
+
+    def put(first, second, at, src, z_at, valid):
+        keep = jnp.where(valid, 1.0, 0.0)
+        keys = (src[z_at, KEYS, :] * (inverse * keep)).astype(bf16)
+        rest = (src[z_at, BLOCK:GRAD, :] * keep).astype(bf16)
+        first[(*at, slice(0, BLOCK))] = keys
+        first[(*at, slice(BLOCK, HALF))] = rest[0 : HALF - BLOCK]
+        second[at] = rest[HALF - BLOCK :]
+
+    steps = z_count // 2
+    put(to_own_a, to_own_b, (0,), sum_own, z, True)
+    put(to_own_a, to_own_b, (1,), sum_other, z, True)
+    for d in range(steps):
+        up, down = lax.rem(z + d + 1, z_count), lax.rem(z - d - 1 + z_count, z_count)
+        here, there = jnp.where(core == 0, up, down), jnp.where(core == 0, down, up)
+        inner = d < steps - 1
+        for r, src in enumerate((sum_own, sum_other)):
+            put(to_mine_a, to_mine_b, (d, r), src, here, inner or core == 0)
+            put(to_theirs_a, to_theirs_b, (d, 1 - r), src, there, inner or core == 1)
+
+
+def finish(heads, meta, out_t, stats, come, far_out, far_dquery, dquery, attended, dquery_out):
+    _, near, far = shares(stats[0, 0:1, :], come[0:1, :], meta[0] == 1)
+    out = out_t[0] * near + far_out[...].astype(f32) * far
+    for h in range(heads):
+        columns = slice(h * HEAD, (h + 1) * HEAD)
+        attended[:, columns] = out[:, columns].T
+    dquery_out[...] = dquery[...] + far_dquery[...].astype(f32)
 
 
 def swap(array, distance):
     count = lax.axis_size("ctx")
     return lax.ppermute(array, "ctx", [(i, i ^ distance) for i in range(count)])
+
+
+def pass_on(array):
+    z_count = lax.axis_size("ctx") // 4
+    route = []
+    for yh in range(2):
+        for z in range(z_count):
+            for core in range(2):
+                to = (z + (-1 if core else 1)) % z_count
+                route.append(((yh * z_count + z) * 2 + core, (yh * z_count + to) * 2 + core))
+    return lax.ppermute(array, "ctx", route)
+
+
+def added(*parts):
+    return sum(part.astype(f32) for part in parts).astype(bf16)
 
 
 def shards(
@@ -339,6 +360,7 @@
     across = 2 * z_count
     exp_count = lax.axis_size("exp")
     place = lax.axis_index("ctx")
+    steps = z_count // 2
     runs = [
         [(yh * z_count + z) * 2 + core for z in range(z_count)]
         for yh in range(2)
@@ -420,7 +442,7 @@
     other = swap(own, 1)
 
     quads = z_count // 2
-    query, start, prob, out, stats, payload = pl.pallas_call(
+    query, start, prob, out, stats = pl.pallas_call(
         functools.partial(forward, heads, z_count),
         out_shape=(
             jax.ShapeDtypeStruct((2, stack, HEAD), bf16),
@@ -428,48 +450,72 @@
             jax.ShapeDtypeStruct((2, quads, QUAD, stack), bf16),
             jax.ShapeDtypeStruct((2, HEAD, stack), f32),
             jax.ShapeDtypeStruct((2, 8, stack), f32),
-            jax.ShapeDtypeStruct((HEAD + 16, stack), bf16),
         ),
-        in_specs=[smem] + [vmem] * 5,
-        out_specs=(vmem,) * 6,
+        in_specs=[smem] + [vmem] * 6,
+        out_specs=(vmem,) * 5,
         scratch_shapes=[pltpu.VMEM((quads, QUAD, stack), f32)],
         compiler_params=pltpu.CompilerParams(vmem_limit_bytes=30 * 1024 * 1024),
-    )(meta, own, other, low, frozen, pick)
-    come = swap(payload, across)
-
-    send = jax.ShapeDtypeStruct((z_count, GRAD, HEAD), bf16)
-    attended, dquery, dquery_across, send_own, send_other = pl.pallas_call(
+    )(meta, own, other, low, frozen, pick, gout_t)
+    come = swap(jnp.where(place < across, stats[1], stats[0]), across)
+
+    to_chip = jax.ShapeDtypeStruct((2, HALF, HEAD), bf16)
+    to_chips = jax.ShapeDtypeStruct((steps, 2, HALF, HEAD), bf16)
+    dquery, dquery_across, own_a, own_b, mine_a, mine_b, theirs_a, theirs_b = pl.pallas_call(
         functools.partial(backward, heads, z_count),
         out_shape=(
             jax.ShapeDtypeStruct((rows, wide), f32),
-            jax.ShapeDtypeStruct((rows, wide), f32),
             jax.ShapeDtypeStruct((rows, wide), bf16),
-            send,
-            send,
+            to_chip,
+            to_chip,
+            to_chips,
+            to_chips,
+            to_chips,
+            to_chips,
         ),
-        in_specs=[smem] + [vmem] * 10,
-        out_specs=(vmem,) * 5,
+        in_specs=[smem] + [vmem] * 9,
+        out_specs=(vmem,) * 8,
         scratch_shapes=[
-            pltpu.VMEM((z_count, KV, HEAD), f32),
-            pltpu.VMEM((z_count, KV, HEAD), f32),
+            pltpu.VMEM((z_count, GRAD, HEAD), f32),
+            pltpu.VMEM((z_count, GRAD, HEAD), f32),
             pltpu.VMEM((stack, HEAD), bf16),
         ],
         compiler_params=pltpu.CompilerParams(vmem_limit_bytes=30 * 1024 * 1024),
-    )(meta, own, other, query, start, prob, out, stats, come, gout_t, low)
-
-    chip = send_own + swap(send_other, 1)
-    grads = lax.psum_scatter(
-        chip, "ctx", scatter_dimension=0, tiled=False, axis_index_groups=runs
-    )
-    dquery_across, _ = lax.optimization_barrier((dquery_across, chip))
-    dquery = dquery + swap(dquery_across, across).astype(f32)
-    up_grad = grads[KV : KV + UPS].astype(f32) + swap(grads[KV + UPS :], across).astype(f32)
+    )(meta, own, other, query, start, prob, stats, come, gout_t, low)
+
+    from_a, from_b = swap(theirs_a, 1), swap(theirs_b, 1)
+    sum_a = added(mine_a[steps - 1], from_a[steps - 1])
+    sum_b = added(mine_b[steps - 1], from_b[steps - 1])
+    first_sum = sum_a
+    for d in reversed(range(steps)):
+        sum_a, sum_b = pass_on(sum_a), pass_on(sum_b)
+        if d > 0:
+            sum_a = added(sum_a, mine_a[d - 1], from_a[d - 1])
+            sum_b = added(sum_b, mine_b[d - 1], from_b[d - 1])
+    part = jnp.concatenate([added(sum_a, own_a), added(sum_b, own_b)], axis=1)
+
+    far_out = jnp.where(place < across, out[1], out[0]).astype(bf16)
+    far, _ = lax.optimization_barrier((jnp.stack([far_out, dquery_across.reshape(HEAD, stack)]), first_sum))
+    far = swap(far, across)
+    attended, dquery = pl.pallas_call(
+        functools.partial(finish, heads),
+        out_shape=(jax.ShapeDtypeStruct((rows, wide), f32),) * 2,
+        in_specs=[smem] + [vmem] * 6,
+        out_specs=(vmem,) * 2,
+    )(meta, out, stats, come, far[0], far[1].reshape(rows, wide), dquery)
+
+    main = slice(0, KV + UPS)
+    grads = part[0, main].astype(f32) + swap(part[1, main], 1).astype(f32)
+    up_grad = (
+        grads[KV:]
+        + swap(part[0, KV + UPS :], across).astype(f32)
+        + swap(part[1, KV + UPS :], across ^ 1).astype(f32)
+    )
     up_grad = up_grad.reshape(heads, up_rows, HEAD).transpose(1, 0, 2)
     return (
         attended,
         dquery,
-        grads[KEYS].astype(f32),
-        grads[VALUES].astype(f32),
+        grads[KEYS],
+        grads[VALUES],
         up_grad.reshape(up_rows, wide),
     )
 

time: 224 us -> 232 us (1.036)
  starting transfers between devices: 36.2 us -> 93.4 us
  waiting for transfers between devices: 123 us -> 67.8 us
  Pallas kernels: 21.7 us -> 25.1 us
    reduce_scatter x1 -> x0, waiting for transfers between devices: 59.8 us -> none  [shards(): lax.psum_scatter(chip, 'ctx', scatter_dimension=0, tiled=False, axis_inde...]
    ppermute x0 -> x16, starting transfers between devices: none -> 50.3 us  [pass_on(): return lax.ppermute(array, 'ctx', route)]
    ppermute x0 -> x16, waiting for transfers between devices: none -> 14.5 us  [pass_on(): return lax.ppermute(array, 'ctx', route)]
    ppermute x9 -> x12, waiting for transfers between devices: 25.4 us -> 15.9 us  [swap(): return lax.ppermute(array, 'ctx', [(i, i ^ distance) for i in range(count)])]
    ppermute x9 -> x12, starting transfers between devices: 26.9 us -> 33.8 us  [swap(): return lax.ppermute(array, 'ctx', [(i, i ^ distance) for i in range(count)])]
    add x3 -> x2, other arithmetic: 3.06 us -> 0.03 us  [the longest x1 0.02 us: shards(): grads = part[0, main].astype(f32) + swap(part[1, main], 1).astype(f32)]
    unnamed x28 -> x50, local copies, waits for them, and re-layouts: 6.26 us -> 8 us
  transfers between devices with their start and end apart: 12 -> 30, of which waited for: 9 -> 14; matrix products, arithmetic and copies ran while one was open for 6% -> 7% of each run, Pallas kernels for 2% -> 3%
where the time goes in v2:
time: 232 us; the launch traced here: 229 us
  starting transfers between devices  93.4 us (40%)
  waiting for transfers between devices  67.8 us (29%)
  Pallas kernels  25.1 us (11%)
  between operations  18.7 us (8%)
  local copies, waits for them, and re-layouts  17.9 us (8%)
  other arithmetic  6.42 us (3%)
    ppermute x16, starting transfers between devices, pass_on(): return lax.ppermute(array, 'ctx', route)  50.3 us
    all_gather x1, waiting for transfers between devices, shards(): lax.all_gather(pack, 'ctx', axis=0, tiled=False, axis_index_groups=runs)  37.3 us
    ppermute x12, starting transfers between devices, swap(): return lax.ppermute(array, 'ctx', [(i, i ^ distance) for i in range(count)])  33.8 us
    ppermute x12, waiting for transfers between devices, swap(): return lax.ppermute(array, 'ctx', [(i, i ^ distance) for i in range(count)])  15.9 us
    ppermute x16, waiting for transfers between devices, pass_on(): return lax.ppermute(array, 'ctx', route)  14.5 us
    pallas_call x1, Pallas kernels, shards(): pl.pallas_call(functools.partial(backward, heads, z_count), out_shape=(ja...  11.8 us
    all_to_all x1, starting transfers between devices, shards(): lax.all_to_all(jnp.broadcast_to(partial[None], (exp_count,) + partial.sha...  9.28 us
    unnamed x50, local copies, waits for them, and re-layouts  8 us
  transfers between devices with their start and end apart: 30, of which 14 were waited for; matrix products, arithmetic and copies ran while one was open for 7% of the time, Pallas kernels for 3%

profile of v2, /device:TPU:6, one launch (start us, length us, event | category | flops | bytes accessed | tf_op | source)
XLA Modules:
  0.0 229.5 jit_solution(2180905353405084760)
XLA Ops:
  8.9 5.1 %collective-permute-start = (bf16[80,128]{1,0:T(8,128)(2,1)S(1)}, bf16[80,128]{1,0:T(8,128)(2,1)S(1)}, u32[]{:S(2)}, u32[]{:S(2)}) collective-permute-start(bf16[80,128]{1,0:T(8,128)(2,1)S(1)} %pad_maximum_fusion.5), channel_id=1, source_target_pairs={{0,256},{8,264},{16,272},{24,280},{32,288},{40,296},{48,304},{56,3... | collective-permute-start | bytes 61448 | tf_op jit(solution)/shard_map/ppermute | solution.py:330
  24.1 9.3 %all-to-all-start = ((f32[8,128,128]{2,1,0:T(8,128)}), f32[8,128,128]{2,1,0:T(8,128)S(1)}, u32[]{:S(2)}, u32[]{:S(2)}) async-start(f32[8,128,128]{2,1,0:T(8,128)} %broadcast_in_dim.2), calls=%async_computation | async-start | bytes 1048576 | tf_op jit(solution)/shard_map/all_to_all | solution.py:400
  35.5 5.4 %collective-permute-start.2 = (bf16[256,512]{1,0:T(8,128)(2,1)S(1)}, bf16[256,512]{1,0:T(8,128)(2,1)S(1)}, u32[]{:S(2)}, u32[]{:S(2)}) collective-permute-start(bf16[256,512]{1,0:T(8,128)(2,1)S(1)} %pad_maximum_fusion.1), channel_id=1, source_target_pairs={{0,256},{8,264},{16,272},{24,280},{32,288},{40,296},{48,304},{56,3... | collective-permute-start | bytes 786440 | tf_op jit(solution)/shard_map/ppermute | solution.py:330
  42.1 2.6 %stack.58.meta = s32[7]{0:T(128)S(1)} concatenate(s32[1]{0:T(128)} %bitcast.17, s32[1]{0:T(128)} %bitcast.18, s32[1]{0:T(128)} %bitcast.19, s32[1]{0:T(128)} %bitcast.20, s32[1]{0:T(128)} %bitcast.21, s32[1]{0:T(128)} %bitcast.22, s32[1]{0:T(128)} %bitcast.23), dimensions={0} | concatenate | bytes 56 | tf_op jit(solution)/shard_map/stack | solution.py:428
  52.7 2.7 %collective-permute-done.1 = bf16[128,128]{1,0:T(8,128)(2,1)S(1)} collective-permute-done((bf16[128,128]{1,0:T(8,128)(2,1)}, bf16[128,128]{1,0:T(8,128)(2,1)S(1)}, u32[]{:S(2)}, u32[]{:S(2)}) %collective-permute-start.1) | collective-permute-done | bytes 32800 | tf_op jit(solution)/shard_map/ppermute | solution.py:330
  56.1 37.3 %all-gather.3.cloned.1.call-done = bf16[6400,128]{1,0:T(8,128)(2,1)} async-done(((bf16[400,128]{1,0:T(8,128)(2,1)}), bf16[6400,128]{1,0:T(8,128)(2,1)}) %all-gather.3.cloned.1.call-update) | async-done | bytes 1638416 | tf_op jit(solution)/shard_map/all_gather | solution.py:393
  95.4 3.7 %collective-permute-done.4.other = bf16[16,400,128]{2,1,0:T(8,128)(2,1)S(1)} collective-permute-done((bf16[16,400,128]{2,1,0:T(8,128)(2,1)}, bf16[16,400,128]{2,1,0:T(8,128)(2,1)S(1)}, u32[]{:S(2)}, u32[]{:S(2)}) %collective-permute-start.4) | collective-permute-done | bytes 1638432 | tf_op jit(solution)/shard_map/ppermute | solution.py:330
  103.3 7.4 %shard_map.130 = (bf16[2,512,128]{2,1,0:T(8,128)(2,1)S(1)}, s32[2,8,512]{2,1,0:T(8,128)S(1)}, bf16[2,8,512,512]{3,2,1,0:T(8,128)(2,1)S(1)}, f32[2,128,512]{2,1,0:T(8,128)S(1)}, f32[2,8,512]{2,1,0:T(8,128)S(1)}) custom-call(s32[7]{0:T(128)S(1)} %stack.58.meta, bf16[16,400,128]{2,1,0:T(8,128)(2,1)S(1)} %bitcast.177, ...), custom_call_target="tpu_custom_call" | custom-call | tf_op jit(solution)/shard_map/pallas_call | solution.py:445
  112.7 5.2 %collective-permute-done.5.come = f32[8,512]{1,0:T(8,128)S(1)} collective-permute-done((f32[8,512]{1,0:T(8,128)S(1)}, f32[8,512]{1,0:T(8,128)S(1)}, u32[]{:S(2)}, u32[]{:S(2)}) %collective-permute-start.5) | collective-permute-done | bytes 16416 | tf_op jit(solution)/shard_map/ppermute | solution.py:330
  118.6 11.8 %shard_map.131 = (f32[128,512]{1,0:T(8,128)S(1)}, bf16[128,512]{1,0:T(8,128)(2,1)S(1)}, bf16[2,192,128]{2,1,0:T(8,128)(2,1)S(1)}, bf16[2,192,128]{2,1,0:T(8,128)...) custom-call(s32[7]{0:T(128)S(1)} %copy-done.16, ...), custom_call_target="tpu_custom_call" | custom-call | tf_op jit(solution)/shard_map/pallas_call | solution.py:463
  134.9 3.5 %collective-permute-start.8 = (bf16[2,192,128]{2,1,0:T(8,128)(2,1)S(1)}, bf16[2,192,128]{2,1,0:T(8,128)(2,1)S(1)}, u32[]{:S(2)}, u32[]{:S(2)}) collective-permute-start(bf16[2,192,128]{2,1,0:T(8,128)(2,1)S(1)} %fusion.17), channel_id=1, source_target_pairs={{0,16},{8,248},{16,32},{24,8},{32,48},{40,24},{48,64},{56,40},{64,... | collective-permute-start | bytes 294920 | tf_op jit(solution)/shard_map/ppermute | solution.py:341
  140.4 4.0 %collective-permute-start.17 = (bf16[2,192,128]{2,1,0:T(8,128)(2,1)S(1)}, bf16[2,192,128]{2,1,0:T(8,128)(2,1)S(1)}, u32[]{:S(2)}, u32[]{:S(2)}) collective-permute-start(bf16[2,192,128]{2,1,0:T(8,128)(2,1)S(1)} %fusion.18), channel_id=1, source_target_pairs={{0,16},{8,248},{16,32},{24,8},{32,48},{40,24},{48,64},{56,40},{64,... | collective-permute-start | bytes 294920 | tf_op jit(solution)/shard_map/ppermute | solution.py:341
  144.5 3.7 %collective-permute-start.9 = (bf16[2,192,128]{2,1,0:T(8,128)(2,1)S(1)}, bf16[2,192,128]{2,1,0:T(8,128)(2,1)S(1)}, u32[]{:S(2)}, u32[]{:S(2)}) collective-permute-start(bf16[2,192,128]{2,1,0:T(8,128)(2,1)S(1)} %fusion.16), channel_id=1, source_target_pairs={{0,16},{8,248},{16,32},{24,8},{32,48},{40,24},{48,64},{56,40},{64,... | collective-permute-start | bytes 294920 | tf_op jit(solution)/shard_map/ppermute | solution.py:341
  148.3 4.5 %collective-permute-start.18 = (bf16[2,192,128]{2,1,0:T(8,128)(2,1)S(1)}, bf16[2,192,128]{2,1,0:T(8,128)(2,1)S(1)}, u32[]{:S(2)}, u32[]{:S(2)}) collective-permute-start(bf16[2,192,128]{2,1,0:T(8,128)(2,1)S(1)} %fusion.9), channel_id=1, source_target_pairs={{0,16},{8,248},{16,32},{24,8},{32,48},{40,24},{48,64},{56,40},{64,... | collective-permute-start | bytes 294920 | tf_op jit(solution)/shard_map/ppermute | solution.py:341
  152.9 3.1 %collective-permute-start.10 = (bf16[2,192,128]{2,1,0:T(8,128)(2,1)S(1)}, bf16[2,192,128]{2,1,0:T(8,128)(2,1)}, u32[]{:S(2)}, u32[]{:S(2)}) collective-permute-start(bf16[2,192,128]{2,1,0:T(8,128)(2,1)S(1)} %fusion.15), channel_id=1, source_target_pairs={{0,16},{8,248},{16,32},{24,8},{32,48},{40,24},{48,64},{56,40},{64,... | collective-permute-start | bytes 294920 | tf_op jit(solution)/shard_map/ppermute | solution.py:341
  156.7 3.3 %collective-permute-start.19 = (bf16[2,192,128]{2,1,0:T(8,128)(2,1)}, bf16[2,192,128]{2,1,0:T(8,128)(2,1)}, u32[]{:S(2)}, u32[]{:S(2)}) collective-permute-start(bf16[2,192,128]{2,1,0:T(8,128)(2,1)} %fusion.8), channel_id=1, source_target_pairs={{0,16},{8,248},{16,32},{24,8},{32,48},{40,24},{48,64},{56,40},{64,... | collective-permute-start | bytes 294920 | tf_op jit(solution)/shard_map/ppermute | solution.py:341
  163.9 4.3 %collective-permute-start.11 = (bf16[2,192,128]{2,1,0:T(8,128)(2,1)S(1)}, bf16[2,192,128]{2,1,0:T(8,128)(2,1)S(1)}, u32[]{:S(2)}, u32[]{:S(2)}) collective-permute-start(bf16[2,192,128]{2,1,0:T(8,128)(2,1)S(1)} %fusion.14), channel_id=1, source_target_pairs={{0,16},{8,248},{16,32},{24,8},{32,48},{40,24},{48,64},{56,40},{64,... | collective-permute-start | bytes 294920 | tf_op jit(solution)/shard_map/ppermute | solution.py:341
  169.2 2.6 %collective-permute-start.20 = (bf16[2,192,128]{2,1,0:T(8,128)(2,1)S(1)}, bf16[2,192,128]{2,1,0:T(8,128)(2,1)S(1)}, u32[]{:S(2)}, u32[]{:S(2)}) collective-permute-start(bf16[2,192,128]{2,1,0:T(8,128)(2,1)S(1)} %fusion.7), channel_id=1, source_target_pairs={{0,16},{8,248},{16,32},{24,8},{32,48},{40,24},{48,64},{56,40},{64,... | collective-permute-start | bytes 294920 | tf_op jit(solution)/shard_map/ppermute | solution.py:341
  171.9 5.0 %collective-permute-start.12 = (bf16[2,192,128]{2,1,0:T(8,128)(2,1)S(1)}, bf16[2,192,128]{2,1,0:T(8,128)(2,1)S(1)}, u32[]{:S(2)}, u32[]{:S(2)}) collective-permute-start(bf16[2,192,128]{2,1,0:T(8,128)(2,1)S(1)} %fusion.13), channel_id=1, source_target_pairs={{0,16},{8,248},{16,32},{24,8},{32,48},{40,24},{48,64},{56,40},{64,... | collective-permute-start | bytes 294920 | tf_op jit(solution)/shard_map/ppermute | solution.py:341
  179.7 3.8 %collective-permute-start.13 = (bf16[2,192,128]{2,1,0:T(8,128)(2,1)S(1)}, bf16[2,192,128]{2,1,0:T(8,128)(2,1)S(1)}, u32[]{:S(2)}, u32[]{:S(2)}) collective-permute-start(bf16[2,192,128]{2,1,0:T(8,128)(2,1)S(1)} %fusion.12), channel_id=1, source_target_pairs={{0,16},{8,248},{16,32},{24,8},{32,48},{40,24},{48,64},{56,40},{64,... | collective-permute-start | bytes 294920 | tf_op jit(solution)/shard_map/ppermute | solution.py:341
  197.1 3.1 %collective-permute-done.23 = bf16[2,192,128]{2,1,0:T(8,128)(2,1)S(1)} collective-permute-done((bf16[2,192,128]{2,1,0:T(8,128)(2,1)S(1)}, bf16[2,192,128]{2,1,0:T(8,128)(2,1)S(1)}, u32[]{:S(2)}, u32[]{:S(2)}) %collective-permute-start.23) | collective-permute-done | bytes 98336 | tf_op jit(solution)/shard_map/ppermute | solution.py:341
  203.0 5.0 %collective-permute-done.24 = bf16[2,192,128]{2,1,0:T(8,128)(2,1)S(1)} collective-permute-done((bf16[2,192,128]{2,1,0:T(8,128)(2,1)S(1)}, bf16[2,192,128]{2,1,0:T(8,128)(2,1)S(1)}, u32[]{:S(2)}, u32[]{:S(2)}) %collective-permute-start.24) | collective-permute-done | bytes 98336 | tf_op jit(solution)/shard_map/ppermute | solution.py:341
  210.0 5.4 %collective-permute-start.26 = (bf16[64,128]{1,0:T(8,128)(2,1)S(1)}, bf16[64,128]{1,0:T(8,128)(2,1)S(1)}, u32[]{:S(2)}, u32[]{:S(2)}) collective-permute-start(bf16[64,128]{1,0:T(8,128)(2,1)S(1)} %get-tuple-element.65), channel_id=1, source_target_pairs={{0,256},{8,264},{16,272},{24,280},{32,288},{40,296},{48,304},{56,3... | collective-permute-start | bytes 49160 | tf_op jit(solution)/shard_map/ppermute | solution.py:330
  218.2 3.8 %collective-permute-done.27 = bf16[64,128]{1,0:T(8,128)(2,1)S(1)} collective-permute-done((bf16[64,128]{1,0:T(8,128)(2,1)S(1)}, bf16[64,128]{1,0:T(8,128)(2,1)S(1)}, u32[]{:S(2)}, u32[]{:S(2)}) %collective-permute-start.27) | collective-permute-done | bytes 16416 | tf_op jit(solution)/shard_map/ppermute | solution.py:330
  (138 shorter events, 65.0 us)
Async XLA Ops:
  7.2 86.2 %all-gather.3.cloned.1.call-start = ((), (), s32[]{:S(2)}) async-start(), calls=%async_computation.1 | async-start | bytes 1740800 | tf_op jit(solution)/shard_map/all_gather | solution.py:393
  24.1 21.2 %all-to-all-start = ((f32[8,128,128]{2,1,0:T(8,128)}), f32[8,128,128]{2,1,0:T(8,128)S(1)}, u32[]{:S(2)}, u32[]{:S(2)}) async-start(f32[8,128,128]{2,1,0:T(8,128)} %broadcast_in_dim.2), calls=%async_computation | async-start | bytes 1048576 | tf_op jit(solution)/shard_map/all_to_all | solution.py:400
  33.5 7.9 %collective-permute-start.3 = (s32[8,128]{1,0:T(8,128)S(1)}, s32[8,128]{1,0:T(8,128)S(1)}, u32[]{:S(2)}, u32[]{:S(2)}) collective-permute-start(s32[8,128]{1,0:T(8,128)S(1)} %pad_add_fusion.1), channel_id=1, source_target_pairs={{0,256},{8,264},{16,272},{24,280},{32,288},{40,296},{48,304},{56,3... | collective-permute-start | bytes 12296 | tf_op jit(solution)/shard_map/ppermute | solution.py:330
  35.5 14.3 %collective-permute-start.2 = (bf16[256,512]{1,0:T(8,128)(2,1)S(1)}, bf16[256,512]{1,0:T(8,128)(2,1)S(1)}, u32[]{:S(2)}, u32[]{:S(2)}) collective-permute-start(bf16[256,512]{1,0:T(8,128)(2,1)S(1)} %pad_maximum_fusion.1), channel_id=1, source_target_pairs={{0,256},{8,264},{16,272},{24,280},{32,288},{40,296},{48,304},{56,3... | collective-permute-start | bytes 786440 | tf_op jit(solution)/shard_map/ppermute | solution.py:330
  132.4 8.0 %collective-permute-start.16 = (bf16[8,2,192,128]{3,2,1,0:T(8,128)(2,1)S(1)}, bf16[8,2,192,128]{3,2,1,0:T(8,128)(2,1)S(1)}, u32[]{:S(2)}, u32[]{:S(2)}) collective-permute-start(bf16[8,2,192,128]{3,2,1,0:T(8,128)(2,1)S(1)} %get-tuple-element.57), channel_id=1, source_target_pairs={{0,8},{8,0},{16,24},{24,16},{32,40},{40,32},{48,56},{56,48},{64,72... | collective-permute-start | bytes 2359304 | tf_op jit(solution)/shard_map/ppermute | solution.py:330
  134.9 9.5 %collective-permute-start.8 = (bf16[2,192,128]{2,1,0:T(8,128)(2,1)S(1)}, bf16[2,192,128]{2,1,0:T(8,128)(2,1)S(1)}, u32[]{:S(2)}, u32[]{:S(2)}) collective-permute-start(bf16[2,192,128]{2,1,0:T(8,128)(2,1)S(1)} %fusion.17), channel_id=1, source_target_pairs={{0,16},{8,248},{16,32},{24,8},{32,48},{40,24},{48,64},{56,40},{64,... | collective-permute-start | bytes 294920 | tf_op jit(solution)/shard_map/ppermute | solution.py:341
  138.4 21.6 %collective-permute-start.7 = (bf16[2,128,512]{2,1,0:T(8,128)(2,1)S(1)}, bf16[2,128,512]{2,1,0:T(8,128)(2,1)S(1)}, u32[]{:S(2)}, u32[]{:S(2)}) collective-permute-start(bf16[2,128,512]{2,1,0:T(8,128)(2,1)S(1)} %pad_maximum_fusion.2), channel_id=1, source_target_pairs={{0,256},{8,264},{16,272},{24,280},{32,288},{40,296},{48,304},{56,3... | collective-permute-start | bytes 786440 | tf_op jit(solution)/shard_map/ppermute | solution.py:330
  140.4 7.8 %collective-permute-start.17 = (bf16[2,192,128]{2,1,0:T(8,128)(2,1)S(1)}, bf16[2,192,128]{2,1,0:T(8,128)(2,1)S(1)}, u32[]{:S(2)}, u32[]{:S(2)}) collective-permute-start(bf16[2,192,128]{2,1,0:T(8,128)(2,1)S(1)} %fusion.18), channel_id=1, source_target_pairs={{0,16},{8,248},{16,32},{24,8},{32,48},{40,24},{48,64},{56,40},{64,... | collective-permute-start | bytes 294920 | tf_op jit(solution)/shard_map/ppermute | solution.py:341
  144.5 8.3 %collective-permute-start.9 = (bf16[2,192,128]{2,1,0:T(8,128)(2,1)S(1)}, bf16[2,192,128]{2,1,0:T(8,128)(2,1)S(1)}, u32[]{:S(2)}, u32[]{:S(2)}) collective-permute-start(bf16[2,192,128]{2,1,0:T(8,128)(2,1)S(1)} %fusion.16), channel_id=1, source_target_pairs={{0,16},{8,248},{16,32},{24,8},{32,48},{40,24},{48,64},{56,40},{64,... | collective-permute-start | bytes 294920 | tf_op jit(solution)/shard_map/ppermute | solution.py:341
  148.3 7.7 %collective-permute-start.18 = (bf16[2,192,128]{2,1,0:T(8,128)(2,1)S(1)}, bf16[2,192,128]{2,1,0:T(8,128)(2,1)S(1)}, u32[]{:S(2)}, u32[]{:S(2)}) collective-permute-start(bf16[2,192,128]{2,1,0:T(8,128)(2,1)S(1)} %fusion.9), channel_id=1, source_target_pairs={{0,16},{8,248},{16,32},{24,8},{32,48},{40,24},{48,64},{56,40},{64,... | collective-permute-start | bytes 294920 | tf_op jit(solution)/shard_map/ppermute | solution.py:341
  152.9 10.1 %collective-permute-start.10 = (bf16[2,192,128]{2,1,0:T(8,128)(2,1)S(1)}, bf16[2,192,128]{2,1,0:T(8,128)(2,1)}, u32[]{:S(2)}, u32[]{:S(2)}) collective-permute-start(bf16[2,192,128]{2,1,0:T(8,128)(2,1)S(1)} %fusion.15), channel_id=1, source_target_pairs={{0,16},{8,248},{16,32},{24,8},{32,48},{40,24},{48,64},{56,40},{64,... | collective-permute-start | bytes 294920 | tf_op jit(solution)/shard_map/ppermute | solution.py:341
  156.7 11.6 %collective-permute-start.19 = (bf16[2,192,128]{2,1,0:T(8,128)(2,1)}, bf16[2,192,128]{2,1,0:T(8,128)(2,1)}, u32[]{:S(2)}, u32[]{:S(2)}) collective-permute-start(bf16[2,192,128]{2,1,0:T(8,128)(2,1)} %fusion.8), channel_id=1, source_target_pairs={{0,16},{8,248},{16,32},{24,8},{32,48},{40,24},{48,64},{56,40},{64,... | collective-permute-start | bytes 294920 | tf_op jit(solution)/shard_map/ppermute | solution.py:341
  163.9 7.9 %collective-permute-start.11 = (bf16[2,192,128]{2,1,0:T(8,128)(2,1)S(1)}, bf16[2,192,128]{2,1,0:T(8,128)(2,1)S(1)}, u32[]{:S(2)}, u32[]{:S(2)}) collective-permute-start(bf16[2,192,128]{2,1,0:T(8,128)(2,1)S(1)} %fusion.14), channel_id=1, source_target_pairs={{0,16},{8,248},{16,32},{24,8},{32,48},{40,24},{48,64},{56,40},{64,... | collective-permute-start | bytes 294920 | tf_op jit(solution)/shard_map/ppermute | solution.py:341
  169.2 7.7 %collective-permute-start.20 = (bf16[2,192,128]{2,1,0:T(8,128)(2,1)S(1)}, bf16[2,192,128]{2,1,0:T(8,128)(2,1)S(1)}, u32[]{:S(2)}, u32[]{:S(2)}) collective-permute-start(bf16[2,192,128]{2,1,0:T(8,128)(2,1)S(1)} %fusion.7), channel_id=1, source_target_pairs={{0,16},{8,248},{16,32},{24,8},{32,48},{40,24},{48,64},{56,40},{64,... | collective-permute-start | bytes 294920 | tf_op jit(solution)/shard_map/ppermute | solution.py:341
  171.9 7.7 %collective-permute-start.12 = (bf16[2,192,128]{2,1,0:T(8,128)(2,1)S(1)}, bf16[2,192,128]{2,1,0:T(8,128)(2,1)S(1)}, u32[]{:S(2)}, u32[]{:S(2)}) collective-permute-start(bf16[2,192,128]{2,1,0:T(8,128)(2,1)S(1)} %fusion.13), channel_id=1, source_target_pairs={{0,16},{8,248},{16,32},{24,8},{32,48},{40,24},{48,64},{56,40},{64,... | collective-permute-start | bytes 294920 | tf_op jit(solution)/shard_map/ppermute | solution.py:341
  177.0 7.7 %collective-permute-start.21 = (bf16[2,192,128]{2,1,0:T(8,128)(2,1)S(1)}, bf16[2,192,128]{2,1,0:T(8,128)(2,1)S(1)}, u32[]{:S(2)}, u32[]{:S(2)}) collective-permute-start(bf16[2,192,128]{2,1,0:T(8,128)(2,1)S(1)} %fusion.6), channel_id=1, source_target_pairs={{0,16},{8,248},{16,32},{24,8},{32,48},{40,24},{48,64},{56,40},{64,... | collective-permute-start | bytes 294920 | tf_op jit(solution)/shard_map/ppermute | solution.py:341
  179.7 7.7 %collective-permute-start.13 = (bf16[2,192,128]{2,1,0:T(8,128)(2,1)S(1)}, bf16[2,192,128]{2,1,0:T(8,128)(2,1)S(1)}, u32[]{:S(2)}, u32[]{:S(2)}) collective-permute-start(bf16[2,192,128]{2,1,0:T(8,128)(2,1)S(1)} %fusion.12), channel_id=1, source_target_pairs={{0,16},{8,248},{16,32},{24,8},{32,48},{40,24},{48,64},{56,40},{64,... | collective-permute-start | bytes 294920 | tf_op jit(solution)/shard_map/ppermute | solution.py:341
  184.7 7.7 %collective-permute-start.22 = (bf16[2,192,128]{2,1,0:T(8,128)(2,1)S(1)}, bf16[2,192,128]{2,1,0:T(8,128)(2,1)S(1)}, u32[]{:S(2)}, u32[]{:S(2)}) collective-permute-start(bf16[2,192,128]{2,1,0:T(8,128)(2,1)S(1)} %fusion.5), channel_id=1, source_target_pairs={{0,16},{8,248},{16,32},{24,8},{32,48},{40,24},{48,64},{56,40},{64,... | collective-permute-start | bytes 294920 | tf_op jit(solution)/shard_map/ppermute | solution.py:341
  187.4 7.7 %collective-permute-start.14 = (bf16[2,192,128]{2,1,0:T(8,128)(2,1)S(1)}, bf16[2,192,128]{2,1,0:T(8,128)(2,1)S(1)}, u32[]{:S(2)}, u32[]{:S(2)}) collective-permute-start(bf16[2,192,128]{2,1,0:T(8,128)(2,1)S(1)} %fusion.11), channel_id=1, source_target_pairs={{0,16},{8,248},{16,32},{24,8},{32,48},{40,24},{48,64},{56,40},{64,... | collective-permute-start | bytes 294920 | tf_op jit(solution)/shard_map/ppermute | solution.py:341
  192.5 7.7 %collective-permute-start.23 = (bf16[2,192,128]{2,1,0:T(8,128)(2,1)S(1)}, bf16[2,192,128]{2,1,0:T(8,128)(2,1)S(1)}, u32[]{:S(2)}, u32[]{:S(2)}) collective-permute-start(bf16[2,192,128]{2,1,0:T(8,128)(2,1)S(1)} %fusion.4), channel_id=1, source_target_pairs={{0,16},{8,248},{16,32},{24,8},{32,48},{40,24},{48,64},{56,40},{64,... | collective-permute-start | bytes 294920 | tf_op jit(solution)/shard_map/ppermute | solution.py:341
  195.2 7.7 %collective-permute-start.15 = (bf16[2,192,128]{2,1,0:T(8,128)(2,1)S(1)}, bf16[2,192,128]{2,1,0:T(8,128)(2,1)S(1)}, u32[]{:S(2)}, u32[]{:S(2)}) collective-permute-start(bf16[2,192,128]{2,1,0:T(8,128)(2,1)S(1)} %fusion.10), channel_id=1, source_target_pairs={{0,16},{8,248},{16,32},{24,8},{32,48},{40,24},{48,64},{56,40},{64,... | collective-permute-start | bytes 294920 | tf_op jit(solution)/shard_map/ppermute | solution.py:341
  200.3 7.7 %collective-permute-start.24 = (bf16[2,192,128]{2,1,0:T(8,128)(2,1)S(1)}, bf16[2,192,128]{2,1,0:T(8,128)(2,1)S(1)}, u32[]{:S(2)}, u32[]{:S(2)}) collective-permute-start(bf16[2,192,128]{2,1,0:T(8,128)(2,1)S(1)} %fusion.3), channel_id=1, source_target_pairs={{0,16},{8,248},{16,32},{24,8},{32,48},{40,24},{48,64},{56,40},{64,... | collective-permute-start | bytes 294920 | tf_op jit(solution)/shard_map/ppermute | solution.py:341
  208.0 9.4 %collective-permute-start.25 = (bf16[320,128]{1,0:T(8,128)(2,1)S(1)}, bf16[320,128]{1,0:T(8,128)(2,1)S(1)}, u32[]{:S(2)}, u32[]{:S(2)}) collective-permute-start(bf16[320,128]{1,0:T(8,128)(2,1)S(1)} %fusion.19), channel_id=1, source_target_pairs={{0,8},{8,0},{16,24},{24,16},{32,40},{40,32},{48,56},{56,48},{64,72... | collective-permute-start | bytes 245768 | tf_op jit(solution)/shard_map/ppermute | solution.py:330
  210.0 8.2 %collective-permute-start.26 = (bf16[64,128]{1,0:T(8,128)(2,1)S(1)}, bf16[64,128]{1,0:T(8,128)(2,1)S(1)}, u32[]{:S(2)}, u32[]{:S(2)}) collective-permute-start(bf16[64,128]{1,0:T(8,128)(2,1)S(1)} %get-tuple-element.65), channel_id=1, source_target_pairs={{0,256},{8,264},{16,272},{24,280},{32,288},{40,296},{48,304},{56,3... | collective-permute-start | bytes 49160 | tf_op jit(solution)/shard_map/ppermute | solution.py:330
  (29 other events, 415.3 us)
Sparse Core Ops, SparseCore 0:
  16.9 76.5 all-gather.2

commit v3 on v2

v3 whole, which is shorter than its diff:
```python
import functools
import math

import jax
import jax.numpy as jnp
from jax import lax
from jax.experimental import pallas as pl
from jax.experimental.pallas import tpu as pltpu
from jax.sharding import PartitionSpec as P

HEAD = 128
RANK = 64
BLOCK = 128
QUAD = 4 * BLOCK

adapter_scale = 0.5
far_below = -1e30
to_two = math.log2(math.e) / math.sqrt(HEAD)
inverse = 1.0 / math.sqrt(HEAD)
f32 = jnp.float32
bf16 = jnp.bfloat16

KV = 2 * BLOCK
UPS = 64
GRAD = KV + 2 * UPS
SMALL = UPS + 16

STACK = 4 * BLOCK
GOUT_AT, LOW_AT, START_AT = STACK, 2 * STACK, 2 * STACK + BLOCK
SIDE = START_AT + 16
KEYS, VALUES = slice(0, BLOCK), slice(BLOCK, KV)


def last_last(a, b):
    return lax.dot_general(a, b, (((1,), (1,)), ((), ())), preferred_element_type=f32)


def first_first(a, b):
    return lax.dot_general(a, b, (((0,), (0,)), ((), ())), preferred_element_type=f32)


def plain(a, b):
    return lax.dot_general(a, b, (((1,), (0,)), ((), ())), preferred_element_type=f32)


def sum_low(lows, low_out):
    low = lows[0]
    for i in range(1, lows.shape[0]):
        low = low + lows[i]
    low_out[...] = low.astype(bf16)


def expert_at(meta, z_count, w, j):
    first = meta[3 + 2 * w + j] * 4
    return lax.rem(first, 2 * z_count) // 2, lax.div(first, 2 * z_count) ^ meta[0]


def query_base(meta, z_count, w):
    yh, z, core = meta[0], meta[1], meta[2]
    across = (1 - 2 * yh) * 2 * z_count * BLOCK
    return (2 * z + core) * BLOCK + w * across


def quad_range(meta, z_count, w, start):
    base = query_base(meta, z_count, w)
    first_key = jnp.min(start.astype(f32)).astype(jnp.int32)
    first = jnp.clip(first_key, 0, z_count * KV) // QUAD
    last = jnp.clip(base, -QUAD, z_count * KV - 1) // QUAD
    last = jnp.where(base < 0, -1, last)
    return first, last


def prepare(heads, z_count, meta, own, other, low_ref, pair, docs, side):
    core = meta[2]

    counts = jnp.zeros((16, 128), f32)
    for i in range(z_count):
        for slot in range(2):
            for ref in (own, other):
                counts += ref[slot, i, UPS:SMALL, :].astype(f32)
    high = jnp.floor(counts * (1.0 / 128.0))
    rest = (counts - 128.0 * high).astype(bf16)
    high = high.astype(bf16)
    lane = lax.broadcasted_iota(jnp.int32, (128, BLOCK), 0)

    for w in range(2):
        low = low_ref[w]
        side[w, LOW_AT:START_AT, :] = low
        for h in range(heads):
            columns = slice(h * HEAD, (h + 1) * HEAD)
            rows = []
            for j in range(2):
                z_at, slot = expert_at(meta, z_count, w, j)
                at = slice(16 * h, 16 * h + 16)
                for step in range(2):
                    mine, theirs = own[slot, z_at + step, at, :], other[slot, z_at + step, at, :]
                    rows.append(jnp.where(core == 0, mine, theirs))
                    rows.append(jnp.where(core == 0, theirs, mine))
            delta = plain(low, jnp.concatenate(rows, axis=0))
            side[w, h * BLOCK : (h + 1) * BLOCK, :] = (
                pair[w, 0:BLOCK, columns].astype(f32) + adapter_scale * delta
            ).astype(bf16)
            gout = pair[w, BLOCK : 2 * BLOCK, columns].astype(f32).T
            side[w, GOUT_AT + h * HEAD : GOUT_AT + (h + 1) * HEAD, :] = gout.astype(bf16)
        pick = jnp.where(lane == docs[w, 0:1, :], 1.0, 0.0).astype(bf16)
        whole = jnp.sum(plain(high, pick), axis=0, keepdims=True)
        part = jnp.sum(plain(rest, pick), axis=0, keepdims=True)
        side[w, START_AT:SIDE, :] = jnp.concatenate(
            [whole, part, jnp.zeros((14, BLOCK), f32)], axis=0
        ).astype(bf16)


def stage(own, side, own_out, side_out):
    own_out[...] = own[...]
    side_out[...] = side[...]


def start_of(meta, z_count, side, w):
    rows = side[w, START_AT:SIDE, :].astype(f32)
    start = 128.0 * rows[0:1] + rows[1:2]
    return start.astype(jnp.int32) - meta[0] * (z_count * KV)


def gout_of(heads, side, w):
    blocks = [side[w, GOUT_AT + h * HEAD : GOUT_AT + (h + 1) * HEAD, :] for h in range(heads)]
    return jnp.concatenate(blocks, axis=1).astype(f32)


def chip_pieces(core, own, other, quad):
    z_at = quad * 2
    return [
        (own, z_at, core),
        (other, z_at, 1 - core),
        (own, z_at + 1, 2 + core),
        (other, z_at + 1, 3 - core),
    ]


def rows_of(n):
    return slice(n * BLOCK, (n + 1) * BLOCK)


def forward(heads, z_count, meta, own, other, side, prob, out_ref, stats, score):
    wide = heads * BLOCK
    core = meta[2]
    ramp = lax.broadcasted_iota(jnp.int32, (BLOCK, wide), 0)

    for w in range(2):
        start = start_of(meta, z_count, side, w)
        whole_key = jnp.max(start.astype(f32)).astype(jnp.int32)
        first_quad, last_quad = quad_range(meta, z_count, w, start)
        start = jnp.concatenate([start] * heads, axis=1)
        place = query_base(meta, z_count, w) + lax.broadcasted_iota(jnp.int32, (1, BLOCK), 1)
        place = jnp.concatenate([place] * heads, axis=1)
        whole_key = jnp.clip(whole_key, 0, z_count * KV)
        whole_quad = jnp.minimum(
            jnp.maximum((whole_key + QUAD - 1) // QUAD, first_quad), last_quad
        )
        queries = side[w, 0:STACK, :]

        def scores(masked, quad, top):
            for n, (src, z_at, at) in enumerate(chip_pieces(core, own, other, quad)):
                s = last_last(src[z_at, KEYS, :], queries)
                if masked:
                    base = quad * QUAD + at * BLOCK
                    s = jnp.where((ramp >= start - base) & (ramp <= place - base), s, far_below)
                score[quad, rows_of(n), :] = s
                top = jnp.maximum(top, jnp.max(s.reshape(BLOCK // 8, 8, wide), axis=0))
            return top

        top = jnp.full((8, wide), far_below, f32)
        top = lax.fori_loop(
            first_quad,
            jnp.where(last_quad >= first_quad, whole_quad + 1, first_quad),
            lambda i, t: scores(True, jnp.where(i == whole_quad, last_quad, i), t),
            top,
        )
        top = lax.fori_loop(
            jnp.maximum(whole_quad, first_quad),
            last_quad,
            functools.partial(scores, False),
            top,
        )
        top = jnp.max(top, axis=0, keepdims=True)
        top = jnp.where(top < 0.5 * far_below, 0.0, top)

        def attend(quad, carry):
            total, out = carry
            values = []
            for n, (src, z_at, _) in enumerate(chip_pieces(core, own, other, quad)):
                p = jnp.exp2((score[quad, rows_of(n), :] - top) * to_two)
                total = total + jnp.sum(p.reshape(BLOCK // 8, 8, wide), axis=0)
                prob[w, quad, rows_of(n), :] = p.astype(bf16)
                values.append(src[z_at, VALUES, :])
            out = out + first_first(jnp.concatenate(values, axis=0), prob[w, quad])
            return total, out

        total, out = lax.fori_loop(
            first_quad,
            last_quad + 1,
            attend,
            (jnp.zeros((8, wide), f32), jnp.zeros((HEAD, wide), f32)),
        )
        total = jnp.sum(total, axis=0, keepdims=True)
        some = total > 0.0
        safe = jnp.where(some, total, 1.0)
        out = out * (1.0 / safe)
        out_ref[w] = out
        row_delta = jnp.sum(gout_of(heads, side, w) * out, axis=0, keepdims=True)
        log_top = top * to_two
        log_sum = jnp.where(some, log_top + jnp.log2(safe), far_below)
        filled = jnp.where(some, 1.0, 0.0)
        stats[w] = jnp.concatenate(
            [log_sum, row_delta, log_top, filled, jnp.zeros((4, wide), f32)], axis=0
        )


def shares(log_sum, far_log, crossed):
    far_log = jnp.where(crossed, far_log, far_below)
    most = jnp.maximum(log_sum, far_log)
    log_all = most + jnp.log2(jnp.exp2(log_sum - most) + jnp.exp2(far_log - most))
    far = jnp.where(crossed, jnp.exp2(far_log - log_all), 0.0)
    return log_all, jnp.exp2(log_sum - log_all), far


def backward(
    heads,
    z_count,
    meta,
    own,
    other,
    side,
    prob,
    stats,
    come,
    dquery,
    dquery_across,
    send_own,
    send_other,
    sum_own,
    sum_other,
    gscaled,
):
    wide = heads * BLOCK
    yh, core = meta[0], meta[2]
    sum_own[...] = jnp.zeros(sum_own.shape, f32)
    sum_other[...] = jnp.zeros(sum_other.shape, f32)

    for w in range(2):
        log_sum, row_delta, log_top, filled = (stats[w, i : i + 1, :] for i in range(4))
        log_all, near, far = shares(log_sum, come[0:1, :], (1 - yh) == w)
        scale = jnp.where(filled > 0.0, jnp.exp2(log_top - log_all), 0.0)
        delta = (row_delta * near + come[1:2, :] * far) * scale
        gout = gout_of(heads, side, w) * scale
        for h in range(heads):
            columns = slice(h * HEAD, (h + 1) * HEAD)
            gscaled[h * BLOCK : (h + 1) * BLOCK, :] = gout[:, columns].T.astype(bf16)
        grads = gscaled[...]
        queries = side[w, 0:STACK, :]
        first_quad, last_quad = quad_range(
            meta, z_count, w, start_of(meta, z_count, side, w)
        )

        def step(quad, dq):
            keys, dscores = [], []
            places = chip_pieces(core, (own, sum_own), (other, sum_other), quad)
            for n, ((src, dst), z_at, _) in enumerate(places):
                p = prob[w, quad, rows_of(n), :]
                dp = last_last(src[z_at, VALUES, :], grads)
                ds = (p.astype(f32) * (dp - delta)).astype(bf16)
                dst[z_at, KEYS, :] += plain(ds, queries)
                dst[z_at, VALUES, :] += plain(p, grads)
                keys.append(src[z_at, KEYS, :])
                dscores.append(ds)
            return dq + first_first(
                jnp.concatenate(keys, axis=0), jnp.concatenate(dscores, axis=0)
            )

        dq = lax.fori_loop(first_quad, last_quad + 1, step, jnp.zeros((HEAD, wide), f32))
        dq = dq * inverse
        low = side[w, LOW_AT:START_AT, :]
        for h in range(heads):
            columns = slice(h * HEAD, (h + 1) * HEAD)
            dq_h = dq[:, columns].T
            dq_low = dq_h.astype(bf16)
            if w == 0:
                dquery[:, columns] = dq_h
            else:
                dquery_across[:, columns] = dq_low
            up = adapter_scale * first_first(low, dq_low)
            for j in range(2):
                z_at, slot = expert_at(meta, z_count, w, j)
                at = pl.ds(pl.multiple_of(KV + slot * UPS + 16 * h, 16), 16)
                for i in range(2):
                    row = j * RANK + 32 * i
                    even, odd = up[row : row + 16, :], up[row + 16 : row + 32, :]
                    sum_own[z_at + i, at, :] += jnp.where(core == 0, even, odd)
                    sum_other[z_at + i, at, :] += jnp.where(core == 0, odd, even)

    for src, dst in ((sum_own, send_own), (sum_other, send_other)):
        dst[:, KEYS, :] = (src[:, KEYS, :] * inverse).astype(bf16)
        dst[:, BLOCK:GRAD, :] = src[:, BLOCK:GRAD, :].astype(bf16)


def finish(heads, meta, out_t, stats, come, far_out, far_dquery, dquery, attended, dquery_out):
    _, near, far = shares(stats[0, 0:1, :], come[0:1, :], meta[0] == 1)
    out = out_t[0] * near + far_out[...].astype(f32) * far
    for h in range(heads):
        columns = slice(h * HEAD, (h + 1) * HEAD)
        attended[:, columns] = out[:, columns].T
    dquery_out[...] = dquery[...] + far_dquery[...].astype(f32)


def swap(array, distance):
    count = lax.axis_size("ctx")
    return lax.ppermute(array, "ctx", [(i, i ^ distance) for i in range(count)])


def shards(
    normed,
    frozen_query,
    input_keys,
    input_values,
    document_index,
    routes,
    adapter_down_weight,
    adapter_up_weight,
    output_gradient,
):
    z_count = lax.axis_size("ctx") // 4
    across = 2 * z_count
    exp_count = lax.axis_size("exp")
    place = lax.axis_index("ctx")
    runs = [
        [(yh * z_count + z) * 2 + core for z in range(z_count)]
        for yh in range(2)
        for core in range(2)
    ]
    rows = normed.shape[0]
    wide = frozen_query.shape[1]
    heads = wide // HEAD
    stack = heads * rows
    up_rows = adapter_up_weight.shape[0]
    vmem = pl.BlockSpec(memory_space=pltpu.VMEM)
    smem = pl.BlockSpec(memory_space=pltpu.SMEM)

    kv = jnp.concatenate([input_keys, input_values], axis=0)
    own = lax.all_gather(kv, "ctx", axis=0, tiled=False, axis_index_groups=runs)

    ups = adapter_up_weight.reshape(up_rows, heads, HEAD).transpose(1, 0, 2)
    ups = ups.reshape(up_rows * heads, HEAD)
    lower = document_index[:, None] < jnp.arange(128, dtype=jnp.int32)[None, :]
    counts = jnp.sum(lower.astype(f32), axis=0, keepdims=True).astype(bf16)
    small = jnp.concatenate([ups, jnp.pad(counts, ((0, 15), (0, 0)))], axis=0)
    small, _ = lax.optimization_barrier((small, kv))
    small = lax.all_gather(small, "ctx", axis=0, tiled=False, axis_index_groups=runs)
    small = jnp.stack([small, swap(small, across)])
    small_other = swap(small, 1)

    chosen = [
        lax.dynamic_index_in_dim(adapter_down_weight, routes[0, j], 0, keepdims=False)
        for j in range(2)
    ]
    partial = jnp.dot(normed, jnp.concatenate(chosen, axis=1), preferred_element_type=f32)
    lows = lax.all_to_all(
        jnp.broadcast_to(partial[None], (exp_count,) + partial.shape), "exp", 0, 0
    )
    low = pl.pallas_call(
        sum_low,
        out_shape=jax.ShapeDtypeStruct(partial.shape, bf16),
        in_specs=[vmem],
        out_specs=vmem,
    )(lows)
    low = jnp.stack([low, swap(low, across)])
    local = jnp.concatenate([frozen_query, output_gradient], axis=0)
    local, _ = lax.optimization_barrier((local, kv))
    pair = jnp.stack([local, swap(local, across)])
    ints = jnp.concatenate(
        [document_index.reshape(1, rows), jnp.pad(routes, ((0, 7 - 1), (0, rows - 2)))], axis=0
    )
    ints, _ = lax.optimization_barrier((ints, kv))
    ints = jnp.stack([ints, swap(ints, across)])
    meta = jnp.stack(
        [
            place // across,
            place // 2 % z_count,
            place % 2,
            ints[0, 1, 0],
            ints[0, 1, 1],
            ints[1, 1, 0],
            ints[1, 1, 1],
        ]
    ).astype(jnp.int32)
    side = pl.pallas_call(
        functools.partial(prepare, heads, z_count),
        out_shape=jax.ShapeDtypeStruct((2, SIDE, HEAD), bf16),
        in_specs=[smem] + [vmem] * 5,
        out_specs=vmem,
    )(meta, small, small_other, low, pair, ints)
    own, side = lax.optimization_barrier((own, side))
    other = swap(own, 1)
    own, side = pl.pallas_call(
        stage,
        out_shape=(
            jax.ShapeDtypeStruct(own.shape, bf16),
            jax.ShapeDtypeStruct(side.shape, bf16),
        ),
        in_specs=[vmem] * 2,
        out_specs=(vmem,) * 2,
    )(own, side)

    quads = z_count // 2
    prob, out, stats = pl.pallas_call(
        functools.partial(forward, heads, z_count),
        out_shape=(
            jax.ShapeDtypeStruct((2, quads, QUAD, stack), bf16),
            jax.ShapeDtypeStruct((2, HEAD, stack), f32),
            jax.ShapeDtypeStruct((2, 8, stack), f32),
        ),
        in_specs=[smem] + [vmem] * 3,
        out_specs=(vmem,) * 3,
        scratch_shapes=[pltpu.VMEM((quads, QUAD, stack), f32)],
        compiler_params=pltpu.CompilerParams(vmem_limit_bytes=30 * 1024 * 1024),
    )(meta, own, other, side)
    come = swap(jnp.where(place < across, stats[1], stats[0]), across)

    send = jax.ShapeDtypeStruct((z_count, GRAD, HEAD), bf16)
    dquery, dquery_across, send_own, send_other = pl.pallas_call(
        functools.partial(backward, heads, z_count),
        out_shape=(
            jax.ShapeDtypeStruct((rows, wide), f32),
            jax.ShapeDtypeStruct((rows, wide), bf16),
            send,
            send,
        ),
        in_specs=[smem] + [vmem] * 6,
        out_specs=(vmem,) * 4,
        scratch_shapes=[
            pltpu.VMEM((z_count, GRAD, HEAD), f32),
            pltpu.VMEM((z_count, GRAD, HEAD), f32),
            pltpu.VMEM((stack, HEAD), bf16),
        ],
        compiler_params=pltpu.CompilerParams(vmem_limit_bytes=30 * 1024 * 1024),
    )(meta, own, other, side, prob, stats, come)

    chip = send_own + swap(send_other, 1)
    part = lax.psum_scatter(
        chip, "ctx", scatter_dimension=0, tiled=False, axis_index_groups=runs
    )

    far_out = jnp.where(place < across, out[1], out[0]).astype(bf16)
    far, _ = lax.optimization_barrier((jnp.stack([far_out, dquery_across.reshape(HEAD, stack)]), chip))
    far = swap(far, across)
    attended, dquery = pl.pallas_call(
        functools.partial(finish, heads),
        out_shape=(jax.ShapeDtypeStruct((rows, wide), f32),) * 2,
        in_specs=[smem] + [vmem] * 6,
        out_specs=(vmem,) * 2,
    )(meta, out, stats, come, far[0], far[1].reshape(rows, wide), dquery)

    up_grad = part[KV : KV + UPS].astype(f32) + swap(part[KV + UPS :], across).astype(f32)
    up_grad = up_grad.reshape(heads, up_rows, HEAD).transpose(1, 0, 2)
    return (
        attended,
        dquery,
        part[KEYS].astype(f32),
        part[VALUES].astype(f32),
        up_grad.reshape(up_rows, wide),
    )


def solution(mesh):
    both = P("ctx", "exp")
    return jax.shard_map(
        shards,
        mesh=mesh,
        in_specs=(
            both,
            both,
            both,
            both,
            P("ctx"),
            P("ctx", None),
            P(None, "exp", None),
            both,
            both,
        ),
        out_specs=(both,) * 5,
        check_vma=False,
    )
```

time: 232 us -> 215 us (0.927)
  starting transfers between devices: 93.4 us -> 34.3 us
  blocking collectives: 0 us -> 37.9 us
  waiting for transfers between devices: 67.8 us -> 78.7 us
  Pallas kernels: 25.1 us -> 19.1 us
    reduce_scatter x0 -> x1, waiting for transfers between devices: none -> 55 us  [shards(): lax.psum_scatter(chip, 'ctx', scatter_dimension=0, tiled=False, axis_inde...]
    ppermute x16 -> x0, starting transfers between devices: 50.3 us -> none  [pass_on(): return lax.ppermute(array, 'ctx', route)]
    all_gather x0 -> x1, blocking collectives: none -> 37.9 us  [shards(): lax.all_gather(small, 'ctx', axis=0, tiled=False, axis_index_groups=runs)]
    all_gather x1, waiting for transfers between devices: 37.3 us -> 0.01 us  [shards(): own = lax.all_gather(kv, 'ctx', axis=0, tiled=False, axis_index_groups=runs)]
    ppermute x16 -> x0, waiting for transfers between devices: 14.5 us -> none  [pass_on(): return lax.ppermute(array, 'ctx', route)]
    ppermute x12 -> x10, waiting for transfers between devices: 15.9 us -> 23.6 us  [swap(): return lax.ppermute(array, 'ctx', [(i, i ^ distance) for i in range(count)])]
    pallas_call x1, Pallas kernels: 11.8 us -> 6.37 us  [shards(): pl.pallas_call(functools.partial(backward, heads, z_count), out_shape=(ja...]
    ppermute x12 -> x10, starting transfers between devices: 33.8 us -> 28.9 us  [swap(): return lax.ppermute(array, 'ctx', [(i, i ^ distance) for i in range(count)])]
  transfers between devices with their start and end apart: 30 -> 13, of which waited for: 14 -> 7; matrix products, arithmetic and copies ran while one was open for 7% -> 7% of each run, Pallas kernels for 3% -> 4%
where the time goes in v3:
time: 215 us; the launch traced here: 214 us
  waiting for transfers between devices  78.7 us (37%)
  blocking collectives  37.9 us (18%)
  starting transfers between devices  34.3 us (16%)
  Pallas kernels  19.1 us (9%)
  between operations  18.2 us (8%)
  local copies, waits for them, and re-layouts  17.2 us (8%)
  other arithmetic  8.18 us (4%)
    reduce_scatter x1, waiting for transfers between devices, shards(): lax.psum_scatter(chip, 'ctx', scatter_dimension=0, tiled=False, axis_inde...  55 us
    all_gather x1, blocking collectives, shards(): lax.all_gather(small, 'ctx', axis=0, tiled=False, axis_index_groups=runs)  37.9 us
    ppermute x10, starting transfers between devices, swap(): return lax.ppermute(array, 'ctx', [(i, i ^ distance) for i in range(count)])  28.9 us
    ppermute x10, waiting for transfers between devices, swap(): return lax.ppermute(array, 'ctx', [(i, i ^ distance) for i in range(count)])  23.6 us
    pallas_call x1, Pallas kernels, shards(): pl.pallas_call(functools.partial(backward, heads, z_count), out_shape=(ja...  6.37 us
    unnamed x29, local copies, waits for them, and re-layouts  6.1 us
    all_to_all x1, starting transfers between devices, shards(): lax.all_to_all(jnp.broadcast_to(partial[None], (exp_count,) + partial.sha...  5.35 us
  transfers between devices with their start and end apart: 13, of which 7 were waited for; matrix products, arithmetic and copies ran while one was open for 7% of the time, Pallas kernels for 4%

profile of v3, /device:TPU:6, one launch (start us, length us, event | category | flops | bytes accessed | tf_op | source)
XLA Modules:
  0.0 213.8 jit_solution(17284859387854814265)
XLA Ops:
  10.1 5.1 %collective-permute-start = (s32[8,128]{1,0:T(8,128)S(1)}, s32[8,128]{1,0:T(8,128)S(1)}, u32[]{:S(2)}, u32[]{:S(2)}) collective-permute-start(s32[8,128]{1,0:T(8,128)S(1)} %pad_add_fusion.1), channel_id=1, source_target_pairs={{0,256},{8,264},{16,272},{24,280},{32,288},{40,296},{48,304},{56,3... | collective-permute-start | bytes 12296 | tf_op jit(solution)/shard_map/ppermute | solution.py:316
  16.7 37.9 %all-gather.1 = bf16[1280,128]{1,0:T(8,128)(2,1)S(1)} all-gather(bf16[80,128]{1,0:T(8,128)(2,1)S(1)} %fusion.6), channel_id=3, replica_groups={{0,16,32,48,64,80,96,112,128,144,160,176,192,208,224,240},{8,24,40,56,7..., dimensions={0}, use_global_device_ids=true | all-gather | bytes 348160 | tf_op jit(solution)/shard_map/all_gather | solution.py:356
  54.6 2.1 collective-permute-start.1
  64.1 5.4 %all-to-all-start = ((f32[8,128,128]{2,1,0:T(8,128)}), f32[8,128,128]{2,1,0:T(8,128)S(1)}, u32[]{:S(2)}, u32[]{:S(2)}) async-start(f32[8,128,128]{2,1,0:T(8,128)} %broadcast_in_dim.2), calls=%async_computation | async-start | bytes 1048576 | tf_op jit(solution)/shard_map/all_to_all | solution.py:365
  69.5 1.9 collective-permute-start.2
  71.5 4.8 %collective-permute-start.4 = (bf16[256,512]{1,0:T(8,128)(2,1)S(1)}, bf16[256,512]{1,0:T(8,128)(2,1)S(1)}, u32[]{:S(2)}, u32[]{:S(2)}) collective-permute-start(bf16[256,512]{1,0:T(8,128)(2,1)S(1)} %pad_maximum_fusion.2), channel_id=1, source_target_pairs={{0,256},{8,264},{16,272},{24,280},{32,288},{40,296},{48,304},{56,3... | collective-permute-start | bytes 786440 | tf_op jit(solution)/shard_map/ppermute | solution.py:316
  77.5 3.1 %stack.60.meta = s32[7]{0:T(128)} concatenate(s32[1]{0:T(128)} %bitcast, s32[1]{0:T(128)} %bitcast.1, s32[1]{0:T(128)} %bitcast.2, s32[1]{0:T(128)} %bitcast.5, s32[1]{0:T(128)} %bitcast.6, s32[1]{0:T(128)} %bitcast.8, s32[1]{0:T(128)} %bitcast.9), dimensions={0} | concatenate | bytes 56 | tf_op jit(solution)/shard_map/stack | solution.py:383
  82.1 1.7 shard_map.128
  83.7 2.5 %collective-permute-start.3 = (bf16[128,128]{1,0:T(8,128)(2,1)}, bf16[128,128]{1,0:T(8,128)(2,1)S(1)}, u32[]{:S(2)}, u32[]{:S(2)}) collective-permute-start(bf16[128,128]{1,0:T(8,128)(2,1)} %shard_map.128), channel_id=1, source_target_pairs={{0,256},{8,264},{16,272},{24,280},{32,288},{40,296},{48,304},{56,3... | collective-permute-start | bytes 98312 | tf_op jit(solution)/shard_map/ppermute | solution.py:316
  87.1 4.1 %collective-permute-done.3 = bf16[128,128]{1,0:T(8,128)(2,1)S(1)} collective-permute-done((bf16[128,128]{1,0:T(8,128)(2,1)}, bf16[128,128]{1,0:T(8,128)(2,1)S(1)}, u32[]{:S(2)}, u32[]{:S(2)}) %collective-permute-start.3) | collective-permute-done | bytes 32800 | tf_op jit(solution)/shard_map/ppermute | solution.py:316
  93.5 2.6 %shard_map.129.side = bf16[2,1168,128]{2,1,0:T(8,128)(2,1)} custom-call(s32[7]{0:T(128)} %stack.60.meta, bf16[2,16,80,128]{3,2,1,0:T(8,128)(2,1)} %copy-done.8, bf16[2,16,80,128]{3,2,1,0:T(8,128)(2,1)} %copy-done.10, bf16[2,128,128]{2,1,0:T(8,128)(2,1)} %pad_maximum_fusion.4.low_ref, bf16[2,256,512]{2,1,0:T(8,128)(2,1)} %pad_maximum_fusion.1.pair, ...), custom_call_target="tpu_custom_call" | custom-call | tf_op jit(solution)/shard_map/pallas_call | solution.py:394
  96.1 1.9 collective-permute-start.5
  98.0 2.6 %shard_map.130 = (bf16[16,256,128]{2,1,0:T(8,128)(2,1)}, bf16[2,1168,128]{2,1,0:T(8,128)(2,1)}) custom-call(bf16[16,256,128]{2,1,0:T(8,128)(2,1)} %bitcast.67, bf16[2,1168,128]{2,1,0:T(8,128)(2,1)} %shard_map.129.side), custom_call_target="tpu_custom_call" | custom-call | tf_op jit(solution)/shard_map/pallas_call | solution.py:402
  103.2 3.7 %shard_map.131 = (bf16[2,8,512,512]{3,2,1,0:T(8,128)(2,1)S(1)}, f32[2,128,512]{2,1,0:T(8,128)S(1)}, f32[2,8,512]{2,1,0:T(8,128)S(1)}) custom-call(s32[7]{0:T(128)S(1)} %copy-done.7, bf16[16,256,128]{2,1,0:T(8,128)(2,1)S(1)} %copy-done.1, bf16[16,256,128]{2,1,0:T(8,128)(2,1)S(1)} %collective-permute-done.5.other, bf16[2,1168,128]{2,1,0:T(8,128)(2,1)S(1)} %copy-done.2), custom_call_target="tpu_custom_call" | custom-call | tf_op jit(solution)/shard_map/pallas_call | solution.py:413
  106.9 1.9 collective-permute-start.6
  108.8 5.2 %collective-permute-done.6.come = f32[8,512]{1,0:T(8,128)S(1)} collective-permute-done((f32[8,512]{1,0:T(8,128)S(1)}, f32[8,512]{1,0:T(8,128)S(1)}, u32[]{:S(2)}, u32[]{:S(2)}) %collective-permute-start.6) | collective-permute-done | bytes 16416 | tf_op jit(solution)/shard_map/ppermute | solution.py:316
  114.0 6.4 %shard_map.132 = (f32[128,512]{1,0:T(8,128)S(1)}, bf16[128,512]{1,0:T(8,128)(2,1)S(1)}, bf16[16,384,128]{2,1,0:T(8,128)(2,1)S(1)}, bf16[16,384,128]{2,1,0:T(8,128)(2,1)S(1)}) custom-call(s32[7]{0:T(128)S(1)} %copy-done.7, bf16[16,256,128]{2,1,0:T(8,128)(2,1)S(1)} %copy-done.1, bf16[16,256,128]{2,1,0:T(8,128)(2,1)S(1)} %collective-permute-done.5.other, ...), custom_call_target="tpu_custom_call" | custom-call | tf_op jit(solution)/shard_map/pallas_call | solution.py:428
  121.1 1.9 collective-permute-start.7
  123.0 3.4 %collective-permute-done.7 = bf16[16,384,128]{2,1,0:T(8,128)(2,1)S(1)} collective-permute-done((bf16[16,384,128]{2,1,0:T(8,128)(2,1)S(1)}, bf16[16,384,128]{2,1,0:T(8,128)(2,1)S(1)}, u32[]{:S(2)}, u32[]{:S(2)}) %collective-permute-start.7) | collective-permute-done | bytes 1572896 | tf_op jit(solution)/shard_map/ppermute | solution.py:316
  128.1 1.9 collective-permute-start.8
  130.0 9.8 %collective-permute-done.8 = bf16[2,128,512]{2,1,0:T(8,128)(2,1)S(1)} collective-permute-done((bf16[2,128,512]{2,1,0:T(8,128)(2,1)S(1)}, bf16[2,128,512]{2,1,0:T(8,128)(2,1)S(1)}, u32[]{:S(2)}, u32[]{:S(2)}) %collective-permute-start.8) | collective-permute-done | bytes 262176 | tf_op jit(solution)/shard_map/ppermute | solution.py:316
  140.6 2.2 %shard_map.133 = (f32[128,512]{1,0:T(8,128)}, f32[128,512]{1,0:T(8,128)}) custom-call(s32[7]{0:T(128)} %stack.60.meta, f32[2,128,512]{2,1,0:T(8,128)} %copy-done.3, f32[2,8,512]{2,1,0:T(8,128)} %copy-done.4, f32[8,512]{1,0:T(8,128)} %copy-done.6, bf16[128,512]{1,0:T(8,128)(2,1)} %get-tuple-element.42.far_out, bf16[128,512]{1,0:T(8,128)(2,1)} %get-tuple-element.41.far_dquery, ...), custom_call_target="tpu_custom_call" | custom-call | tf_op jit(solution)/shard_map/pallas_call | solution.py:454
  142.8 55.0 %reduce-scatter.2.cloned.1.call-done = bf16[1,384,128]{2,1,0:T(8,128)(2,1)} async-done(((bf16[16,384,128]{2,1,0:T(8,128)(2,1)}), bf16[1,384,128]{2,1,0:T(8,128)(2,1)}) %reduce-scatter.2.cloned.1.call-update) | async-done | bytes 98320 | tf_op jit(solution)/shard_map/reduce_scatter | solution.py:447
  198.5 4.8 %collective-permute-start.9 = (bf16[64,128]{1,0:T(8,128)(2,1)S(1)}, bf16[64,128]{1,0:T(8,128)(2,1)S(1)}, u32[]{:S(2)}, u32[]{:S(2)}) collective-permute-start(bf16[64,128]{1,0:T(8,128)(2,1)S(1)} %slice_bitcast_fusion.4), channel_id=1, source_target_pairs={{0,256},{8,264},{16,272},{24,280},{32,288},{40,296},{48,304},{56,3... | collective-permute-start | bytes 49160 | tf_op jit(solution)/shard_map/ppermute | solution.py:316
  (68 shorter events, 23.7 us)
Async XLA Ops:
  7.2 55.7 %copy-start = (bf16[128,1024]{1,0:T(8,128)(2,1)S(1)}, bf16[128,1024]{1,0:T(8,128)(2,1)}, u32[]{:S(2)}) copy-start(bf16[128,1024]{1,0:T(8,128)(2,1)} %param.9) | copy-start | bytes 786436
  7.2 88.9 %all-gather.4.cloned.1.call-start = ((), (), s32[]{:S(2)}) async-start(), calls=%async_computation.3 | async-start | bytes 1114112 | tf_op jit(solution)/shard_map/all_gather | solution.py:348
  10.1 66.8 %collective-permute-start = (s32[8,128]{1,0:T(8,128)S(1)}, s32[8,128]{1,0:T(8,128)S(1)}, u32[]{:S(2)}, u32[]{:S(2)}) collective-permute-start(s32[8,128]{1,0:T(8,128)S(1)} %pad_add_fusion.1), channel_id=1, source_target_pairs={{0,256},{8,264},{16,272},{24,280},{32,288},{40,296},{48,304},{56,3... | collective-permute-start | bytes 12296 | tf_op jit(solution)/shard_map/ppermute | solution.py:316
  54.6 14.9 %collective-permute-start.1 = (bf16[16,80,128]{2,1,0:T(8,128)(2,1)S(1)}, bf16[16,80,128]{2,1,0:T(8,128)(2,1)S(1)}, u32[]{:S(2)}, u32[]{:S(2)}) collective-permute-start(bf16[16,80,128]{2,1,0:T(8,128)(2,1)S(1)} %bitcast.64), channel_id=1, source_target_pairs={{0,256},{8,264},{16,272},{24,280},{32,288},{40,296},{48,304},{56,3... | collective-permute-start | bytes 983048 | tf_op jit(solution)/shard_map/ppermute | solution.py:316
  63.1 8.3 %copy-start.12 = (bf16[128,512]{1,0:T(8,128)(2,1)S(1)}, bf16[128,512]{1,0:T(8,128)(2,1)}, u32[]{:S(2)}) copy-start(bf16[128,512]{1,0:T(8,128)(2,1)} %param.17) | copy-start | bytes 393220
  63.2 8.3 %copy-start.13 = (bf16[128,512]{1,0:T(8,128)(2,1)S(1)}, bf16[128,512]{1,0:T(8,128)(2,1)}, u32[]{:S(2)}) copy-start(bf16[128,512]{1,0:T(8,128)(2,1)} %param.10) | copy-start | bytes 393220
  64.1 17.2 %all-to-all-start = ((f32[8,128,128]{2,1,0:T(8,128)}), f32[8,128,128]{2,1,0:T(8,128)S(1)}, u32[]{:S(2)}, u32[]{:S(2)}) async-start(f32[8,128,128]{2,1,0:T(8,128)} %broadcast_in_dim.2), calls=%async_computation | async-start | bytes 1048576 | tf_op jit(solution)/shard_map/all_to_all | solution.py:365
  69.5 128.3 %reduce-scatter.2.cloned.1.call-start = ((), (), s32[]{:S(2)}) async-start(), calls=%async_computation.2 | async-start | bytes 1671168 | tf_op jit(solution)/shard_map/reduce_scatter | solution.py:447
  69.5 23.1 %copy-start.8 = (bf16[2,16,80,128]{3,2,1,0:T(8,128)(2,1)}, bf16[2,16,80,128]{3,2,1,0:T(8,128)(2,1)S(1)}, u32[]{:S(2)}) copy-start(bf16[2,16,80,128]{3,2,1,0:T(8,128)(2,1)S(1)} %pad_maximum_fusion.own) | copy-start | bytes 1966084
  69.5 23.1 %collective-permute-start.2 = (bf16[2,16,80,128]{3,2,1,0:T(8,128)(2,1)S(1)}, bf16[2,16,80,128]{3,2,1,0:T(8,128)(2,1)S(1)}, u32[]{:S(2)}, u32[]{:S(2)}) collective-permute-start(bf16[2,16,80,128]{3,2,1,0:T(8,128)(2,1)S(1)} %pad_maximum_fusion.own), channel_id=1, source_target_pairs={{0,8},{8,0},{16,24},{24,16},{32,40},{40,32},{48,56},{56,48},{64,72... | collective-permute-start | bytes 1966088 | tf_op jit(solution)/shard_map/ppermute | solution.py:316
  71.5 14.8 %collective-permute-start.4 = (bf16[256,512]{1,0:T(8,128)(2,1)S(1)}, bf16[256,512]{1,0:T(8,128)(2,1)S(1)}, u32[]{:S(2)}, u32[]{:S(2)}) collective-permute-start(bf16[256,512]{1,0:T(8,128)(2,1)S(1)} %pad_maximum_fusion.2), channel_id=1, source_target_pairs={{0,256},{8,264},{16,272},{24,280},{32,288},{40,296},{48,304},{56,3... | collective-permute-start | bytes 786440 | tf_op jit(solution)/shard_map/ppermute | solution.py:316
  83.7 7.5 %collective-permute-start.3 = (bf16[128,128]{1,0:T(8,128)(2,1)}, bf16[128,128]{1,0:T(8,128)(2,1)S(1)}, u32[]{:S(2)}, u32[]{:S(2)}) collective-permute-start(bf16[128,128]{1,0:T(8,128)(2,1)} %shard_map.128), channel_id=1, source_target_pairs={{0,256},{8,264},{16,272},{24,280},{32,288},{40,296},{48,304},{56,3... | collective-permute-start | bytes 98312 | tf_op jit(solution)/shard_map/ppermute | solution.py:316
  92.7 8.2 %copy-start.7 = (s32[7]{0:T(128)S(1)}, s32[7]{0:T(128)}, u32[]{:S(2)}) copy-start(s32[7]{0:T(128)} %stack.60.meta) | copy-start | bytes 88
  92.7 0.9 copy-start.10
  96.1 4.8 %collective-permute-start.5 = (bf16[16,256,128]{2,1,0:T(8,128)(2,1)}, bf16[16,256,128]{2,1,0:T(8,128)(2,1)S(1)}, u32[]{:S(2)}, u32[]{:S(2)}) collective-permute-start(bf16[16,256,128]{2,1,0:T(8,128)(2,1)} %bitcast.66), channel_id=1, source_target_pairs={{0,8},{8,0},{16,24},{24,16},{32,40},{40,32},{48,56},{56,48},{64,72... | collective-permute-start | bytes 3145736 | tf_op jit(solution)/shard_map/ppermute | solution.py:316
  100.9 1.2 copy-start.1
  102.1 1.1 copy-start.2
  106.8 13.6 %copy-start.4 = (f32[2,8,512]{2,1,0:T(8,128)}, f32[2,8,512]{2,1,0:T(8,128)S(1)}, u32[]{:S(2)}) copy-start(f32[2,8,512]{2,1,0:T(8,128)S(1)} %get-tuple-element.30.stats) | copy-start | bytes 98308
  106.9 21.2 %copy-start.3 = (f32[2,128,512]{2,1,0:T(8,128)}, f32[2,128,512]{2,1,0:T(8,128)S(1)}, u32[]{:S(2)}) copy-start(f32[2,128,512]{2,1,0:T(8,128)S(1)} %get-tuple-element.29.out_t) | copy-start | bytes 1572868
  106.9 7.1 %collective-permute-start.6 = (f32[8,512]{1,0:T(8,128)S(1)}, f32[8,512]{1,0:T(8,128)S(1)}, u32[]{:S(2)}, u32[]{:S(2)}) collective-permute-start(f32[8,512]{1,0:T(8,128)S(1)} %select_bitcast_fusion), channel_id=1, source_target_pairs={{0,256},{8,264},{16,272},{24,280},{32,288},{40,296},{48,304},{56,3... | collective-permute-start | bytes 49160 | tf_op jit(solution)/shard_map/ppermute | solution.py:316
  114.0 6.4 %copy-start.6 = (f32[8,512]{1,0:T(8,128)}, f32[8,512]{1,0:T(8,128)S(1)}, u32[]{:S(2)}) copy-start(f32[8,512]{1,0:T(8,128)S(1)} %collective-permute-done.6.come) | copy-start | bytes 49156
  121.1 5.3 %collective-permute-start.7 = (bf16[16,384,128]{2,1,0:T(8,128)(2,1)S(1)}, bf16[16,384,128]{2,1,0:T(8,128)(2,1)S(1)}, u32[]{:S(2)}, u32[]{:S(2)}) collective-permute-start(bf16[16,384,128]{2,1,0:T(8,128)(2,1)S(1)} %get-tuple-element.34), channel_id=1, source_target_pairs={{0,8},{8,0},{16,24},{24,16},{32,40},{40,32},{48,56},{56,48},{64,72... | collective-permute-start | bytes 4718600 | tf_op jit(solution)/shard_map/ppermute | solution.py:316
  128.1 11.7 %collective-permute-start.8 = (bf16[2,128,512]{2,1,0:T(8,128)(2,1)S(1)}, bf16[2,128,512]{2,1,0:T(8,128)(2,1)S(1)}, u32[]{:S(2)}, u32[]{:S(2)}) collective-permute-start(bf16[2,128,512]{2,1,0:T(8,128)(2,1)S(1)} %pad_maximum_fusion.3), channel_id=1, source_target_pairs={{0,256},{8,264},{16,272},{24,280},{32,288},{40,296},{48,304},{56,3... | collective-permute-start | bytes 786440 | tf_op jit(solution)/shard_map/ppermute | solution.py:316
  198.5 7.1 %collective-permute-start.9 = (bf16[64,128]{1,0:T(8,128)(2,1)S(1)}, bf16[64,128]{1,0:T(8,128)(2,1)S(1)}, u32[]{:S(2)}, u32[]{:S(2)}) collective-permute-start(bf16[64,128]{1,0:T(8,128)(2,1)S(1)} %slice_bitcast_fusion.4), channel_id=1, source_target_pairs={{0,256},{8,264},{16,272},{24,280},{32,288},{40,296},{48,304},{56,3... | collective-permute-start | bytes 49160 | tf_op jit(solution)/shard_map/ppermute | solution.py:316
  (3 other events, 2.1 us)
Sparse Core Ops, SparseCore 0:
  10.7 75.4 all-gather.3
  128.2 69.5 reduce-scatter.1

commit v4 on v3

--- a/solution.py
+++ b/solution.py
@@ -108,11 +108,6 @@
         side[w, START_AT:SIDE, :] = jnp.concatenate(
             [whole, part, jnp.zeros((14, BLOCK), f32)], axis=0
         ).astype(bf16)
-
-
-def stage(own, side, own_out, side_out):
-    own_out[...] = own[...]
-    side_out[...] = side[...]
 
 
 def start_of(meta, z_count, side, w):
@@ -347,30 +342,30 @@
     kv = jnp.concatenate([input_keys, input_values], axis=0)
     own = lax.all_gather(kv, "ctx", axis=0, tiled=False, axis_index_groups=runs)
 
-    ups = adapter_up_weight.reshape(up_rows, heads, HEAD).transpose(1, 0, 2)
-    ups = ups.reshape(up_rows * heads, HEAD)
-    lower = document_index[:, None] < jnp.arange(128, dtype=jnp.int32)[None, :]
-    counts = jnp.sum(lower.astype(f32), axis=0, keepdims=True).astype(bf16)
-    small = jnp.concatenate([ups, jnp.pad(counts, ((0, 15), (0, 0)))], axis=0)
-    small, _ = lax.optimization_barrier((small, kv))
-    small = lax.all_gather(small, "ctx", axis=0, tiled=False, axis_index_groups=runs)
-    small = jnp.stack([small, swap(small, across)])
-    small_other = swap(small, 1)
-
     chosen = [
         lax.dynamic_index_in_dim(adapter_down_weight, routes[0, j], 0, keepdims=False)
         for j in range(2)
     ]
     partial = jnp.dot(normed, jnp.concatenate(chosen, axis=1), preferred_element_type=f32)
-    lows = lax.all_to_all(
-        jnp.broadcast_to(partial[None], (exp_count,) + partial.shape), "exp", 0, 0
-    )
+    spread = jnp.broadcast_to(partial[None], (exp_count,) + partial.shape)
+    lows = lax.all_to_all(spread, "exp", 0, 0)
     low = pl.pallas_call(
         sum_low,
         out_shape=jax.ShapeDtypeStruct(partial.shape, bf16),
         in_specs=[vmem],
         out_specs=vmem,
     )(lows)
+    ups = adapter_up_weight.reshape(up_rows, heads, HEAD).transpose(1, 0, 2)
+    ups = ups.reshape(up_rows * heads, HEAD)
+    lower = document_index[:, None] < jnp.arange(128, dtype=jnp.int32)[None, :]
+    counts = jnp.sum(lower.astype(f32), axis=0, keepdims=True).astype(bf16)
+    small = jnp.concatenate([ups, jnp.pad(counts, ((0, 15), (0, 0)))], axis=0)
+    small, _ = lax.optimization_barrier((small, (kv, spread)))
+    small = lax.all_gather(small, "ctx", axis=0, tiled=False, axis_index_groups=runs)
+    small, low = lax.optimization_barrier((small, low))
+    small = jnp.stack([small, swap(small, across)])
+    small_other = swap(small, 1)
+
     low = jnp.stack([low, swap(low, across)])
     local = jnp.concatenate([frozen_query, output_gradient], axis=0)
     local, _ = lax.optimization_barrier((local, kv))
@@ -399,16 +394,6 @@
     )(meta, small, small_other, low, pair, ints)
     own, side = lax.optimization_barrier((own, side))
     other = swap(own, 1)
-    own, side = pl.pallas_call(
-        stage,
-        out_shape=(
-            jax.ShapeDtypeStruct(own.shape, bf16),
-            jax.ShapeDtypeStruct(side.shape, bf16),
-        ),
-        in_specs=[vmem] * 2,
-        out_specs=(vmem,) * 2,
-    )(own, side)
-
     quads = z_count // 2
     prob, out, stats = pl.pallas_call(
         functools.partial(forward, heads, z_count),

time: 215 us -> 216 us (level)
  starting transfers between devices: 34.3 us -> 38.6 us
  blocking collectives: 37.9 us -> 34.6 us
  waiting for transfers between devices: 78.7 us -> 81.3 us
    ppermute x10, waiting for transfers between devices: 23.6 us -> 29 us  [swap(): return lax.ppermute(array, 'ctx', [(i, i ^ distance) for i in range(count)])]
    all_to_all x1, starting transfers between devices: 5.35 us -> 9.41 us  [shards(): lows = lax.all_to_all(spread, 'exp', 0, 0)]
    all_gather x1, blocking collectives: 37.9 us -> 34.6 us  [shards(): lax.all_gather(small, 'ctx', axis=0, tiled=False, axis_index_groups=runs)]
    reduce_scatter x1, waiting for transfers between devices: 55 us -> 52.3 us  [shards(): lax.psum_scatter(chip, 'ctx', scatter_dimension=0, tiled=False, axis_inde...]
    pallas_call x1 -> x0, Pallas kernels: 2.63 us -> none  [shards(): pl.pallas_call(stage, out_shape=(jax.ShapeDtypeStruct(own.shape, bf16), j...]
    unnamed x29 -> x37, local copies, waits for them, and re-layouts: 6.1 us -> 6.09 us
  transfers between devices with their start and end apart: 13 -> 13, of which waited for: 7 -> 8; matrix products, arithmetic and copies ran while one was open for 7% -> 6% of each run, Pallas kernels for 4% -> 3%
where the time goes in v4:
time: 216 us
  waiting for transfers between devices  81.3 us (38%)
  starting transfers between devices  38.6 us (18%)
  blocking collectives  34.6 us (16%)
  Pallas kernels  20 us (9%)
  between operations  18.2 us (8%)
  local copies, waits for them, and re-layouts  16.5 us (8%)
  other arithmetic  6.11 us (3%)
    reduce_scatter x1, waiting for transfers between devices, shards(): lax.psum_scatter(chip, 'ctx', scatter_dimension=0, tiled=False, axis_inde...  52.3 us
    all_gather x1, blocking collectives, shards(): lax.all_gather(small, 'ctx', axis=0, tiled=False, axis_index_groups=runs)  34.6 us
    ppermute x10, starting transfers between devices, swap(): return lax.ppermute(array, 'ctx', [(i, i ^ distance) for i in range(count)])  29.2 us
    ppermute x10, waiting for transfers between devices, swap(): return lax.ppermute(array, 'ctx', [(i, i ^ distance) for i in range(count)])  29 us
    all_to_all x1, starting transfers between devices, shards(): lows = lax.all_to_all(spread, 'exp', 0, 0)  9.41 us
    pallas_call x1, Pallas kernels, shards(): pl.pallas_call(functools.partial(backward, heads, z_count), out_shape=(ja...  8.51 us
    unnamed x37, local copies, waits for them, and re-layouts  6.09 us
    pallas_call x1, Pallas kernels, shards(): pl.pallas_call(functools.partial(forward, heads, z_count), out_shape=(jax...  5.01 us
  transfers between devices with their start and end apart: 13, of which 8 were waited for; matrix products, arithmetic and copies ran while one was open for 6% of the time, Pallas kernels for 3%

profile of v4, /device:TPU:6, one launch (start us, length us, event | category | flops | bytes accessed | tf_op | source)
XLA Modules:
  0.0 215.7 jit_solution(14413635790304404921)
XLA Ops:
  16.8 9.4 %all-to-all-start = ((f32[8,128,128]{2,1,0:T(8,128)}), f32[8,128,128]{2,1,0:T(8,128)S(1)}, u32[]{:S(2)}, u32[]{:S(2)}) async-start(f32[8,128,128]{2,1,0:T(8,128)} %broadcast_in_dim.2), calls=%async_computation | async-start | bytes 1048576 | tf_op jit(solution)/shard_map/all_to_all | solution.py:351
  26.4 34.6 %all-gather.1 = bf16[1280,128]{1,0:T(8,128)(2,1)S(1)} all-gather(bf16[80,128]{1,0:T(8,128)(2,1)S(1)} %fusion.6), channel_id=3, replica_groups={{0,16,32,48,64,80,96,112,128,144,160,176,192,208,224,240},{8,24,40,56,7..., dimensions={0}, use_global_device_ids=true | all-gather | bytes 348160 | tf_op jit(solution)/shard_map/all_gather | solution.py:364
  63.5 4.8 %collective-permute-start.1 = (bf16[16,80,128]{2,1,0:T(8,128)(2,1)S(1)}, bf16[16,80,128]{2,1,0:T(8,128)(2,1)S(1)}, u32[]{:S(2)}, u32[]{:S(2)}) collective-permute-start(bf16[16,80,128]{2,1,0:T(8,128)(2,1)S(1)} %bitcast.67), channel_id=1, source_target_pairs={{0,256},{8,264},{16,272},{24,280},{32,288},{40,296},{48,304},{56,3... | collective-permute-start | bytes 983048 | tf_op jit(solution)/shard_map/ppermute | solution.py:311
  68.4 2.7 %collective-permute-start = (s32[8,128]{1,0:T(8,128)S(1)}, s32[8,128]{1,0:T(8,128)S(1)}, u32[]{:S(2)}, u32[]{:S(2)}) collective-permute-start(s32[8,128]{1,0:T(8,128)S(1)} %pad_add_fusion.1), channel_id=1, source_target_pairs={{0,256},{8,264},{16,272},{24,280},{32,288},{40,296},{48,304},{56,3... | collective-permute-start | bytes 12296 | tf_op jit(solution)/shard_map/ppermute | solution.py:311
  71.1 3.1 %collective-permute-done.1 = bf16[16,80,128]{2,1,0:T(8,128)(2,1)S(1)} collective-permute-done((bf16[16,80,128]{2,1,0:T(8,128)(2,1)S(1)}, bf16[16,80,128]{2,1,0:T(8,128)(2,1)S(1)}, u32[]{:S(2)}, u32[]{:S(2)}) %collective-permute-start.1) | collective-permute-done | bytes 327712 | tf_op jit(solution)/shard_map/ppermute | solution.py:311
  74.2 1.9 collective-permute-start.2
  76.2 4.7 %collective-permute-start.4 = (bf16[256,512]{1,0:T(8,128)(2,1)S(1)}, bf16[256,512]{1,0:T(8,128)(2,1)S(1)}, u32[]{:S(2)}, u32[]{:S(2)}) collective-permute-start(bf16[256,512]{1,0:T(8,128)(2,1)S(1)} %pad_maximum_fusion.2), channel_id=1, source_target_pairs={{0,256},{8,264},{16,272},{24,280},{32,288},{40,296},{48,304},{56,3... | collective-permute-start | bytes 786440 | tf_op jit(solution)/shard_map/ppermute | solution.py:311
  82.1 3.1 %stack.60.meta = s32[7]{0:T(128)} concatenate(s32[1]{0:T(128)} %bitcast, s32[1]{0:T(128)} %bitcast.1, s32[1]{0:T(128)} %bitcast.2, s32[1]{0:T(128)} %bitcast.5, s32[1]{0:T(128)} %bitcast.6, s32[1]{0:T(128)} %bitcast.8, s32[1]{0:T(128)} %bitcast.9), dimensions={0} | concatenate | bytes 56 | tf_op jit(solution)/shard_map/stack | solution.py:378
  85.8 2.7 %collective-permute-start.3 = (bf16[128,128]{1,0:T(8,128)(2,1)S(1)}, bf16[128,128]{1,0:T(8,128)(2,1)S(1)}, u32[]{:S(2)}, u32[]{:S(2)}) collective-permute-start(bf16[128,128]{1,0:T(8,128)(2,1)S(1)} %copy-done.12), channel_id=1, source_target_pairs={{0,256},{8,264},{16,272},{24,280},{32,288},{40,296},{48,304},{56,3... | collective-permute-start | bytes 98312 | tf_op jit(solution)/shard_map/ppermute | solution.py:311
  89.4 3.7 %collective-permute-done.3 = bf16[128,128]{1,0:T(8,128)(2,1)S(1)} collective-permute-done((bf16[128,128]{1,0:T(8,128)(2,1)S(1)}, bf16[128,128]{1,0:T(8,128)(2,1)S(1)}, u32[]{:S(2)}, u32[]{:S(2)}) %collective-permute-start.3) | collective-permute-done | bytes 32800 | tf_op jit(solution)/shard_map/ppermute | solution.py:311
  94.6 2.6 %shard_map.129.side = bf16[2,1168,128]{2,1,0:T(8,128)(2,1)} custom-call(s32[7]{0:T(128)} %stack.60.meta, bf16[2,16,80,128]{3,2,1,0:T(8,128)(2,1)} %copy-done.8, bf16[2,16,80,128]{3,2,1,0:T(8,128)(2,1)} %copy-done.10, bf16[2,128,128]{2,1,0:T(8,128)(2,1)} %pad_maximum_fusion.4.low_ref, bf16[2,256,512]{2,1,0:T(8,128)(2,1)} %pad_maximum_fusion.1.pair, ...), custom_call_target="tpu_custom_call" | custom-call | tf_op jit(solution)/shard_map/pallas_call | solution.py:389
  97.2 1.9 collective-permute-start.5
  99.1 2.8 %collective-permute-done.5.other = bf16[16,256,128]{2,1,0:T(8,128)(2,1)S(1)} collective-permute-done((bf16[16,256,128]{2,1,0:T(8,128)(2,1)}, bf16[16,256,128]{2,1,0:T(8,128)(2,1)S(1)}, u32[]{:S(2)}, u32[]{:S(2)}) %collective-permute-start.5) | collective-permute-done | bytes 1048608 | tf_op jit(solution)/shard_map/ppermute | solution.py:311
  104.2 5.0 %shard_map.130 = (bf16[2,8,512,512]{3,2,1,0:T(8,128)(2,1)S(1)}, f32[2,128,512]{2,1,0:T(8,128)S(1)}, f32[2,8,512]{2,1,0:T(8,128)S(1)}) custom-call(s32[7]{0:T(128)S(1)} %copy-done.7, bf16[16,256,128]{2,1,0:T(8,128)(2,1)S(1)} %bitcast.64, bf16[16,256,128]{2,1,0:T(8,128)(2,1)S(1)} %collective-permute-done.5.other, bf16[2,1168,128]{2,1,0:T(8,128)(2,1)S(1)} %copy-done.1), custom_call_target="tpu_custom_call" | custom-call | tf_op jit(solution)/shard_map/pallas_call | solution.py:398
  109.3 1.9 collective-permute-start.6
  111.2 5.2 %collective-permute-done.6.come = f32[8,512]{1,0:T(8,128)S(1)} collective-permute-done((f32[8,512]{1,0:T(8,128)S(1)}, f32[8,512]{1,0:T(8,128)S(1)}, u32[]{:S(2)}, u32[]{:S(2)}) %collective-permute-start.6) | collective-permute-done | bytes 16416 | tf_op jit(solution)/shard_map/ppermute | solution.py:311
  116.4 8.5 %shard_map.131 = (f32[128,512]{1,0:T(8,128)S(1)}, bf16[128,512]{1,0:T(8,128)(2,1)S(1)}, bf16[16,384,128]{2,1,0:T(8,128)(2,1)S(1)}, bf16[16,384,128]{2,1,0:T(8,128)(2,1)S(1)}) custom-call(s32[7]{0:T(128)S(1)} %copy-done.7, bf16[16,256,128]{2,1,0:T(8,128)(2,1)S(1)} %bitcast.65, bf16[16,256,128]{2,1,0:T(8,128)(2,1)S(1)} %collective-permute-done.5.other, ...), custom_call_target="tpu_custom_call" | custom-call | tf_op jit(solution)/shard_map/pallas_call | solution.py:413
  125.6 1.9 collective-permute-start.7
  127.6 3.4 %collective-permute-done.7 = bf16[16,384,128]{2,1,0:T(8,128)(2,1)S(1)} collective-permute-done((bf16[16,384,128]{2,1,0:T(8,128)(2,1)S(1)}, bf16[16,384,128]{2,1,0:T(8,128)(2,1)S(1)}, u32[]{:S(2)}, u32[]{:S(2)}) %collective-permute-start.7) | collective-permute-done | bytes 1572896 | tf_op jit(solution)/shard_map/ppermute | solution.py:311
  132.6 1.9 collective-permute-start.8
  134.6 9.8 %collective-permute-done.8 = bf16[2,128,512]{2,1,0:T(8,128)(2,1)S(1)} collective-permute-done((bf16[2,128,512]{2,1,0:T(8,128)(2,1)S(1)}, bf16[2,128,512]{2,1,0:T(8,128)(2,1)S(1)}, u32[]{:S(2)}, u32[]{:S(2)}) %collective-permute-start.8) | collective-permute-done | bytes 262176 | tf_op jit(solution)/shard_map/ppermute | solution.py:311
  145.1 2.2 %shard_map.132 = (f32[128,512]{1,0:T(8,128)}, f32[128,512]{1,0:T(8,128)}) custom-call(s32[7]{0:T(128)} %stack.60.meta, f32[2,128,512]{2,1,0:T(8,128)} %copy-done.3, f32[2,8,512]{2,1,0:T(8,128)} %copy-done.4, f32[8,512]{1,0:T(8,128)} %copy-done.6, bf16[128,512]{1,0:T(8,128)(2,1)} %get-tuple-element.42.far_out, bf16[128,512]{1,0:T(8,128)(2,1)} %get-tuple-element.41.far_dquery, ...), custom_call_target="tpu_custom_call" | custom-call | tf_op jit(solution)/shard_map/pallas_call | solution.py:439
  147.3 52.3 %reduce-scatter.2.cloned.1.call-done = bf16[1,384,128]{2,1,0:T(8,128)(2,1)} async-done(((bf16[16,384,128]{2,1,0:T(8,128)(2,1)}), bf16[1,384,128]{2,1,0:T(8,128)(2,1)}) %reduce-scatter.2.cloned.1.call-update) | async-done | bytes 98320 | tf_op jit(solution)/shard_map/reduce_scatter | solution.py:432
  200.3 4.8 %collective-permute-start.9 = (bf16[64,128]{1,0:T(8,128)(2,1)S(1)}, bf16[64,128]{1,0:T(8,128)(2,1)S(1)}, u32[]{:S(2)}, u32[]{:S(2)}) collective-permute-start(bf16[64,128]{1,0:T(8,128)(2,1)S(1)} %slice_bitcast_fusion.4), channel_id=1, source_target_pairs={{0,256},{8,264},{16,272},{24,280},{32,288},{40,296},{48,304},{56,3... | collective-permute-start | bytes 49160 | tf_op jit(solution)/shard_map/ppermute | solution.py:311
  (75 shorter events, 22.4 us)
Async XLA Ops:
  7.2 90.0 %all-gather.4.cloned.1.call-start = ((), (), s32[]{:S(2)}) async-start(), calls=%async_computation.3 | async-start | bytes 1114112 | tf_op jit(solution)/shard_map/all_gather | solution.py:343
  8.0 18.2 %copy-start.15 = (bf16[16,512]{1,0:T(8,128)(2,1)S(1)}, bf16[16,512]{1,0:T(8,128)(2,1)}, u32[]{:S(2)}) copy-start(bf16[16,512]{1,0:T(8,128)(2,1)} %param.16) | copy-start | bytes 49156
  8.8 17.5 %copy-start.17 = (s32[128]{0:T(128)S(1)}, s32[128]{0:T(128)}, u32[]{:S(2)}) copy-start(s32[128]{0:T(128)} %param.13) | copy-start | bytes 1540
  15.7 52.7 %copy-start.16 = (s32[1,2]{1,0:T(1,128)S(1)}, s32[1,2]{1,0:T(1,128)}, u32[]{:S(2)}) copy-start(s32[1,2]{1,0:T(1,128)} %param.14) | copy-start | bytes 28
  16.8 59.3 %copy-start.13 = (bf16[128,512]{1,0:T(8,128)(2,1)S(1)}, bf16[128,512]{1,0:T(8,128)(2,1)}, u32[]{:S(2)}) copy-start(bf16[128,512]{1,0:T(8,128)(2,1)} %param.17) | copy-start | bytes 393220
  16.8 59.3 %copy-start.14 = (bf16[128,512]{1,0:T(8,128)(2,1)S(1)}, bf16[128,512]{1,0:T(8,128)(2,1)}, u32[]{:S(2)}) copy-start(bf16[128,512]{1,0:T(8,128)(2,1)} %param.10) | copy-start | bytes 393220
  16.8 44.2 %all-to-all-start = ((f32[8,128,128]{2,1,0:T(8,128)}), f32[8,128,128]{2,1,0:T(8,128)S(1)}, u32[]{:S(2)}, u32[]{:S(2)}) async-start(f32[8,128,128]{2,1,0:T(8,128)} %broadcast_in_dim.2), calls=%async_computation | async-start | bytes 1048576 | tf_op jit(solution)/shard_map/all_to_all | solution.py:351
  26.3 173.4 %reduce-scatter.2.cloned.1.call-start = ((), (), s32[]{:S(2)}) async-start(), calls=%async_computation.2 | async-start | bytes 1671168 | tf_op jit(solution)/shard_map/reduce_scatter | solution.py:432
  63.5 22.3 %copy-start.12 = (bf16[128,128]{1,0:T(8,128)(2,1)S(1)}, bf16[128,128]{1,0:T(8,128)(2,1)}, u32[]{:S(2)}) copy-start(bf16[128,128]{1,0:T(8,128)(2,1)} %shard_map.128) | copy-start | bytes 98308
  63.5 10.6 %collective-permute-start.1 = (bf16[16,80,128]{2,1,0:T(8,128)(2,1)S(1)}, bf16[16,80,128]{2,1,0:T(8,128)(2,1)S(1)}, u32[]{:S(2)}, u32[]{:S(2)}) collective-permute-start(bf16[16,80,128]{2,1,0:T(8,128)(2,1)S(1)} %bitcast.67), channel_id=1, source_target_pairs={{0,256},{8,264},{16,272},{24,280},{32,288},{40,296},{48,304},{56,3... | collective-permute-start | bytes 983048 | tf_op jit(solution)/shard_map/ppermute | solution.py:311
  68.4 13.1 %collective-permute-start = (s32[8,128]{1,0:T(8,128)S(1)}, s32[8,128]{1,0:T(8,128)S(1)}, u32[]{:S(2)}, u32[]{:S(2)}) collective-permute-start(s32[8,128]{1,0:T(8,128)S(1)} %pad_add_fusion.1), channel_id=1, source_target_pairs={{0,256},{8,264},{16,272},{24,280},{32,288},{40,296},{48,304},{56,3... | collective-permute-start | bytes 12296 | tf_op jit(solution)/shard_map/ppermute | solution.py:311
  74.2 19.5 %copy-start.8 = (bf16[2,16,80,128]{3,2,1,0:T(8,128)(2,1)}, bf16[2,16,80,128]{3,2,1,0:T(8,128)(2,1)S(1)}, u32[]{:S(2)}) copy-start(bf16[2,16,80,128]{3,2,1,0:T(8,128)(2,1)S(1)} %pad_maximum_fusion.own) | copy-start | bytes 1966084
  74.2 19.5 %collective-permute-start.2 = (bf16[2,16,80,128]{3,2,1,0:T(8,128)(2,1)S(1)}, bf16[2,16,80,128]{3,2,1,0:T(8,128)(2,1)S(1)}, u32[]{:S(2)}, u32[]{:S(2)}) collective-permute-start(bf16[2,16,80,128]{3,2,1,0:T(8,128)(2,1)S(1)} %pad_maximum_fusion.own), channel_id=1, source_target_pairs={{0,8},{8,0},{16,24},{24,16},{32,40},{40,32},{48,56},{56,48},{64,72... | collective-permute-start | bytes 1966088 | tf_op jit(solution)/shard_map/ppermute | solution.py:311
  76.2 12.3 %collective-permute-start.4 = (bf16[256,512]{1,0:T(8,128)(2,1)S(1)}, bf16[256,512]{1,0:T(8,128)(2,1)S(1)}, u32[]{:S(2)}, u32[]{:S(2)}) collective-permute-start(bf16[256,512]{1,0:T(8,128)(2,1)S(1)} %pad_maximum_fusion.2), channel_id=1, source_target_pairs={{0,256},{8,264},{16,272},{24,280},{32,288},{40,296},{48,304},{56,3... | collective-permute-start | bytes 786440 | tf_op jit(solution)/shard_map/ppermute | solution.py:311
  85.8 7.3 %collective-permute-start.3 = (bf16[128,128]{1,0:T(8,128)(2,1)S(1)}, bf16[128,128]{1,0:T(8,128)(2,1)S(1)}, u32[]{:S(2)}, u32[]{:S(2)}) collective-permute-start(bf16[128,128]{1,0:T(8,128)(2,1)S(1)} %copy-done.12), channel_id=1, source_target_pairs={{0,256},{8,264},{16,272},{24,280},{32,288},{40,296},{48,304},{56,3... | collective-permute-start | bytes 98312 | tf_op jit(solution)/shard_map/ppermute | solution.py:311
  89.4 12.6 %copy-start.7 = (s32[7]{0:T(128)S(1)}, s32[7]{0:T(128)}, u32[]{:S(2)}) copy-start(s32[7]{0:T(128)} %stack.60.meta) | copy-start | bytes 88
  97.2 4.8 %collective-permute-start.5 = (bf16[16,256,128]{2,1,0:T(8,128)(2,1)}, bf16[16,256,128]{2,1,0:T(8,128)(2,1)S(1)}, u32[]{:S(2)}, u32[]{:S(2)}) collective-permute-start(bf16[16,256,128]{2,1,0:T(8,128)(2,1)} %bitcast.63), channel_id=1, source_target_pairs={{0,8},{8,0},{16,24},{24,16},{32,40},{40,32},{48,56},{56,48},{64,72... | collective-permute-start | bytes 3145736 | tf_op jit(solution)/shard_map/ppermute | solution.py:311
  109.2 15.7 %copy-start.4 = (f32[2,8,512]{2,1,0:T(8,128)}, f32[2,8,512]{2,1,0:T(8,128)S(1)}, u32[]{:S(2)}) copy-start(f32[2,8,512]{2,1,0:T(8,128)S(1)} %get-tuple-element.30.stats) | copy-start | bytes 98308
  109.2 23.3 %copy-start.3 = (f32[2,128,512]{2,1,0:T(8,128)}, f32[2,128,512]{2,1,0:T(8,128)S(1)}, u32[]{:S(2)}) copy-start(f32[2,128,512]{2,1,0:T(8,128)S(1)} %get-tuple-element.29.out_t) | copy-start | bytes 1572868
  109.3 7.1 %collective-permute-start.6 = (f32[8,512]{1,0:T(8,128)S(1)}, f32[8,512]{1,0:T(8,128)S(1)}, u32[]{:S(2)}, u32[]{:S(2)}) collective-permute-start(f32[8,512]{1,0:T(8,128)S(1)} %select_bitcast_fusion), channel_id=1, source_target_pairs={{0,256},{8,264},{16,272},{24,280},{32,288},{40,296},{48,304},{56,3... | collective-permute-start | bytes 49160 | tf_op jit(solution)/shard_map/ppermute | solution.py:311
  116.4 8.5 %copy-start.6 = (f32[8,512]{1,0:T(8,128)}, f32[8,512]{1,0:T(8,128)S(1)}, u32[]{:S(2)}) copy-start(f32[8,512]{1,0:T(8,128)S(1)} %collective-permute-done.6.come) | copy-start | bytes 49156
  125.6 5.3 %collective-permute-start.7 = (bf16[16,384,128]{2,1,0:T(8,128)(2,1)S(1)}, bf16[16,384,128]{2,1,0:T(8,128)(2,1)S(1)}, u32[]{:S(2)}, u32[]{:S(2)}) collective-permute-start(bf16[16,384,128]{2,1,0:T(8,128)(2,1)S(1)} %get-tuple-element.34), channel_id=1, source_target_pairs={{0,8},{8,0},{16,24},{24,16},{32,40},{40,32},{48,56},{56,48},{64,72... | collective-permute-start | bytes 4718600 | tf_op jit(solution)/shard_map/ppermute | solution.py:311
  132.6 11.7 %collective-permute-start.8 = (bf16[2,128,512]{2,1,0:T(8,128)(2,1)S(1)}, bf16[2,128,512]{2,1,0:T(8,128)(2,1)S(1)}, u32[]{:S(2)}, u32[]{:S(2)}) collective-permute-start(bf16[2,128,512]{2,1,0:T(8,128)(2,1)S(1)} %pad_maximum_fusion.3), channel_id=1, source_target_pairs={{0,256},{8,264},{16,272},{24,280},{32,288},{40,296},{48,304},{56,3... | collective-permute-start | bytes 786440 | tf_op jit(solution)/shard_map/ppermute | solution.py:311
  200.3 7.1 %collective-permute-start.9 = (bf16[64,128]{1,0:T(8,128)(2,1)S(1)}, bf16[64,128]{1,0:T(8,128)(2,1)S(1)}, u32[]{:S(2)}, u32[]{:S(2)}) collective-permute-start(bf16[64,128]{1,0:T(8,128)(2,1)S(1)} %slice_bitcast_fusion.4), channel_id=1, source_target_pairs={{0,256},{8,264},{16,272},{24,280},{32,288},{40,296},{48,304},{56,3... | collective-permute-start | bytes 49160 | tf_op jit(solution)/shard_map/ppermute | solution.py:311
  (7 other events, 13.7 us)
Sparse Core Ops, SparseCore 0:
  10.7 75.5 all-gather.3
  132.7 66.8 reduce-scatter.1

commit v5 on v4

--- a/solution.py
+++ b/solution.py
@@ -355,26 +355,28 @@
         in_specs=[vmem],
         out_specs=vmem,
     )(lows)
+    local = jnp.concatenate([frozen_query, output_gradient], axis=0)
+    ints = jnp.concatenate(
+        [document_index.reshape(1, rows), jnp.pad(routes, ((0, 6), (0, rows - 2)))], axis=0
+    )
+    local, ints, _ = lax.optimization_barrier((local, ints, kv))
+
     ups = adapter_up_weight.reshape(up_rows, heads, HEAD).transpose(1, 0, 2)
     ups = ups.reshape(up_rows * heads, HEAD)
     lower = document_index[:, None] < jnp.arange(128, dtype=jnp.int32)[None, :]
     counts = jnp.sum(lower.astype(f32), axis=0, keepdims=True).astype(bf16)
     small = jnp.concatenate([ups, jnp.pad(counts, ((0, 15), (0, 0)))], axis=0)
-    small, _ = lax.optimization_barrier((small, (kv, spread)))
+    small, _ = lax.optimization_barrier((small, (kv, spread, local, ints)))
     small = lax.all_gather(small, "ctx", axis=0, tiled=False, axis_index_groups=runs)
+    small, low, local_far, ints_far = lax.optimization_barrier(
+        (small, low, swap(local, across), swap(ints, across))
+    )
+    pair, ints = jnp.stack([local, local_far]), jnp.stack([ints, ints_far])
+    small = jnp.stack([small, swap(small, across)])
+    low = jnp.stack([low, swap(low, across)])
     small, low = lax.optimization_barrier((small, low))
-    small = jnp.stack([small, swap(small, across)])
     small_other = swap(small, 1)
 
-    low = jnp.stack([low, swap(low, across)])
-    local = jnp.concatenate([frozen_query, output_gradient], axis=0)
-    local, _ = lax.optimization_barrier((local, kv))
-    pair = jnp.stack([local, swap(local, across)])
-    ints = jnp.concatenate(
-        [document_index.reshape(1, rows), jnp.pad(routes, ((0, 7 - 1), (0, rows - 2)))], axis=0
-    )
-    ints, _ = lax.optimization_barrier((ints, kv))
-    ints = jnp.stack([ints, swap(ints, across)])
     meta = jnp.stack(
         [
             place // across,

time: 216 us -> 219 us (1.014)
  Pallas kernels: 20 us -> 25.2 us
  waiting for transfers between devices: 81.3 us -> 76.4 us
    pallas_call x1, Pallas kernels: 8.51 us -> 11.7 us  [shards(): pl.pallas_call(functools.partial(backward, heads, z_count), out_shape=(ja...]
    reduce_scatter x1, waiting for transfers between devices: 52.3 us -> 49.7 us  [shards(): lax.psum_scatter(chip, 'ctx', scatter_dimension=0, tiled=False, axis_inde...]
    ppermute x10, waiting for transfers between devices: 29 us -> 26.7 us  [swap(): return lax.ppermute(array, 'ctx', [(i, i ^ distance) for i in range(count)])]
    unnamed x37 -> x35, local copies, waits for them, and re-layouts: 6.09 us -> 6.1 us
  transfers between devices with their start and end apart: 13 -> 13, of which waited for: 8 -> 7; matrix products, arithmetic and copies ran while one was open for 6% -> 6% of each run, Pallas kernels for 3% -> 3%
where the time goes in v5:
time: 219 us; the launch traced here: 218 us
  waiting for transfers between devices  76.4 us (35%)
  starting transfers between devices  39.1 us (18%)
  blocking collectives  35.1 us (16%)
  Pallas kernels  25.2 us (12%)
  between operations  18.3 us (8%)
  local copies, waits for them, and re-layouts  16.6 us (8%)
  other arithmetic  6.86 us (3%)
    reduce_scatter x1, waiting for transfers between devices, shards(): lax.psum_scatter(chip, 'ctx', scatter_dimension=0, tiled=False, axis_inde...  49.7 us
    all_gather x1, blocking collectives, shards(): lax.all_gather(small, 'ctx', axis=0, tiled=False, axis_index_groups=runs)  35.1 us
    ppermute x10, starting transfers between devices, swap(): return lax.ppermute(array, 'ctx', [(i, i ^ distance) for i in range(count)])  29.8 us
    ppermute x10, waiting for transfers between devices, swap(): return lax.ppermute(array, 'ctx', [(i, i ^ distance) for i in range(count)])  26.7 us
    pallas_call x1, Pallas kernels, shards(): pl.pallas_call(functools.partial(backward, heads, z_count), out_shape=(ja...  11.7 us
    all_to_all x1, starting transfers between devices, shards(): lows = lax.all_to_all(spread, 'exp', 0, 0)  9.28 us
    pallas_call x1, Pallas kernels, shards(): pl.pallas_call(functools.partial(forward, heads, z_count), out_shape=(jax...  7.03 us
    unnamed x35, local copies, waits for them, and re-layouts  6.1 us
  transfers between devices with their start and end apart: 13, of which 7 were waited for; matrix products, arithmetic and copies ran while one was open for 6% of the time, Pallas kernels for 3%

profile of v5, /device:TPU:6, one launch (start us, length us, event | category | flops | bytes accessed | tf_op | source)
XLA Modules:
  0.0 217.8 jit_solution(17813158456899287864)
XLA Ops:
  16.9 9.3 %all-to-all-start = ((f32[8,128,128]{2,1,0:T(8,128)}), f32[8,128,128]{2,1,0:T(8,128)S(1)}, u32[]{:S(2)}, u32[]{:S(2)}) async-start(f32[8,128,128]{2,1,0:T(8,128)} %broadcast_in_dim.2), calls=%async_computation | async-start | bytes 1048576 | tf_op jit(solution)/shard_map/all_to_all | solution.py:351
  26.3 1.9 collective-permute-start.1
  28.2 5.4 %collective-permute-start = (bf16[256,512]{1,0:T(8,128)(2,1)S(1)}, bf16[256,512]{1,0:T(8,128)(2,1)S(1)}, u32[]{:S(2)}, u32[]{:S(2)}) collective-permute-start(bf16[256,512]{1,0:T(8,128)(2,1)S(1)} %pad_maximum_fusion.2), channel_id=1, source_target_pairs={{0,256},{8,264},{16,272},{24,280},{32,288},{40,296},{48,304},{56,3... | collective-permute-start | bytes 786440 | tf_op jit(solution)/shard_map/ppermute | solution.py:311
  33.8 35.1 %all-gather = bf16[1280,128]{1,0:T(8,128)(2,1)S(1)} all-gather(bf16[80,128]{1,0:T(8,128)(2,1)S(1)} %fusion.6), channel_id=2, replica_groups={{0,16,32,48,64,80,96,112,128,144,160,176,192,208,224,240},{8,24,40,56,7..., dimensions={0}, use_global_device_ids=true | all-gather | bytes 348160 | tf_op jit(solution)/shard_map/all_gather | solution.py:370
  69.7 1.7 shard_map.128
  71.4 5.0 %collective-permute-start.2 = (bf16[16,80,128]{2,1,0:T(8,128)(2,1)S(1)}, bf16[16,80,128]{2,1,0:T(8,128)(2,1)S(1)}, u32[]{:S(2)}, u32[]{:S(2)}) collective-permute-start(bf16[16,80,128]{2,1,0:T(8,128)(2,1)S(1)} %bitcast.67), channel_id=1, source_target_pairs={{0,256},{8,264},{16,272},{24,280},{32,288},{40,296},{48,304},{56,3... | collective-permute-start | bytes 983048 | tf_op jit(solution)/shard_map/ppermute | solution.py:311
  76.4 2.3 %collective-permute-start.3 = (bf16[128,128]{1,0:T(8,128)(2,1)}, bf16[128,128]{1,0:T(8,128)(2,1)S(1)}, u32[]{:S(2)}, u32[]{:S(2)}) collective-permute-start(bf16[128,128]{1,0:T(8,128)(2,1)} %shard_map.128), channel_id=1, source_target_pairs={{0,256},{8,264},{16,272},{24,280},{32,288},{40,296},{48,304},{56,3... | collective-permute-start | bytes 98312 | tf_op jit(solution)/shard_map/ppermute | solution.py:311
  78.7 5.2 %collective-permute-done.3 = bf16[128,128]{1,0:T(8,128)(2,1)S(1)} collective-permute-done((bf16[128,128]{1,0:T(8,128)(2,1)}, bf16[128,128]{1,0:T(8,128)(2,1)S(1)}, u32[]{:S(2)}, u32[]{:S(2)}) %collective-permute-start.3) | collective-permute-done | bytes 32800 | tf_op jit(solution)/shard_map/ppermute | solution.py:311
  85.4 1.9 collective-permute-start.4
  88.6 3.1 %stack.60.meta = s32[7]{0:T(128)} concatenate(s32[1]{0:T(128)} %bitcast, s32[1]{0:T(128)} %bitcast.1, s32[1]{0:T(128)} %bitcast.2, s32[1]{0:T(128)} %bitcast.5, s32[1]{0:T(128)} %bitcast.6, s32[1]{0:T(128)} %bitcast.17, s32[1]{0:T(128)} %bitcast.18), dimensions={0} | concatenate | bytes 56 | tf_op jit(solution)/shard_map/stack | solution.py:380
  94.0 2.6 %shard_map.129.side = bf16[2,1168,128]{2,1,0:T(8,128)(2,1)} custom-call(s32[7]{0:T(128)} %stack.60.meta, bf16[2,16,80,128]{3,2,1,0:T(8,128)(2,1)} %copy-done.8, bf16[2,16,80,128]{3,2,1,0:T(8,128)(2,1)} %copy-done.10, bf16[2,128,128]{2,1,0:T(8,128)(2,1)} %pad_maximum_fusion.4.low_ref, bf16[2,256,512]{2,1,0:T(8,128)(2,1)} %pad_maximum_fusion.1.pair, ...), custom_call_target="tpu_custom_call" | custom-call | tf_op jit(solution)/shard_map/pallas_call | solution.py:391
  96.5 2.4 %collective-permute-start.5 = (bf16[16,256,128]{2,1,0:T(8,128)(2,1)}, bf16[16,256,128]{2,1,0:T(8,128)(2,1)S(1)}, u32[]{:S(2)}, u32[]{:S(2)}) collective-permute-start(bf16[16,256,128]{2,1,0:T(8,128)(2,1)} %bitcast.63), channel_id=1, source_target_pairs={{0,8},{8,0},{16,24},{24,16},{32,40},{40,32},{48,56},{56,48},{64,72... | collective-permute-start | bytes 3145736 | tf_op jit(solution)/shard_map/ppermute | solution.py:311
  98.9 2.5 %collective-permute-done.5.other = bf16[16,256,128]{2,1,0:T(8,128)(2,1)S(1)} collective-permute-done((bf16[16,256,128]{2,1,0:T(8,128)(2,1)}, bf16[16,256,128]{2,1,0:T(8,128)(2,1)S(1)}, u32[]{:S(2)}, u32[]{:S(2)}) %collective-permute-start.5) | collective-permute-done | bytes 1048608 | tf_op jit(solution)/shard_map/ppermute | solution.py:311
  103.7 7.0 %shard_map.130 = (bf16[2,8,512,512]{3,2,1,0:T(8,128)(2,1)S(1)}, f32[2,128,512]{2,1,0:T(8,128)S(1)}, f32[2,8,512]{2,1,0:T(8,128)S(1)}) custom-call(s32[7]{0:T(128)S(1)} %copy-done.7, bf16[16,256,128]{2,1,0:T(8,128)(2,1)S(1)} %bitcast.64, bf16[16,256,128]{2,1,0:T(8,128)(2,1)S(1)} %collective-permute-done.5.other, bf16[2,1168,128]{2,1,0:T(8,128)(2,1)S(1)} %copy-done.1), custom_call_target="tpu_custom_call" | custom-call | tf_op jit(solution)/shard_map/pallas_call | solution.py:400
  110.8 1.9 collective-permute-start.6
  112.7 5.2 %collective-permute-done.6.come = f32[8,512]{1,0:T(8,128)S(1)} collective-permute-done((f32[8,512]{1,0:T(8,128)S(1)}, f32[8,512]{1,0:T(8,128)S(1)}, u32[]{:S(2)}, u32[]{:S(2)}) %collective-permute-start.6) | collective-permute-done | bytes 16416 | tf_op jit(solution)/shard_map/ppermute | solution.py:311
  117.9 11.7 %shard_map.131 = (f32[128,512]{1,0:T(8,128)S(1)}, bf16[128,512]{1,0:T(8,128)(2,1)S(1)}, bf16[16,384,128]{2,1,0:T(8,128)(2,1)S(1)}, bf16[16,384,128]{2,1,0:T(8,128)(2,1)S(1)}) custom-call(s32[7]{0:T(128)S(1)} %copy-done.7, bf16[16,256,128]{2,1,0:T(8,128)(2,1)S(1)} %bitcast.65, bf16[16,256,128]{2,1,0:T(8,128)(2,1)S(1)} %collective-permute-done.5.other, ...), custom_call_target="tpu_custom_call" | custom-call | tf_op jit(solution)/shard_map/pallas_call | solution.py:415
  130.4 1.9 collective-permute-start.7
  132.3 3.4 %collective-permute-done.7 = bf16[16,384,128]{2,1,0:T(8,128)(2,1)S(1)} collective-permute-done((bf16[16,384,128]{2,1,0:T(8,128)(2,1)S(1)}, bf16[16,384,128]{2,1,0:T(8,128)(2,1)S(1)}, u32[]{:S(2)}, u32[]{:S(2)}) %collective-permute-start.7) | collective-permute-done | bytes 1572896 | tf_op jit(solution)/shard_map/ppermute | solution.py:311
  137.4 1.9 collective-permute-start.8
  139.3 9.8 %collective-permute-done.8 = bf16[2,128,512]{2,1,0:T(8,128)(2,1)S(1)} collective-permute-done((bf16[2,128,512]{2,1,0:T(8,128)(2,1)S(1)}, bf16[2,128,512]{2,1,0:T(8,128)(2,1)S(1)}, u32[]{:S(2)}, u32[]{:S(2)}) %collective-permute-start.8) | collective-permute-done | bytes 262176 | tf_op jit(solution)/shard_map/ppermute | solution.py:311
  149.9 2.2 %shard_map.132 = (f32[128,512]{1,0:T(8,128)}, f32[128,512]{1,0:T(8,128)}) custom-call(s32[7]{0:T(128)} %stack.60.meta, f32[2,128,512]{2,1,0:T(8,128)} %copy-done.3, f32[2,8,512]{2,1,0:T(8,128)} %copy-done.4, f32[8,512]{1,0:T(8,128)} %copy-done.6, bf16[128,512]{1,0:T(8,128)(2,1)} %get-tuple-element.50.far_out, bf16[128,512]{1,0:T(8,128)(2,1)} %get-tuple-element.49.far_dquery, ...), custom_call_target="tpu_custom_call" | custom-call | tf_op jit(solution)/shard_map/pallas_call | solution.py:441
  152.1 49.7 %reduce-scatter.2.cloned.1.call-done = bf16[1,384,128]{2,1,0:T(8,128)(2,1)} async-done(((bf16[16,384,128]{2,1,0:T(8,128)(2,1)}), bf16[1,384,128]{2,1,0:T(8,128)(2,1)}) %reduce-scatter.2.cloned.1.call-update) | async-done | bytes 98320 | tf_op jit(solution)/shard_map/reduce_scatter | solution.py:434
  202.5 5.1 %collective-permute-start.9 = (bf16[64,128]{1,0:T(8,128)(2,1)S(1)}, bf16[64,128]{1,0:T(8,128)(2,1)S(1)}, u32[]{:S(2)}, u32[]{:S(2)}) collective-permute-start(bf16[64,128]{1,0:T(8,128)(2,1)S(1)} %slice_bitcast_fusion.4), channel_id=1, source_target_pairs={{0,256},{8,264},{16,272},{24,280},{32,288},{40,296},{48,304},{56,3... | collective-permute-start | bytes 49160 | tf_op jit(solution)/shard_map/ppermute | solution.py:311
  (73 shorter events, 21.2 us)
Async XLA Ops:
  7.2 8.6 %copy-start = (bf16[128,1024]{1,0:T(8,128)(2,1)S(1)}, bf16[128,1024]{1,0:T(8,128)(2,1)}, u32[]{:S(2)}) copy-start(bf16[128,1024]{1,0:T(8,128)(2,1)} %param.9) | copy-start | bytes 786436
  7.2 89.4 %all-gather.4.cloned.1.call-start = ((), (), s32[]{:S(2)}) async-start(), calls=%async_computation.3 | async-start | bytes 1114112 | tf_op jit(solution)/shard_map/all_gather | solution.py:343
  8.0 18.2 %copy-start.12 = (bf16[128,512]{1,0:T(8,128)(2,1)S(1)}, bf16[128,512]{1,0:T(8,128)(2,1)}, u32[]{:S(2)}) copy-start(bf16[128,512]{1,0:T(8,128)(2,1)} %param.17) | copy-start | bytes 393220
  8.0 18.2 %copy-start.13 = (bf16[128,512]{1,0:T(8,128)(2,1)S(1)}, bf16[128,512]{1,0:T(8,128)(2,1)}, u32[]{:S(2)}) copy-start(bf16[128,512]{1,0:T(8,128)(2,1)} %param.10) | copy-start | bytes 393220
  15.7 10.6 %copy-start.15 = (s32[1,2]{1,0:T(1,128)S(1)}, s32[1,2]{1,0:T(1,128)}, u32[]{:S(2)}) copy-start(s32[1,2]{1,0:T(1,128)} %param.14) | copy-start | bytes 28
  15.7 10.6 %copy-start.16 = (s32[128]{0:T(128)S(1)}, s32[128]{0:T(128)}, u32[]{:S(2)}) copy-start(s32[128]{0:T(128)} %param.13) | copy-start | bytes 1540
  15.7 17.9 %copy-start.14 = (bf16[16,512]{1,0:T(8,128)(2,1)S(1)}, bf16[16,512]{1,0:T(8,128)(2,1)}, u32[]{:S(2)}) copy-start(bf16[16,512]{1,0:T(8,128)(2,1)} %param.16) | copy-start | bytes 49156
  16.9 52.0 %all-to-all-start = ((f32[8,128,128]{2,1,0:T(8,128)}), f32[8,128,128]{2,1,0:T(8,128)S(1)}, u32[]{:S(2)}, u32[]{:S(2)}) async-start(f32[8,128,128]{2,1,0:T(8,128)} %broadcast_in_dim.2), calls=%async_computation | async-start | bytes 1048576 | tf_op jit(solution)/shard_map/all_to_all | solution.py:351
  26.2 175.5 %reduce-scatter.2.cloned.1.call-start = ((), (), s32[]{:S(2)}) async-start(), calls=%async_computation.2 | async-start | bytes 1671168 | tf_op jit(solution)/shard_map/reduce_scatter | solution.py:434
  26.3 45.1 %collective-permute-start.1 = (s32[8,128]{1,0:T(8,128)S(1)}, s32[8,128]{1,0:T(8,128)S(1)}, u32[]{:S(2)}, u32[]{:S(2)}) collective-permute-start(s32[8,128]{1,0:T(8,128)S(1)} %pad_add_fusion.1), channel_id=1, source_target_pairs={{0,256},{8,264},{16,272},{24,280},{32,288},{40,296},{48,304},{56,3... | collective-permute-start | bytes 12296 | tf_op jit(solution)/shard_map/ppermute | solution.py:311
  28.2 43.2 %collective-permute-start = (bf16[256,512]{1,0:T(8,128)(2,1)S(1)}, bf16[256,512]{1,0:T(8,128)(2,1)S(1)}, u32[]{:S(2)}, u32[]{:S(2)}) collective-permute-start(bf16[256,512]{1,0:T(8,128)(2,1)S(1)} %pad_maximum_fusion.2), channel_id=1, source_target_pairs={{0,256},{8,264},{16,272},{24,280},{32,288},{40,296},{48,304},{56,3... | collective-permute-start | bytes 786440 | tf_op jit(solution)/shard_map/ppermute | solution.py:311
  71.4 13.9 %collective-permute-start.2 = (bf16[16,80,128]{2,1,0:T(8,128)(2,1)S(1)}, bf16[16,80,128]{2,1,0:T(8,128)(2,1)S(1)}, u32[]{:S(2)}, u32[]{:S(2)}) collective-permute-start(bf16[16,80,128]{2,1,0:T(8,128)(2,1)S(1)} %bitcast.67), channel_id=1, source_target_pairs={{0,256},{8,264},{16,272},{24,280},{32,288},{40,296},{48,304},{56,3... | collective-permute-start | bytes 983048 | tf_op jit(solution)/shard_map/ppermute | solution.py:311
  76.4 7.5 %collective-permute-start.3 = (bf16[128,128]{1,0:T(8,128)(2,1)}, bf16[128,128]{1,0:T(8,128)(2,1)S(1)}, u32[]{:S(2)}, u32[]{:S(2)}) collective-permute-start(bf16[128,128]{1,0:T(8,128)(2,1)} %shard_map.128), channel_id=1, source_target_pairs={{0,256},{8,264},{16,272},{24,280},{32,288},{40,296},{48,304},{56,3... | collective-permute-start | bytes 98312 | tf_op jit(solution)/shard_map/ppermute | solution.py:311
  85.4 7.8 %copy-start.8 = (bf16[2,16,80,128]{3,2,1,0:T(8,128)(2,1)}, bf16[2,16,80,128]{3,2,1,0:T(8,128)(2,1)S(1)}, u32[]{:S(2)}) copy-start(bf16[2,16,80,128]{3,2,1,0:T(8,128)(2,1)S(1)} %pad_maximum_fusion.own) | copy-start | bytes 1966084
  85.4 7.7 %collective-permute-start.4 = (bf16[2,16,80,128]{3,2,1,0:T(8,128)(2,1)S(1)}, bf16[2,16,80,128]{3,2,1,0:T(8,128)(2,1)S(1)}, u32[]{:S(2)}, u32[]{:S(2)}) collective-permute-start(bf16[2,16,80,128]{3,2,1,0:T(8,128)(2,1)S(1)} %pad_maximum_fusion.own), channel_id=1, source_target_pairs={{0,8},{8,0},{16,24},{24,16},{32,40},{40,32},{48,56},{56,48},{64,72... | collective-permute-start | bytes 1966088 | tf_op jit(solution)/shard_map/ppermute | solution.py:311
  92.3 9.1 %copy-start.7 = (s32[7]{0:T(128)S(1)}, s32[7]{0:T(128)}, u32[]{:S(2)}) copy-start(s32[7]{0:T(128)} %stack.60.meta) | copy-start | bytes 88
  96.5 4.9 %collective-permute-start.5 = (bf16[16,256,128]{2,1,0:T(8,128)(2,1)}, bf16[16,256,128]{2,1,0:T(8,128)(2,1)S(1)}, u32[]{:S(2)}, u32[]{:S(2)}) collective-permute-start(bf16[16,256,128]{2,1,0:T(8,128)(2,1)} %bitcast.63), channel_id=1, source_target_pairs={{0,8},{8,0},{16,24},{24,16},{32,40},{40,32},{48,56},{56,48},{64,72... | collective-permute-start | bytes 3145736 | tf_op jit(solution)/shard_map/ppermute | solution.py:311
  110.7 18.9 %copy-start.4 = (f32[2,8,512]{2,1,0:T(8,128)}, f32[2,8,512]{2,1,0:T(8,128)S(1)}, u32[]{:S(2)}) copy-start(f32[2,8,512]{2,1,0:T(8,128)S(1)} %get-tuple-element.38.stats) | copy-start | bytes 98308
  110.8 26.6 %copy-start.3 = (f32[2,128,512]{2,1,0:T(8,128)}, f32[2,128,512]{2,1,0:T(8,128)S(1)}, u32[]{:S(2)}) copy-start(f32[2,128,512]{2,1,0:T(8,128)S(1)} %get-tuple-element.37.out_t) | copy-start | bytes 1572868
  110.8 7.2 %collective-permute-start.6 = (f32[8,512]{1,0:T(8,128)S(1)}, f32[8,512]{1,0:T(8,128)S(1)}, u32[]{:S(2)}, u32[]{:S(2)}) collective-permute-start(f32[8,512]{1,0:T(8,128)S(1)} %select_bitcast_fusion), channel_id=1, source_target_pairs={{0,256},{8,264},{16,272},{24,280},{32,288},{40,296},{48,304},{56,3... | collective-permute-start | bytes 49160 | tf_op jit(solution)/shard_map/ppermute | solution.py:311
  117.9 11.7 %copy-start.6 = (f32[8,512]{1,0:T(8,128)}, f32[8,512]{1,0:T(8,128)S(1)}, u32[]{:S(2)}) copy-start(f32[8,512]{1,0:T(8,128)S(1)} %collective-permute-done.6.come) | copy-start | bytes 49156
  130.4 5.3 %collective-permute-start.7 = (bf16[16,384,128]{2,1,0:T(8,128)(2,1)S(1)}, bf16[16,384,128]{2,1,0:T(8,128)(2,1)S(1)}, u32[]{:S(2)}, u32[]{:S(2)}) collective-permute-start(bf16[16,384,128]{2,1,0:T(8,128)(2,1)S(1)} %get-tuple-element.42), channel_id=1, source_target_pairs={{0,8},{8,0},{16,24},{24,16},{32,40},{40,32},{48,56},{56,48},{64,72... | collective-permute-start | bytes 4718600 | tf_op jit(solution)/shard_map/ppermute | solution.py:311
  137.4 11.7 %collective-permute-start.8 = (bf16[2,128,512]{2,1,0:T(8,128)(2,1)S(1)}, bf16[2,128,512]{2,1,0:T(8,128)(2,1)S(1)}, u32[]{:S(2)}, u32[]{:S(2)}) collective-permute-start(bf16[2,128,512]{2,1,0:T(8,128)(2,1)S(1)} %pad_maximum_fusion.3), channel_id=1, source_target_pairs={{0,256},{8,264},{16,272},{24,280},{32,288},{40,296},{48,304},{56,3... | collective-permute-start | bytes 786440 | tf_op jit(solution)/shard_map/ppermute | solution.py:311
  202.5 7.1 %collective-permute-start.9 = (bf16[64,128]{1,0:T(8,128)(2,1)S(1)}, bf16[64,128]{1,0:T(8,128)(2,1)S(1)}, u32[]{:S(2)}, u32[]{:S(2)}) collective-permute-start(bf16[64,128]{1,0:T(8,128)(2,1)S(1)} %slice_bitcast_fusion.4), channel_id=1, source_target_pairs={{0,256},{8,264},{16,272},{24,280},{32,288},{40,296},{48,304},{56,3... | collective-permute-start | bytes 49160 | tf_op jit(solution)/shard_map/ppermute | solution.py:311
  (6 other events, 5.3 us)
Sparse Core Ops, SparseCore 0:
  10.7 75.5 all-gather.3
  137.4 64.2 reduce-scatter.1

commit v6 on v4

--- a/solution.py
+++ b/solution.py
@@ -50,8 +50,8 @@
     low_out[...] = low.astype(bf16)
 
 
-def expert_at(meta, z_count, w, j):
-    first = meta[3 + 2 * w + j] * 4
+def expert_at(meta, ids, z_count, w, j):
+    first = ids[w, 1, j] * 4
     return lax.rem(first, 2 * z_count) // 2, lax.div(first, 2 * z_count) ^ meta[0]
 
 
@@ -70,7 +70,7 @@
     return first, last
 
 
-def prepare(heads, z_count, meta, own, other, low_ref, pair, docs, side):
+def prepare(heads, z_count, meta, ids, own, other, low_ref, pair, docs, side):
     core = meta[2]
 
     counts = jnp.zeros((16, 128), f32)
@@ -90,7 +90,7 @@
             columns = slice(h * HEAD, (h + 1) * HEAD)
             rows = []
             for j in range(2):
-                z_at, slot = expert_at(meta, z_count, w, j)
+                z_at, slot = expert_at(meta, ids, z_count, w, j)
                 at = slice(16 * h, 16 * h + 16)
                 for step in range(2):
                     mine, theirs = own[slot, z_at + step, at, :], other[slot, z_at + step, at, :]
@@ -222,6 +222,7 @@
     heads,
     z_count,
     meta,
+    ids,
     own,
     other,
     side,
@@ -284,7 +285,7 @@
                 dquery_across[:, columns] = dq_low
             up = adapter_scale * first_first(low, dq_low)
             for j in range(2):
-                z_at, slot = expert_at(meta, z_count, w, j)
+                z_at, slot = expert_at(meta, ids, z_count, w, j)
                 at = pl.ds(pl.multiple_of(KV + slot * UPS + 16 * h, 16), 16)
                 for i in range(2):
                     row = j * RANK + 32 * i
@@ -380,18 +381,14 @@
             place // across,
             place // 2 % z_count,
             place % 2,
-            ints[0, 1, 0],
-            ints[0, 1, 1],
-            ints[1, 1, 0],
-            ints[1, 1, 1],
         ]
     ).astype(jnp.int32)
     side = pl.pallas_call(
         functools.partial(prepare, heads, z_count),
         out_shape=jax.ShapeDtypeStruct((2, SIDE, HEAD), bf16),
-        in_specs=[smem] + [vmem] * 5,
+        in_specs=[smem] * 2 + [vmem] * 5,
         out_specs=vmem,
-    )(meta, small, small_other, low, pair, ints)
+    )(meta, ints, small, small_other, low, pair, ints)
     own, side = lax.optimization_barrier((own, side))
     other = swap(own, 1)
     quads = z_count // 2
@@ -418,7 +415,7 @@
             send,
             send,
         ),
-        in_specs=[smem] + [vmem] * 6,
+        in_specs=[smem] * 2 + [vmem] * 6,
         out_specs=(vmem,) * 4,
         scratch_shapes=[
             pltpu.VMEM((z_count, GRAD, HEAD), f32),
@@ -426,7 +423,7 @@
             pltpu.VMEM((stack, HEAD), bf16),
         ],
         compiler_params=pltpu.CompilerParams(vmem_limit_bytes=30 * 1024 * 1024),
-    )(meta, own, other, side, prob, stats, come)
+    )(meta, ints, own, other, side, prob, stats, come)
 
     chip = send_own + swap(send_other, 1)
     part = lax.psum_scatter(

time: 216 us -> 221 us (1.023)
  waiting for transfers between devices: 81.3 us -> 89.5 us
  local copies, waits for them, and re-layouts: 16.5 us -> 12.2 us
  Pallas kernels: 20 us -> 16.6 us
  starting transfers between devices: 38.6 us -> 41.2 us
    ppermute x10, waiting for transfers between devices: 29 us -> 33.2 us  [swap(): return lax.ppermute(array, 'ctx', [(i, i ^ distance) for i in range(count)])]
    reduce_scatter x1, waiting for transfers between devices: 52.3 us -> 56.2 us  [shards(): lax.psum_scatter(chip, 'ctx', scatter_dimension=0, tiled=False, axis_inde...]
    another operation x1 -> x0, local copies, waits for them, and re-layouts: 3.1 us -> none  [shards(): jnp.stack([place // across, place // 2 % z_count, place % 2, ints[0, 1, 0...]
    ppermute x10, starting transfers between devices: 29.2 us -> 31.7 us  [swap(): return lax.ppermute(array, 'ctx', [(i, i ^ distance) for i in range(count)])]
    unnamed x37 -> x41, local copies, waits for them, and re-layouts: 6.09 us -> 6.09 us
  transfers between devices with their start and end apart: 13 -> 13, of which waited for: 8 -> 9; matrix products, arithmetic and copies ran while one was open for 6% -> 4% of each run, Pallas kernels for 3% -> 3%
where the time goes in v6:
time: 221 us; the launch traced here: 219 us
  waiting for transfers between devices  89.5 us (40%)
  starting transfers between devices  41.2 us (19%)
  blocking collectives  34.6 us (16%)
  between operations  18.3 us (8%)
  Pallas kernels  16.6 us (8%)
  local copies, waits for them, and re-layouts  12.2 us (6%)
  other arithmetic  6.78 us (3%)
    reduce_scatter x1, waiting for transfers between devices, shards(): lax.psum_scatter(chip, 'ctx', scatter_dimension=0, tiled=False, axis_inde...  56.2 us
    all_gather x1, blocking collectives, shards(): lax.all_gather(small, 'ctx', axis=0, tiled=False, axis_index_groups=runs)  34.6 us
    ppermute x10, waiting for transfers between devices, swap(): return lax.ppermute(array, 'ctx', [(i, i ^ distance) for i in range(count)])  33.2 us
    ppermute x10, starting transfers between devices, swap(): return lax.ppermute(array, 'ctx', [(i, i ^ distance) for i in range(count)])  31.7 us
    all_to_all x1, starting transfers between devices, shards(): lows = lax.all_to_all(spread, 'exp', 0, 0)  9.41 us
    pallas_call x1, Pallas kernels, shards(): pl.pallas_call(functools.partial(backward, heads, z_count), out_shape=(ja...  6.5 us
    unnamed x41, local copies, waits for them, and re-layouts  6.09 us
  transfers between devices with their start and end apart: 13, of which 9 were waited for; matrix products, arithmetic and copies ran while one was open for 4% of the time, Pallas kernels for 3%

profile of v6, /device:TPU:6, one launch (start us, length us, event | category | flops | bytes accessed | tf_op | source)
XLA Modules:
  0.0 219.4 jit_solution(9744030189168194192)
XLA Ops:
  16.8 9.4 %all-to-all-start = ((f32[8,128,128]{2,1,0:T(8,128)}), f32[8,128,128]{2,1,0:T(8,128)S(1)}, u32[]{:S(2)}, u32[]{:S(2)}) async-start(f32[8,128,128]{2,1,0:T(8,128)} %broadcast_in_dim.2), calls=%async_computation | async-start | bytes 1048576 | tf_op jit(solution)/shard_map/all_to_all | solution.py:352
  26.4 34.6 %all-gather.1 = bf16[1280,128]{1,0:T(8,128)(2,1)S(1)} all-gather(bf16[80,128]{1,0:T(8,128)(2,1)S(1)} %fusion.6), channel_id=3, replica_groups={{0,16,32,48,64,80,96,112,128,144,160,176,192,208,224,240},{8,24,40,56,7..., dimensions={0}, use_global_device_ids=true | all-gather | bytes 348160 | tf_op jit(solution)/shard_map/all_gather | solution.py:365
  63.5 4.7 %collective-permute-start.1 = (bf16[16,80,128]{2,1,0:T(8,128)(2,1)S(1)}, bf16[16,80,128]{2,1,0:T(8,128)(2,1)S(1)}, u32[]{:S(2)}, u32[]{:S(2)}) collective-permute-start(bf16[16,80,128]{2,1,0:T(8,128)(2,1)S(1)} %bitcast.63), channel_id=1, source_target_pairs={{0,256},{8,264},{16,272},{24,280},{32,288},{40,296},{48,304},{56,3... | collective-permute-start | bytes 983048 | tf_op jit(solution)/shard_map/ppermute | solution.py:312
  68.2 5.9 %collective-permute-done.1 = bf16[16,80,128]{2,1,0:T(8,128)(2,1)S(1)} collective-permute-done((bf16[16,80,128]{2,1,0:T(8,128)(2,1)S(1)}, bf16[16,80,128]{2,1,0:T(8,128)(2,1)S(1)}, u32[]{:S(2)}, u32[]{:S(2)}) %collective-permute-start.1) | collective-permute-done | bytes 327712 | tf_op jit(solution)/shard_map/ppermute | solution.py:312
  74.2 1.9 collective-permute-start.2
  76.2 4.6 %collective-permute-start.4 = (bf16[256,512]{1,0:T(8,128)(2,1)S(1)}, bf16[256,512]{1,0:T(8,128)(2,1)S(1)}, u32[]{:S(2)}, u32[]{:S(2)}) collective-permute-start(bf16[256,512]{1,0:T(8,128)(2,1)S(1)} %pad_maximum_fusion.2), channel_id=1, source_target_pairs={{0,256},{8,264},{16,272},{24,280},{32,288},{40,296},{48,304},{56,3... | collective-permute-start | bytes 786440 | tf_op jit(solution)/shard_map/ppermute | solution.py:312
  80.8 2.8 %collective-permute-start = (s32[8,128]{1,0:T(8,128)S(1)}, s32[8,128]{1,0:T(8,128)S(1)}, u32[]{:S(2)}, u32[]{:S(2)}) collective-permute-start(s32[8,128]{1,0:T(8,128)S(1)} %pad_add_fusion.1), channel_id=1, source_target_pairs={{0,256},{8,264},{16,272},{24,280},{32,288},{40,296},{48,304},{56,3... | collective-permute-start | bytes 12296 | tf_op jit(solution)/shard_map/ppermute | solution.py:312
  84.3 4.1 %collective-permute-done = s32[8,128]{1,0:T(8,128)S(1)} collective-permute-done((s32[8,128]{1,0:T(8,128)S(1)}, s32[8,128]{1,0:T(8,128)S(1)}, u32[]{:S(2)}, u32[]{:S(2)}) %collective-permute-start) | collective-permute-done | bytes 4128 | tf_op jit(solution)/shard_map/ppermute | solution.py:312
  89.0 4.6 %collective-permute-start.3 = (bf16[128,128]{1,0:T(8,128)(2,1)S(1)}, bf16[128,128]{1,0:T(8,128)(2,1)S(1)}, u32[]{:S(2)}, u32[]{:S(2)}) collective-permute-start(bf16[128,128]{1,0:T(8,128)(2,1)S(1)} %copy-done.14), channel_id=1, source_target_pairs={{0,256},{8,264},{16,272},{24,280},{32,288},{40,296},{48,304},{56,3... | collective-permute-start | bytes 98312 | tf_op jit(solution)/shard_map/ppermute | solution.py:312
  94.4 1.9 collective-permute-done.3
  97.7 2.6 %shard_map.129.side = bf16[2,1168,128]{2,1,0:T(8,128)(2,1)} custom-call(s32[3]{0:T(128)} %pad_add_fusion.2.meta, s32[2,8,128]{2,1,0:T(8,128)} %pad_add_fusion.ids.docs, bf16[2,16,80,128]{3,2,1,0:T(8,128)(2,1)} %copy-done.10, bf16[2,16,80,128]{3,2,1,0:T(8,128)(2,1)} %copy-done.12, bf16[2,128,128]{2,1,0:T(8,128)(2,1)} %pad_maximum_fusion.4.low_ref, ...), custom_call_target="tpu_custom_call" | custom-call | tf_op jit(solution)/shard_map/pallas_call | solution.py:386
  100.3 1.9 collective-permute-start.5
  102.3 2.8 %collective-permute-done.5.other = bf16[16,256,128]{2,1,0:T(8,128)(2,1)S(1)} collective-permute-done((bf16[16,256,128]{2,1,0:T(8,128)(2,1)}, bf16[16,256,128]{2,1,0:T(8,128)(2,1)S(1)}, u32[]{:S(2)}, u32[]{:S(2)}) %collective-permute-start.5) | collective-permute-done | bytes 1048608 | tf_op jit(solution)/shard_map/ppermute | solution.py:312
  107.4 3.7 %shard_map.130 = (bf16[2,8,512,512]{3,2,1,0:T(8,128)(2,1)S(1)}, f32[2,128,512]{2,1,0:T(8,128)S(1)}, f32[2,8,512]{2,1,0:T(8,128)S(1)}) custom-call(s32[3]{0:T(128)S(1)} %copy-done.9, bf16[16,256,128]{2,1,0:T(8,128)(2,1)S(1)} %bitcast.60, bf16[16,256,128]{2,1,0:T(8,128)(2,1)S(1)} %collective-permute-done.5.other, bf16[2,1168,128]{2,1,0:T(8,128)(2,1)S(1)} %copy-done.1), custom_call_target="tpu_custom_call" | custom-call | tf_op jit(solution)/shard_map/pallas_call | solution.py:395
  111.1 2.5 %collective-permute-start.6 = (f32[8,512]{1,0:T(8,128)S(1)}, f32[8,512]{1,0:T(8,128)S(1)}, u32[]{:S(2)}, u32[]{:S(2)}) collective-permute-start(f32[8,512]{1,0:T(8,128)S(1)} %select_bitcast_fusion), channel_id=1, source_target_pairs={{0,256},{8,264},{16,272},{24,280},{32,288},{40,296},{48,304},{56,3... | collective-permute-start | bytes 49160 | tf_op jit(solution)/shard_map/ppermute | solution.py:312
  113.6 4.6 %collective-permute-done.6.come = f32[8,512]{1,0:T(8,128)S(1)} collective-permute-done((f32[8,512]{1,0:T(8,128)S(1)}, f32[8,512]{1,0:T(8,128)S(1)}, u32[]{:S(2)}, u32[]{:S(2)}) %collective-permute-start.6) | collective-permute-done | bytes 16416 | tf_op jit(solution)/shard_map/ppermute | solution.py:312
  118.3 6.5 %shard_map.131 = (f32[128,512]{1,0:T(8,128)S(1)}, bf16[128,512]{1,0:T(8,128)(2,1)S(1)}, bf16[16,384,128]{2,1,0:T(8,128)(2,1)S(1)}, bf16[16,384,128]{2,1,0:T(8,128)(2,1)S(1)}) custom-call(s32[3]{0:T(128)S(1)} %copy-done.9, s32[2,8,128]{2,1,0:T(8,128)S(1)} %copy-done.7, bf16[16,256,128]{2,1,0:T(8,128)(2,1)S(1)} %bitcast.61, ...), custom_call_target="tpu_custom_call" | custom-call | tf_op jit(solution)/shard_map/pallas_call | solution.py:410
  125.5 1.9 collective-permute-start.7
  127.4 3.4 %collective-permute-done.7 = bf16[16,384,128]{2,1,0:T(8,128)(2,1)S(1)} collective-permute-done((bf16[16,384,128]{2,1,0:T(8,128)(2,1)S(1)}, bf16[16,384,128]{2,1,0:T(8,128)(2,1)S(1)}, u32[]{:S(2)}, u32[]{:S(2)}) %collective-permute-start.7) | collective-permute-done | bytes 1572896 | tf_op jit(solution)/shard_map/ppermute | solution.py:312
  132.5 1.9 collective-permute-start.8
  134.4 9.8 %collective-permute-done.8 = bf16[2,128,512]{2,1,0:T(8,128)(2,1)S(1)} collective-permute-done((bf16[2,128,512]{2,1,0:T(8,128)(2,1)S(1)}, bf16[2,128,512]{2,1,0:T(8,128)(2,1)S(1)}, u32[]{:S(2)}, u32[]{:S(2)}) %collective-permute-start.8) | collective-permute-done | bytes 262176 | tf_op jit(solution)/shard_map/ppermute | solution.py:312
  145.0 2.2 shard_map.132
  147.2 56.2 %reduce-scatter.2.cloned.1.call-done = bf16[1,384,128]{2,1,0:T(8,128)(2,1)} async-done(((bf16[16,384,128]{2,1,0:T(8,128)(2,1)}), bf16[1,384,128]{2,1,0:T(8,128)(2,1)}) %reduce-scatter.2.cloned.1.call-update) | async-done | bytes 98320 | tf_op jit(solution)/shard_map/reduce_scatter | solution.py:429
  204.1 4.9 %collective-permute-start.9 = (bf16[64,128]{1,0:T(8,128)(2,1)S(1)}, bf16[64,128]{1,0:T(8,128)(2,1)S(1)}, u32[]{:S(2)}, u32[]{:S(2)}) collective-permute-start(bf16[64,128]{1,0:T(8,128)(2,1)S(1)} %slice_bitcast_fusion.4), channel_id=1, source_target_pairs={{0,256},{8,264},{16,272},{24,280},{32,288},{40,296},{48,304},{56,3... | collective-permute-start | bytes 49160 | tf_op jit(solution)/shard_map/ppermute | solution.py:312
  (77 shorter events, 21.7 us)
Async XLA Ops:
  7.2 93.2 %all-gather.4.cloned.1.call-start = ((), (), s32[]{:S(2)}) async-start(), calls=%async_computation.3 | async-start | bytes 1114112 | tf_op jit(solution)/shard_map/all_gather | solution.py:344
  8.0 18.2 %copy-start.17 = (bf16[16,512]{1,0:T(8,128)(2,1)S(1)}, bf16[16,512]{1,0:T(8,128)(2,1)}, u32[]{:S(2)}) copy-start(bf16[16,512]{1,0:T(8,128)(2,1)} %param.16) | copy-start | bytes 49156
  8.8 17.5 %copy-start.19 = (s32[128]{0:T(128)S(1)}, s32[128]{0:T(128)}, u32[]{:S(2)}) copy-start(s32[128]{0:T(128)} %param.13) | copy-start | bytes 1540
  16.8 59.3 %copy-start.15 = (bf16[128,512]{1,0:T(8,128)(2,1)S(1)}, bf16[128,512]{1,0:T(8,128)(2,1)}, u32[]{:S(2)}) copy-start(bf16[128,512]{1,0:T(8,128)(2,1)} %param.17) | copy-start | bytes 393220
  16.8 59.3 %copy-start.16 = (bf16[128,512]{1,0:T(8,128)(2,1)S(1)}, bf16[128,512]{1,0:T(8,128)(2,1)}, u32[]{:S(2)}) copy-start(bf16[128,512]{1,0:T(8,128)(2,1)} %param.10) | copy-start | bytes 393220
  16.8 44.2 %all-to-all-start = ((f32[8,128,128]{2,1,0:T(8,128)}), f32[8,128,128]{2,1,0:T(8,128)S(1)}, u32[]{:S(2)}, u32[]{:S(2)}) async-start(f32[8,128,128]{2,1,0:T(8,128)} %broadcast_in_dim.2), calls=%async_computation | async-start | bytes 1048576 | tf_op jit(solution)/shard_map/all_to_all | solution.py:352
  26.2 54.5 %copy-start.18 = (s32[1,2]{1,0:T(1,128)S(1)}, s32[1,2]{1,0:T(1,128)}, u32[]{:S(2)}) copy-start(s32[1,2]{1,0:T(1,128)} %param.14) | copy-start | bytes 28
  26.2 177.1 %reduce-scatter.2.cloned.1.call-start = ((), (), s32[]{:S(2)}) async-start(), calls=%async_computation.2 | async-start | bytes 1671168 | tf_op jit(solution)/shard_map/reduce_scatter | solution.py:429
  63.5 25.4 %copy-start.14 = (bf16[128,128]{1,0:T(8,128)(2,1)S(1)}, bf16[128,128]{1,0:T(8,128)(2,1)}, u32[]{:S(2)}) copy-start(bf16[128,128]{1,0:T(8,128)(2,1)} %shard_map.128) | copy-start | bytes 98308
  63.5 10.6 %collective-permute-start.1 = (bf16[16,80,128]{2,1,0:T(8,128)(2,1)S(1)}, bf16[16,80,128]{2,1,0:T(8,128)(2,1)S(1)}, u32[]{:S(2)}, u32[]{:S(2)}) collective-permute-start(bf16[16,80,128]{2,1,0:T(8,128)(2,1)S(1)} %bitcast.63), channel_id=1, source_target_pairs={{0,256},{8,264},{16,272},{24,280},{32,288},{40,296},{48,304},{56,3... | collective-permute-start | bytes 983048 | tf_op jit(solution)/shard_map/ppermute | solution.py:312
  74.2 22.7 %copy-start.10 = (bf16[2,16,80,128]{3,2,1,0:T(8,128)(2,1)}, bf16[2,16,80,128]{3,2,1,0:T(8,128)(2,1)S(1)}, u32[]{:S(2)}) copy-start(bf16[2,16,80,128]{3,2,1,0:T(8,128)(2,1)S(1)} %pad_maximum_fusion.own) | copy-start | bytes 1966084
  74.2 22.7 %collective-permute-start.2 = (bf16[2,16,80,128]{3,2,1,0:T(8,128)(2,1)S(1)}, bf16[2,16,80,128]{3,2,1,0:T(8,128)(2,1)S(1)}, u32[]{:S(2)}, u32[]{:S(2)}) collective-permute-start(bf16[2,16,80,128]{3,2,1,0:T(8,128)(2,1)S(1)} %pad_maximum_fusion.own), channel_id=1, source_target_pairs={{0,8},{8,0},{16,24},{24,16},{32,40},{40,32},{48,56},{56,48},{64,72... | collective-permute-start | bytes 1966088 | tf_op jit(solution)/shard_map/ppermute | solution.py:312
  76.2 17.4 %collective-permute-start.4 = (bf16[256,512]{1,0:T(8,128)(2,1)S(1)}, bf16[256,512]{1,0:T(8,128)(2,1)S(1)}, u32[]{:S(2)}, u32[]{:S(2)}) collective-permute-start(bf16[256,512]{1,0:T(8,128)(2,1)S(1)} %pad_maximum_fusion.2), channel_id=1, source_target_pairs={{0,256},{8,264},{16,272},{24,280},{32,288},{40,296},{48,304},{56,3... | collective-permute-start | bytes 786440 | tf_op jit(solution)/shard_map/ppermute | solution.py:312
  80.8 7.6 %collective-permute-start = (s32[8,128]{1,0:T(8,128)S(1)}, s32[8,128]{1,0:T(8,128)S(1)}, u32[]{:S(2)}, u32[]{:S(2)}) collective-permute-start(s32[8,128]{1,0:T(8,128)S(1)} %pad_add_fusion.1), channel_id=1, source_target_pairs={{0,256},{8,264},{16,272},{24,280},{32,288},{40,296},{48,304},{56,3... | collective-permute-start | bytes 12296 | tf_op jit(solution)/shard_map/ppermute | solution.py:312
  89.0 7.3 %collective-permute-start.3 = (bf16[128,128]{1,0:T(8,128)(2,1)S(1)}, bf16[128,128]{1,0:T(8,128)(2,1)S(1)}, u32[]{:S(2)}, u32[]{:S(2)}) collective-permute-start(bf16[128,128]{1,0:T(8,128)(2,1)S(1)} %copy-done.14), channel_id=1, source_target_pairs={{0,256},{8,264},{16,272},{24,280},{32,288},{40,296},{48,304},{56,3... | collective-permute-start | bytes 98312 | tf_op jit(solution)/shard_map/ppermute | solution.py:312
  97.7 20.5 %copy-start.7 = (s32[2,8,128]{2,1,0:T(8,128)S(1)}, s32[2,8,128]{2,1,0:T(8,128)}, u32[]{:S(2)}) copy-start(s32[2,8,128]{2,1,0:T(8,128)} %pad_add_fusion.ids.docs) | copy-start | bytes 24580
  100.3 4.8 %collective-permute-start.5 = (bf16[16,256,128]{2,1,0:T(8,128)(2,1)}, bf16[16,256,128]{2,1,0:T(8,128)(2,1)S(1)}, u32[]{:S(2)}, u32[]{:S(2)}) collective-permute-start(bf16[16,256,128]{2,1,0:T(8,128)(2,1)} %bitcast.59), channel_id=1, source_target_pairs={{0,8},{8,0},{16,24},{24,16},{32,40},{40,32},{48,56},{56,48},{64,72... | collective-permute-start | bytes 3145736 | tf_op jit(solution)/shard_map/ppermute | solution.py:312
  107.4 10.9 %copy-start.2 = (bf16[2,1168,128]{2,1,0:T(8,128)(2,1)S(1)}, bf16[2,1168,128]{2,1,0:T(8,128)(2,1)}, u32[]{:S(2)}) copy-start(bf16[2,1168,128]{2,1,0:T(8,128)(2,1)} %shard_map.129.side) | copy-start | bytes 1794052
  111.1 13.7 %copy-start.5 = (f32[2,8,512]{2,1,0:T(8,128)}, f32[2,8,512]{2,1,0:T(8,128)S(1)}, u32[]{:S(2)}) copy-start(f32[2,8,512]{2,1,0:T(8,128)S(1)} %get-tuple-element.30.stats) | copy-start | bytes 98308
  111.1 21.3 %copy-start.4 = (f32[2,128,512]{2,1,0:T(8,128)}, f32[2,128,512]{2,1,0:T(8,128)S(1)}, u32[]{:S(2)}) copy-start(f32[2,128,512]{2,1,0:T(8,128)S(1)} %get-tuple-element.29.out_t) | copy-start | bytes 1572868
  111.1 7.1 %collective-permute-start.6 = (f32[8,512]{1,0:T(8,128)S(1)}, f32[8,512]{1,0:T(8,128)S(1)}, u32[]{:S(2)}, u32[]{:S(2)}) collective-permute-start(f32[8,512]{1,0:T(8,128)S(1)} %select_bitcast_fusion), channel_id=1, source_target_pairs={{0,256},{8,264},{16,272},{24,280},{32,288},{40,296},{48,304},{56,3... | collective-permute-start | bytes 49160 | tf_op jit(solution)/shard_map/ppermute | solution.py:312
  125.5 5.3 %collective-permute-start.7 = (bf16[16,384,128]{2,1,0:T(8,128)(2,1)S(1)}, bf16[16,384,128]{2,1,0:T(8,128)(2,1)S(1)}, u32[]{:S(2)}, u32[]{:S(2)}) collective-permute-start(bf16[16,384,128]{2,1,0:T(8,128)(2,1)S(1)} %get-tuple-element.34), channel_id=1, source_target_pairs={{0,8},{8,0},{16,24},{24,16},{32,40},{40,32},{48,56},{56,48},{64,72... | collective-permute-start | bytes 4718600 | tf_op jit(solution)/shard_map/ppermute | solution.py:312
  132.5 11.7 %collective-permute-start.8 = (bf16[2,128,512]{2,1,0:T(8,128)(2,1)S(1)}, bf16[2,128,512]{2,1,0:T(8,128)(2,1)S(1)}, u32[]{:S(2)}, u32[]{:S(2)}) collective-permute-start(bf16[2,128,512]{2,1,0:T(8,128)(2,1)S(1)} %pad_maximum_fusion.3), channel_id=1, source_target_pairs={{0,256},{8,264},{16,272},{24,280},{32,288},{40,296},{48,304},{56,3... | collective-permute-start | bytes 786440 | tf_op jit(solution)/shard_map/ppermute | solution.py:312
  204.1 7.1 %collective-permute-start.9 = (bf16[64,128]{1,0:T(8,128)(2,1)S(1)}, bf16[64,128]{1,0:T(8,128)(2,1)S(1)}, u32[]{:S(2)}, u32[]{:S(2)}) collective-permute-start(bf16[64,128]{1,0:T(8,128)(2,1)S(1)} %slice_bitcast_fusion.4), channel_id=1, source_target_pairs={{0,256},{8,264},{16,272},{24,280},{32,288},{40,296},{48,304},{56,3... | collective-permute-start | bytes 49160 | tf_op jit(solution)/shard_map/ppermute | solution.py:312
  (9 other events, 31.0 us)
Sparse Core Ops, SparseCore 0:
  10.7 75.4 all-gather.3
  132.5 70.7 reduce-scatter.1
